TPU v7x, 512 devices: a whole 4x4x16 slice. The times are simulated.
512 devices in a mesh: tm: 32 (over z, core), seq: 16 (over x, y).
Axes of the slice: x: 4, y: 4, z: 16, core: 2. Of those that a mesh axis runs over, the one named last changes fastest.
Arguments:
- states: float32 [32, 512, 64], P('tm', 'seq'), may hold values from -6 to 6
- initial: float32 [512, 64], P('seq'), may hold values from -6 to 6
- noise_draws: float32 [32, 512, 64], P('tm', 'seq'), may hold values from -6 to 6
- timesteps: int32 [32, 2], P('tm'), may hold values from 0 to 999, as said below
- context: bfloat16 [512, 5120], P('seq'), may hold values from -6 to 6
- modulation: float32 [32, 2, 5120], P('tm'), may hold values from -1.5 to 1.5
- out_gate: float32 [32, 64], P('tm'), may hold values from -3 to 3
- embed_weight: bfloat16 [64, 5120], replicated, may hold values from -0.75 to 0.75
- qkv_weight: bfloat16 [3, 5120, 4096], P(None, 'tm', 'seq'), may hold values from -1 to 1
- out_weight: bfloat16 [4096, 5120], P('seq', 'tm'), may hold values from -0.09375 to 0.09375
- head_weight: bfloat16 [64, 5120], P(None, 'tm'), may hold values from -0.078125 to 0.078125
Outputs:
- new_states: float32 [32, 512, 64], P('tm', 'seq')
- velocity: bfloat16 [32, 512, 64], P('tm', 'seq')
Inputs may be any that keep to these rules, and one draw needn't show every extreme that they name: `timesteps`: row k holds step k's timestep index and the next, smaller one, which is the first entry of row k + 1; row 0 starts at 999.
All inputs are finite; a program needn't handle non-finite values.
Results may differ from a plain program's by a relative error of at most 0.02.
Values may be sent and summed in bfloat16 or wider, within the bound.
No kernel may reach another device: no remote copies, remote signals or barrier semaphores. Data moves between devices by JAX's collectives and lax.ppermute only.
A program may use at most 64 MiB of HBM per device.

v0:
```python
import functools
import math

import jax
import jax.numpy as jnp
from jax import lax
from jax.sharding import PartitionSpec as P

HEAD = 128
NT = 1000


def entering(value, axis, join, neutral):
    count, mine = (lax.axis_size(axis), lax.axis_index(axis))
    pieces = lax.all_gather(value, axis)
    subtotal = jnp.full_like(value, 0) + jnp.asarray(neutral, value.dtype)

    def turn(position, subtotal):
        longer = join(subtotal, pieces[position])
        return jnp.where(position < mine, longer, subtotal)

    return lax.fori_loop(0, count - 1, turn, subtotal)


def sigma_of(level_ids):
    fraction = (level_ids.astype(jnp.float32) + 1.0) / NT
    return 5.0 * fraction / (1.0 + 4.0 * fraction)


def attend_block(query_block, keys_all, values_all):
    scores = jnp.einsum(
        "qhd,khd->hqk", query_block, keys_all, preferred_element_type=jnp.float32
    ) / math.sqrt(query_block.shape[-1])
    row_peak = jnp.max(scores, axis=-1, keepdims=True)
    weights = jnp.exp(scores - row_peak)
    probs = weights / jnp.sum(weights, axis=-1, keepdims=True)
    probs_bf = probs.astype(jnp.bfloat16)
    output = jnp.einsum("hqk,khd->qhd", probs_bf, values_all, preferred_element_type=jnp.float32)
    return output.astype(jnp.bfloat16)


def attend_heads(queries, keys_all, values_all):
    total_rows, heads_here, head_size = queries.shape
    block_rows = min(512, total_rows)
    blocks = queries.reshape(total_rows // block_rows, block_rows, heads_here, head_size)
    worker = functools.partial(attend_block, keys_all=keys_all, values_all=values_all)
    return lax.map(worker, blocks).reshape(total_rows, heads_here * head_size)


def add_terms(earlier, later):
    return earlier + later


def per_device(
    states,
    initial,
    noise_draws,
    timesteps,
    context,
    modulation,
    out_gate,
    embed_weight,
    qkv_weight,
    out_weight,
    head_weight,
):
    current = states[0]
    mods = modulation[0]
    gate_row = out_gate[0]
    level_now = timesteps[0, 0]
    level_next = timesteps[0, 1]
    latent_bf = current.astype(jnp.bfloat16)
    hidden = jnp.dot(latent_bf, embed_weight, preferred_element_type=jnp.float32) + context.astype(
        jnp.float32
    )
    mean_square = jnp.mean(hidden * hidden, axis=-1, keepdims=True)
    normed = hidden * lax.rsqrt(mean_square + 1e-06)
    modded = (normed * (1.0 + mods[1]) + mods[0]).astype(jnp.bfloat16)
    full_qkv = lax.all_gather(qkv_weight, "tm", axis=1, tiled=True)
    everyone = lax.all_gather(modded, "seq", axis=0, tiled=True)
    all_rows = everyone.shape[0]
    col_width = full_qkv.shape[2]
    heads_here = col_width // HEAD
    projected = jnp.einsum(
        "td,idc->itc", everyone, full_qkv, preferred_element_type=jnp.float32
    ).astype(jnp.bfloat16)
    queries = projected[0].reshape(all_rows, heads_here, HEAD)
    keys_all = projected[1].reshape(all_rows, heads_here, HEAD)
    values_all = projected[2].reshape(all_rows, heads_here, HEAD)
    attended = attend_heads(queries, keys_all, values_all)
    out_full, head_full = (
        lax.all_gather(out_weight, "tm", axis=1, tiled=True),
        lax.all_gather(head_weight, "tm", axis=1, tiled=True),
    )
    head_float = head_full.astype(jnp.float32)
    mixed = jnp.dot(attended, out_full, preferred_element_type=jnp.float32)
    mixed_rows = lax.psum_scatter(
        jnp.dot(mixed, head_float.T, precision=lax.Precision.HIGHEST).astype(jnp.bfloat16),
        "seq",
        scatter_dimension=0,
        tiled=True,
    ).astype(jnp.float32)
    velocity_f = (1.0 + gate_row) * mixed_rows
    step_size = sigma_of(level_next) - sigma_of(level_now)
    drift_term = step_size * velocity_f + jnp.sqrt(-step_size) * noise_draws[0]
    before = entering(drift_term, "tm", add_terms, jnp.zeros_like(drift_term))
    new_states = (initial + before)[None]
    return (new_states, velocity_f.astype(jnp.bfloat16)[None])


def solution(mesh):
    in_specs = (
        P("tm", "seq", None),
        P("seq", None),
        P("tm", "seq", None),
        P("tm", None),
        P("seq", None),
        P("tm", None, None),
        P("tm", None),
        P(),
        P(None, "tm", "seq"),
        P("seq", "tm"),
        P(None, "tm"),
    )
    out_specs = (P("tm", "seq", None), P("tm", "seq", None))
    return jax.shard_map(
        per_device, mesh=mesh, in_specs=in_specs, out_specs=out_specs, check_vma=False
    )
```

profile of v0, /device:TPU:1, one launch (start us, length us, event | category | flops | bytes accessed | tf_op | source)
XLA Modules:
  0.0 376.5 jit_solution(6053437538962559389)
XLA Ops:
  7.2 0.0 copy-start
  7.2 0.0 all-gather.6.cloned.1.call-start
  7.2 1.0 copy-done
  8.3 1.3 multiply_reduce_fusion.1
  9.6 0.9 slice_add_fusion
  10.5 0.9 add_convert_fusion
  11.4 0.0 all-gather.6.cloned.1.call-update
  11.4 0.0 all-gather.8.cloned.1.call-start
  11.5 0.7 all-gather.8.cloned.1.call-update
  12.2 0.0 all-gather.10.cloned.1.call-start
  12.2 0.7 all-gather.10.cloned.1.call-update
  12.9 0.0 reduce-scatter.2.cloned.1.call-start
  13.0 0.6 fusion.26
  14.9 40.4 %all-gather.1 = bf16[32,160,64]{1,2,0:T(8,128)(2,1)S(1)} all-gather(bf16[1,160,64]{1,2,0:T(8,128)(2,1)S(1)} %bitcast.61), channel_id=1, replica_groups=mesh['tm'=32,'seq'=16] {'tm'}, dimensions={0}, use_global_device_ids=true | all-gather | bytes 675840 | tf_op jit(solution)/shard_map/all_gather | solution.py:93
  55.3 0.6 copy.23
  55.9 1.7 reshape.57
  57.7 30.9 %all-gather.6.cloned.1.call-done = bf16[512,5120]{1,0:T(8,128)(2,1)} async-done(((bf16[32,5120]{1,0:T(8,128)(2,1)}), bf16[512,5120]{1,0:T(8,128)(2,1)}) %all-gather.6.cloned.1.call-update) | async-done | bytes 5242896 | tf_op jit(solution)/shard_map/all_gather | solution.py:80
  88.6 81.2 %all-gather.8.cloned.1.call-done = bf16[3,5120,256]{2,1,0:T(8,128)(2,1)} async-done(((bf16[3,160,256]{2,1,0:T(8,128)(2,1)}), bf16[3,5120,256]{2,1,0:T(8,128)(2,1)}) %all-gather.8.cloned.1.call-update) | async-done | bytes 7864336 | tf_op jit(solution)/shard_map/all_gather | solution.py:79
  169.8 9.1 %fusion.7 = bf16[3,512,256]{1,2,0:T(8,128)(2,1)S(1)} fusion(bf16[3,5120,256]{2,1,0:T(8,128)(2,1)} %all-gather.8.cloned.1.call-done, bf16[512,5120]{1,0:T(8,128)(2,1)} %all-gather.6.cloned.1.call-done), kind=kOutput, calls=%fused_computation.10 | convolution fusion | flops 4026925056 | bytes 13893632 | tf_op jit(solution)/shard_map/td,idc->itc/dot_general | solution.py:84
  178.8 0.1 fusion.25
  178.9 0.9 fusion.27
  179.7 1.2 convolution_convert_fusion
  180.9 60.3 %all-gather.10.cloned.1.call-done = bf16[256,5120]{0,1:T(8,128)(2,1)} async-done(((bf16[256,160]{0,1:T(8,128)(2,1)}), bf16[256,5120]{0,1:T(8,128)(2,1)}) %all-gather.10.cloned.1.call-update) | async-done | bytes 2621456 | tf_op jit(solution)/shard_map/all_gather | solution.py:92
  241.2 3.3 fusion.28
  244.5 0.0 copy-start.2
  244.6 5.6 %convolution_convert_fusion.1 = bf16[512,64]{1,0:T(8,128)(2,1)} fusion(f32[512,5120]{1,0:T(8,128)S(1)} %fusion.28, bf16[5120,64]{0,1:T(8,128)(2,1)S(1)} %reshape.57), kind=kOutput, calls=%fused_computation.12 | convolution fusion | flops 2013298688 | bytes 11206656 | tf_op jit(solution)/shard_map/dot_general | solution.py:98
  250.2 0.0 reduce-scatter.2.cloned.1.call-update
  250.2 81.9 %reduce-scatter.2.cloned.1.call-done = bf16[32,64]{1,0:T(8,128)(2,1)} async-done(((bf16[512,64]{1,0:T(8,128)(2,1)}), bf16[32,64]{1,0:T(8,128)(2,1)}) %reduce-scatter.2.cloned.1.call-update) | async-done | bytes 4112 | tf_op jit(solution)/shard_map/reduce_scatter | solution.py:97
  332.1 1.3 fusion.14
  333.4 34.8 %all-gather = f32[1024,64]{1,0:T(8,128)S(1)} all-gather(f32[32,64]{1,0:T(8,128)S(1)} %get-tuple-element.126), channel_id=2, replica_groups=mesh['tm'=32,'seq'=16] {'tm'}, dimensions={0}, use_global_device_ids=true | all-gather | bytes 270336 | tf_op jit(solution)/shard_map/all_gather | solution.py:15
  368.2 1.1 while.18
  369.4 0.6 add_bitcast_fusion
  (43 shorter events, 0.3 us)
Async XLA Ops:
  7.2 1.1 copy-start
  7.2 5.8 %copy-start.4 = (s32[1,2]{1,0:T(1,128)S(1)}, s32[1,2]{1,0:T(1,128)}, u32[]{:S(2)}) copy-start(s32[1,2]{1,0:T(1,128)} %param.16) | copy-start | bytes 28
  7.2 7.7 %copy-start.1 = (bf16[64,160]{1,0:T(8,128)(2,1)S(1)}, bf16[64,160]{1,0:T(8,128)(2,1)}, u32[]{:S(2)}) copy-start(bf16[64,160]{1,0:T(8,128)(2,1)} %param.23) | copy-start | bytes 61444
  7.2 81.4 %all-gather.6.cloned.1.call-start = ((), (), s32[]{:S(2)}) async-start(), calls=%async_computation.1 | async-start | bytes 5570560 | tf_op jit(solution)/shard_map/all_gather | solution.py:80
  11.4 158.4 %all-gather.8.cloned.1.call-start = ((), (), s32[]{:S(2)}) async-start(), calls=%async_computation.2 | async-start | bytes 8110080 | tf_op jit(solution)/shard_map/all_gather | solution.py:79
  12.2 229.0 %all-gather.10.cloned.1.call-start = ((), (), s32[]{:S(2)}) async-start(), calls=%async_computation.3 | async-start | bytes 2703360 | tf_op jit(solution)/shard_map/all_gather | solution.py:92
  12.9 319.2 %reduce-scatter.2.cloned.1.call-start = ((), (), s32[]{:S(2)}) async-start(), calls=%async_computation.4 | async-start | bytes 139264 | tf_op jit(solution)/shard_map/reduce_scatter | solution.py:97
  244.5 5.7 %copy-start.5 = (f32[1,64]{1,0:T(1,128)S(1)}, f32[1,64]{1,0:T(1,128)}, u32[]{:S(2)}) copy-start(f32[1,64]{1,0:T(1,128)} %param.19) | copy-start | bytes 772
  244.5 87.5 %copy-start.2 = (f32[1,32,64]{2,1,0:T(8,128)S(1)}, f32[1,32,64]{2,1,0:T(8,128)}, u32[]{:S(2)}) copy-start(f32[1,32,64]{2,1,0:T(8,128)} %param.15) | copy-start | bytes 24580
  244.5 124.8 %copy-start.3 = (f32[32,64]{1,0:T(8,128)S(1)}, f32[32,64]{1,0:T(8,128)}, u32[]{:S(2)}) copy-start(f32[32,64]{1,0:T(8,128)} %param.14) | copy-start | bytes 24580
Sparse Core Ops, SparseCore 0:
  11.5 76.9 all-gather.5
  90.7 79.0 all-gather.7
  171.9 69.2 all-gather.9
  250.3 81.7 reduce-scatter.1
where the time goes:
time: 377 us
  waiting for transfers between devices  256 us (68%)
  blocking collectives  75.3 us (20%)
  matrix products  21.3 us (6%)
  between operations  15.4 us (4%)
  other arithmetic  4.01 us (1%)
  local copies, waits for them, and re-layouts  3.94 us (1%)
    reduce_scatter x1, waiting for transfers between devices, per_device(): lax.psum_scatter(jnp.dot(mixed, head_float.T, precision=lax.Precision.HIG...  81.9 us
    all_gather x1, waiting for transfers between devices, per_device(): full_qkv = lax.all_gather(qkv_weight, 'tm', axis=1, tiled=True)  81.2 us
    all_gather x1, waiting for transfers between devices, per_device(): lax.all_gather(out_weight, 'tm', axis=1, tiled=True)  60.3 us
    all_gather x1, blocking collectives, per_device(): lax.all_gather(head_weight, 'tm', axis=1, tiled=True)  40.4 us
    all_gather x1, blocking collectives, entering(): pieces = lax.all_gather(value, axis)  34.8 us
    all_gather x1, waiting for transfers between devices, per_device(): everyone = lax.all_gather(modded, 'seq', axis=0, tiled=True)  30.9 us
    dot_general x1, matrix products, per_device(): jnp.einsum('td,idc->itc', everyone, full_qkv, preferred_element_type=jnp....  9.06 us
  transfers between devices with their start and end apart: 4, of which 4 were waited for; matrix products, arithmetic and copies ran while one was open for 4% of the time, Pallas kernels for 0%

commit v1 on v0

v1 whole, which is shorter than its diff:
```python
import functools
import math

import jax
import jax.numpy as jnp
from jax import lax
from jax.experimental import pallas as pl
from jax.experimental.pallas import tpu as pltpu
from jax.sharding import PartitionSpec as P

HEAD = 128
NT = 1000
F32 = jnp.float32
BF16 = jnp.bfloat16
VMEM_LIMIT = 56 * 1024 * 1024
GROUPS = (10, 3, 3)


def sigma_of(level_ids):
    fraction = (level_ids.astype(F32) + 1.0) / NT
    return 5.0 * fraction / (1.0 + 4.0 * fraction)


def dot_nt(a, b):
    return lax.dot_general(a, b, (((1,), (1,)), ((), ())), preferred_element_type=F32)


def dot_nn(a, b):
    return lax.dot_general(a, b, (((1,), (0,)), ((), ())), preferred_element_type=F32)


def split_two(value):
    high = value.astype(BF16)
    return high, (value - high.astype(F32)).astype(BF16)


def kernel_call(body, out_shape, n_in, n_smem=0, flops=0, moved=0, aliases=None):
    one = pl.BlockSpec(memory_space=pltpu.VMEM)
    scalar = pl.BlockSpec(memory_space=pltpu.SMEM)
    many = isinstance(out_shape, (tuple, list))
    return pl.pallas_call(
        body,
        out_shape=out_shape,
        in_specs=[scalar] * n_smem + [one] * n_in,
        out_specs=[one] * len(out_shape) if many else one,
        input_output_aliases=aliases or {},
        compiler_params=pltpu.CompilerParams(vmem_limit_bytes=VMEM_LIMIT),
        cost_estimate=pl.CostEstimate(flops=flops, bytes_accessed=moved, transcendentals=0),
    )


def pack_weights(qkv_ref, out_ref, head_ref, chunk_ref):
    count, rows, _ = qkv_ref.shape
    for i in range(count):
        chunk_ref[i * rows : (i + 1) * rows, :] = qkv_ref[i]
    chunk_ref[count * rows :, :] = dot_nt(head_ref[...], out_ref[...]).astype(BF16)


def pack_context(core_ref, states_ref, embed_ref, context_ref, mods_ref, payload_ref, embed_out, mine_ref, other_ref):
    chips, _, rows = embed_out.shape
    peers = payload_ref.shape[0]
    tokens, width = context_ref.shape
    channels = embed_ref.shape[0]
    second = core_ref[0] == 1
    latent = states_ref[...].astype(BF16)
    context = context_ref[...].astype(F32)
    hidden = dot_nn(latent, embed_ref[...]) + context
    scale = lax.rsqrt(jnp.mean(hidden * hidden, axis=-1, keepdims=True) + 1e-06)

    def halves(value):
        moved = pltpu.roll(value, width - rows, 1)
        return jnp.where(second, moved, value), jnp.where(second, value, moved)

    mine, _ = halves(context)
    for j in range(chips):
        payload_ref[0, :, j * rows : (j + 1) * rows] = mine[:, 2 * j * rows : (2 * j + 1) * rows].astype(BF16)
    high, low = split_two(scale)
    base = chips * rows
    lane = lax.broadcasted_iota(jnp.int32, (tokens, 128), 1)
    tail = jnp.concatenate([latent.astype(F32), jnp.zeros((tokens, 128 - channels), F32)], axis=1)
    tail = jnp.where(lane == channels, high.astype(F32), tail)
    tail = jnp.where(lane == channels + 1, low.astype(F32), tail)
    payload_ref[0, :, base:] = tail.astype(BF16)
    for p in range(1, peers):
        payload_ref[p] = payload_ref[0]
    mine, _ = halves(embed_ref[...].astype(F32))
    for j in range(chips):
        embed_out[j] = mine[:, 2 * j * rows : (2 * j + 1) * rows].astype(BF16)
    mine, other = halves(mods_ref[...])
    for j in range(chips):
        mine_ref[j] = mine[:, 2 * j * rows : (2 * j + 1) * rows]
        other_ref[j] = other[:, 2 * j * rows : (2 * j + 1) * rows]


def cut_context(full_ref, blocks_ref, tail_ref):
    chips, _, rows = blocks_ref.shape
    for j in range(chips):
        blocks_ref[j] = full_ref[:, j * rows : (j + 1) * rows]
    tail_ref[...] = full_ref[:, chips * rows :]


def project(chunk_count, first, last, *refs):
    where_ref, blocks_ref, embed_ref, mine_ref, other_ref = refs[:5]
    chunk_refs = refs[5 : 5 + chunk_count]
    refs = refs[5 + chunk_count :]
    if not first:
        sums_ref, heads_ref = refs[:2]
        refs = refs[2:]
    rows = blocks_ref.shape[2]
    half = blocks_ref.shape[1] + embed_ref.shape[1] + 16
    count = 3
    total = [None] * count
    heads = None if first else heads_ref[...]
    for at, chunk_ref in enumerate(chunk_refs):
        chip = where_ref[at]
        context = blocks_ref[chip].astype(F32)
        embed = embed_ref[chip].astype(F32)
        parts = []
        for mods_ref in (mine_ref, other_ref):
            mods = mods_ref[chip]
            gain = 1.0 + mods[1:2]
            parts.append((context * gain).astype(BF16))
            parts.append((embed * gain).astype(BF16))
            row = lax.broadcasted_iota(jnp.int32, (16, rows), 0)
            parts.append(jnp.where(row == 0, mods[0:1], 0.0).astype(BF16))
        left = jnp.concatenate(parts, axis=0)
        for i in range(count):
            term = dot_nn(left, chunk_ref[i * rows : (i + 1) * rows, :])
            total[i] = term if total[i] is None else total[i] + term
        share = chunk_ref[count * rows :, :].astype(F32)
        heads = share if heads is None else heads + share
    if not first:
        total = [total[i] + sums_ref[i] for i in range(count)]
    if last:
        own_ref, send_ref = refs
        for i in range(count):
            own_ref[i * half : (i + 1) * half, :] = total[i][:half]
            send_ref[i * half : (i + 1) * half, :] = total[i][half:].astype(BF16)
        own_ref[count * half :, :] = heads
        send_ref[count * half :, :] = heads.astype(BF16)
    else:
        sums_out, heads_out = refs
        for i in range(count):
            sums_out[i] = total[i]
        heads_out[...] = heads


def attend(own_ref, got_ref, tail_ref, out_ref):
    peers, pair_rows, lanes = out_ref.shape
    channels = lanes // 2
    tokens = tail_ref.shape[0]
    half = tokens + channels + 16
    latent = tail_ref[:, :channels]
    scale = tail_ref[:, channels : channels + 1].astype(F32) + tail_ref[:, channels + 1 : channels + 2].astype(F32)
    made = []
    for i in range(3):
        at = i * half
        body = own_ref[at : at + tokens, :] + got_ref[at : at + tokens, :].astype(F32)
        at += tokens
        embed = own_ref[at : at + channels, :] + got_ref[at : at + channels, :].astype(F32)
        at += channels
        shift = own_ref[at : at + 16, :] + got_ref[at : at + 16, :].astype(F32)
        high, low = split_two(embed)
        body = body + dot_nn(latent, high) + dot_nn(latent, low)
        made.append((body * scale + shift[0:1]).astype(BF16))
    queries, keys, values = made
    outs = []
    for h in range(queries.shape[1] // HEAD):
        cols = slice(h * HEAD, (h + 1) * HEAD)
        scores = dot_nt(queries[:, cols], keys[:, cols]) * (1.0 / math.sqrt(HEAD))
        weights = jnp.exp(scores - jnp.max(scores, axis=-1, keepdims=True))
        total = jnp.sum(weights, axis=-1, keepdims=True)
        outs.append((dot_nn(weights.astype(BF16), values[:, cols]) / total).astype(BF16))
    attended = jnp.concatenate(outs, axis=1)
    heads = own_ref[3 * half :, :] + got_ref[3 * half :, :].astype(F32)
    high, low = split_two(heads)
    result = dot_nt(attended, high) + dot_nt(attended, low)
    for p in range(peers):
        at = 2 * p * pair_rows
        block = jnp.concatenate([result[at : at + pair_rows], result[at + pair_rows : at + 2 * pair_rows]], axis=1)
        out_ref[p] = block.astype(BF16)


def per_device(
    states, initial, noise_draws, timesteps, context, modulation, out_gate, embed_weight, qkv_weight, out_weight, head_weight
):
    steps, peers = lax.axis_size("tm"), lax.axis_size("seq")
    chips = steps // 2
    mine = lax.axis_index("tm")
    z, core = mine // 2, mine % 2
    tokens_here, channels = initial.shape
    width = context.shape[1]
    rows = qkv_weight.shape[1]
    cols = qkv_weight.shape[2]
    tokens = tokens_here * peers
    half = tokens + channels + 16
    shape = jax.ShapeDtypeStruct

    flip = [(i, i ^ 1) for i in range(steps)]
    forth = [(i, (i + (2 if i % 2 == 0 else -2)) % steps) for i in range(steps)]
    back = [(b, a) for a, b in forth]

    payload, embed_blocks, mods_mine, mods_other = kernel_call(
        pack_context,
        (
            shape((peers, tokens_here, chips * rows + 128), BF16),
            shape((chips, channels, rows), BF16),
            shape((chips, 2, rows), F32),
            shape((chips, 2, rows), F32),
        ),
        4,
        1,
        flops=2 * tokens_here * channels * width,
        moved=5000000,
    )(core[None], states[0], embed_weight, context, modulation[0])
    gathered = lax.all_to_all(payload, "seq", 0, 0).reshape(tokens, chips * rows + 128)

    chunk = kernel_call(
        pack_weights, shape((3 * rows + channels, cols), BF16), 3, flops=2 * channels * rows * cols, moved=700000
    )(qkv_weight, out_weight, head_weight)
    mods_sibling = lax.ppermute(mods_other, "tm", flip)

    sign = 1 - 2 * core
    arrived, places = [chunk], [z]
    ahead = behind = chunk
    for k in range(1, chips // 2 + 1):
        ahead = lax.ppermute(ahead, "tm", forth)
        arrived.append(ahead)
        places.append((z - sign * k) % chips)
        if k < chips // 2:
            behind = lax.ppermute(behind, "tm", back)
            arrived.append(behind)
            places.append((z + sign * k) % chips)
    places = jnp.stack(places).astype(jnp.int32)

    blocks, tail = kernel_call(
        cut_context, (shape((chips, tokens, rows), BF16), shape((tokens, 128), BF16)), 1, moved=8000000
    )(gathered)

    groups = GROUPS if sum(GROUPS) == len(arrived) else (len(arrived) - 1, 1)
    at, sums = 0, ()
    for g, size in enumerate(groups):
        first, last = g == 0, g == len(groups) - 1
        if last:
            out_shape = (shape((3 * half + channels, cols), F32), shape((3 * half + channels, cols), BF16))
        else:
            out_shape = (shape((3, 2 * half, cols), F32), shape((channels, cols), F32))
        sums = kernel_call(
            functools.partial(project, size, first, last),
            out_shape,
            4 + size + len(sums),
            1,
            flops=size * 2 * 2 * half * rows * 3 * cols,
            moved=8000000,
        )(places[at : at + size], blocks, embed_blocks, mods_mine, mods_sibling, *arrived[at : at + size], *sums)
        at += size
    own, send = sums
    got = lax.ppermute(send, "tm", flip)

    pair_rows = tokens_here // 2
    shares = kernel_call(
        attend, shape((peers, pair_rows, 2 * channels), BF16), 3, flops=600000000, moved=4000000
    )(own, got, tail)
    shares = lax.all_to_all(shares, "seq", 0, 0)
    mixed = jnp.sum(shares.astype(F32), axis=0)

    def pairs(value):
        return jnp.concatenate([value[:pair_rows], value[pair_rows:]], axis=1)

    def unpairs(value):
        return jnp.concatenate([value[:, :channels], value[:, channels:]], axis=0)

    gate = jnp.concatenate([out_gate, out_gate], axis=1)
    velocity_f = (1.0 + gate) * mixed
    step_size = sigma_of(timesteps[0, 1]) - sigma_of(timesteps[0, 0])
    drift = step_size * velocity_f + jnp.sqrt(-step_size) * pairs(noise_draws[0])
    both = lax.all_gather(drift, "tm", axis_index_groups=[[2 * i, 2 * i + 1] for i in range(chips)])
    same_core = [list(range(0, steps, 2)), list(range(1, steps, 2))]
    spread = jnp.broadcast_to((both[0] + both[1])[None], (chips, pair_rows, 2 * channels))
    everyone = lax.all_to_all(spread, "tm", 0, 0, axis_index_groups=same_core)
    earlier = lax.broadcasted_iota(jnp.int32, (chips, 1, 1), 0) < z
    before = jnp.sum(jnp.where(earlier, everyone, 0.0), axis=0) + jnp.where(core == 1, both[0], 0.0)
    new_states = initial + unpairs(before)
    return (new_states[None], unpairs(velocity_f).astype(BF16)[None])


def solution(mesh):
    in_specs = (
        P("tm", "seq", None),
        P("seq", None),
        P("tm", "seq", None),
        P("tm", None),
        P("seq", None),
        P("tm", None, None),
        P("tm", None),
        P(),
        P(None, "tm", "seq"),
        P("seq", "tm"),
        P(None, "tm"),
    )
    out_specs = (P("tm", "seq", None), P("tm", "seq", None))
    return jax.shard_map(per_device, mesh=mesh, in_specs=in_specs, out_specs=out_specs, check_vma=False)
```

time: 377 us -> 183 us (0.49)
  waiting for transfers between devices: 256 us -> 34.3 us
  starting transfers between devices: 0.16 us -> 94.4 us
  blocking collectives: 75.3 us -> 3.2 us
  Pallas kernels: 0 us -> 37.9 us
  matrix products: 21.3 us -> 0 us
  between operations: 15.4 us -> 2.54 us
    all_gather x3 -> x0, waiting for transfers between devices: 172 us -> none  [the longest x1 81.2 us: per_device(): full_qkv = lax.all_gather(qkv_weight, 'tm', axis=1, tiled=True)]
    reduce_scatter x1 -> x0, waiting for transfers between devices: 81.9 us -> none  [per_device(): lax.psum_scatter(jnp.dot(mixed, head_float.T, precision=lax.Precision.HIG...]
    all_gather x2 -> x1, blocking collectives: 75.3 us -> 3.2 us  [per_device(): lax.all_gather(drift, 'tm', axis_index_groups=[[2 * i, 2 * i + 1] for i i...]
    ppermute x0 -> x17, starting transfers between devices: none -> 71.3 us  [the longest x8 46.3 us: per_device(): ahead = lax.ppermute(ahead, 'tm', forth)]
    pallas_call x0 -> x7, Pallas kernels: none -> 37.9 us  [the longest x3 23.6 us: per_device(): kernel_call(functools.partial(project, size, first, last), out_shape, 4 +...]
    all_to_all x0 -> x3, starting transfers between devices: none -> 23 us  [the longest x1 8.62 us: per_device(): everyone = lax.all_to_all(spread, 'tm', 0, 0, axis_index_groups=same_core)]
    dot_general x5 -> x0, matrix products: 20.5 us -> none  [the longest x1 9.06 us: per_device(): jnp.einsum('td,idc->itc', everyone, full_qkv, preferred_element_type=jnp....]
    all_to_all x0 -> x3, waiting for transfers between devices: none -> 17.9 us  [the longest x1 11.5 us: per_device(): everyone = lax.all_to_all(spread, 'tm', 0, 0, axis_index_groups=same_core)]
  transfers between devices with their start and end apart: 4 -> 20, of which waited for: 4 -> 10; matrix products, arithmetic and copies ran while one was open for 4% -> 2% of each run, Pallas kernels for 0% -> 13%
where the time goes in v1:
time: 183 us; the launch traced here: 181 us
  starting transfers between devices  94.4 us (52%)
  Pallas kernels  37.9 us (21%)
  waiting for transfers between devices  34.3 us (19%)
  local copies, waits for them, and re-layouts  6.09 us (3%)
  blocking collectives  3.2 us (2%)
  other arithmetic  2.81 us (2%)
  between operations  2.54 us (1%)
    ppermute x8, starting transfers between devices, per_device(): ahead = lax.ppermute(ahead, 'tm', forth)  46.3 us
    pallas_call x3, Pallas kernels, per_device(): kernel_call(functools.partial(project, size, first, last), out_shape, 4 +...  23.6 us
    ppermute x7, starting transfers between devices, per_device(): behind = lax.ppermute(behind, 'tm', back)  13.4 us
    ppermute x7, waiting for transfers between devices, per_device(): behind = lax.ppermute(behind, 'tm', back)  12 us
    all_to_all x1, waiting for transfers between devices, per_device(): everyone = lax.all_to_all(spread, 'tm', 0, 0, axis_index_groups=same_core)  11.5 us
    ppermute x1, starting transfers between devices, per_device(): mods_sibling = lax.ppermute(mods_other, 'tm', flip)  9.32 us
    all_to_all x1, starting transfers between devices, per_device(): everyone = lax.all_to_all(spread, 'tm', 0, 0, axis_index_groups=same_core)  8.62 us
    all_to_all x1, starting transfers between devices, per_device(): lax.all_to_all(payload, 'seq', 0, 0).reshape(tokens, chips * rows + 128)  7.72 us
  transfers between devices with their start and end apart: 20, of which 10 were waited for; matrix products, arithmetic and copies ran while one was open for 2% of the time, Pallas kernels for 13%

profile of v1, /device:TPU:1, one launch (start us, length us, event | category | flops | bytes accessed | tf_op | source)
XLA Modules:
  0.0 181.2 jit_solution(10316925203222986975)
XLA Ops:
  0.7 3.5 %shard_map.122 = (bf16[16,32,2688]{2,1,0:T(8,128)(2,1)}, bf16[16,64,160]{2,1,0:T(8,128)(2,1)}, f32[16,2,160]{2,1,0:T(2,128)}, f32[16,2,160]{2,1,0:T(2,128)}) custom-call(s32[1]{0:T(128)} %bitcast.5.core_ref, f32[32,64]{1,0:T(8,128)} %bitcast.40, bf16[64,5120]{1,0:T(8,128)(2,1)} %embed_ref.1, bf16[32,5120]{1,0:T(8,128)(2,1)} %context_ref.1, f32[2,5120]{1,0:T(2,128)} %bitcast.39), custom_call_target="tpu_custom_call" | custom-call | flops 20971520 | bytes 5000000 | tf_op jit(solution)/shard_map/pallas_call | solution.py:203
  4.2 7.7 %all-to-all-start = ((bf16[16,32,2688]{2,1,0:T(8,128)(2,1)}), bf16[16,32,2688]{2,1,0:T(8,128)(2,1)S(1)}, u32[]{:S(2)}, u32[]{:S(2)}) async-start(bf16[16,32,2688]{2,1,0:T(8,128)(2,1)} %get-tuple-element.14), calls=%async_computation | async-start | bytes 5505024 | tf_op jit(solution)/shard_map/all_to_all | solution.py:216
  12.7 1.9 %shard_map.124.refs_5_ = bf16[544,256]{1,0:T(8,128)(2,1)} custom-call(bf16[3,160,256]{2,1,0:T(8,128)(2,1)} %qkv_ref.1, bf16[256,160]{1,0:T(8,128)(2,1)} %copy.15.out_ref, bf16[64,160]{1,0:T(8,128)(2,1)} %head_ref.1), custom_call_target="tpu_custom_call" | custom-call | flops 5242880 | bytes 700000 | tf_op jit(solution)/shard_map/pallas_call | solution.py:218
  14.6 11.1 %collective-permute-start.1 = (bf16[544,256]{1,0:T(8,128)(2,1)}, bf16[544,256]{1,0:T(8,128)(2,1)S(1)}, u32[]{:S(2)}, u32[]{:S(2)}) collective-permute-start(bf16[544,256]{1,0:T(8,128)(2,1)} %shard_map.124.refs_5_), channel_id=1, source_target_pairs={{0,32},{16,496},{32,64},{48,16},{64,96},{80,48},{96,128},{112,80},... | collective-permute-start | bytes 835592 | tf_op jit(solution)/shard_map/ppermute | solution.py:227
  25.7 1.9 %collective-permute-start.8 = (bf16[544,256]{1,0:T(8,128)(2,1)}, bf16[544,256]{1,0:T(8,128)(2,1)S(1)}, u32[]{:S(2)}, u32[]{:S(2)}) collective-permute-start(bf16[544,256]{1,0:T(8,128)(2,1)} %shard_map.124.refs_5_), channel_id=1, source_target_pairs={{32,0},{496,16},{64,32},{16,48},{96,64},{48,80},{128,96},{80,112},... | collective-permute-start | bytes 835592 | tf_op jit(solution)/shard_map/ppermute | solution.py:231
  29.5 5.2 %collective-permute-start.2 = (bf16[544,256]{1,0:T(8,128)(2,1)S(1)}, bf16[544,256]{1,0:T(8,128)(2,1)S(1)}, u32[]{:S(2)}, u32[]{:S(2)}) collective-permute-start(bf16[544,256]{1,0:T(8,128)(2,1)S(1)} %collective-permute-done.1.refs_6_), channel_id=1, source_target_pairs={{0,32},{16,496},{32,64},{48,16},{64,96},{80,48},{96,128},{112,80},... | collective-permute-start | bytes 835592 | tf_op jit(solution)/shard_map/ppermute | solution.py:227
  34.7 1.9 %collective-permute-start.9 = (bf16[544,256]{1,0:T(8,128)(2,1)S(1)}, bf16[544,256]{1,0:T(8,128)(2,1)S(1)}, u32[]{:S(2)}, u32[]{:S(2)}) collective-permute-start(bf16[544,256]{1,0:T(8,128)(2,1)S(1)} %collective-permute-done.8.refs_7_), channel_id=1, source_target_pairs={{32,0},{496,16},{64,32},{16,48},{96,64},{48,80},{128,96},{80,112},... | collective-permute-start | bytes 835592 | tf_op jit(solution)/shard_map/ppermute | solution.py:231
  38.2 5.3 %collective-permute-start.3 = (bf16[544,256]{1,0:T(8,128)(2,1)S(1)}, bf16[544,256]{1,0:T(8,128)(2,1)S(1)}, u32[]{:S(2)}, u32[]{:S(2)}) collective-permute-start(bf16[544,256]{1,0:T(8,128)(2,1)S(1)} %collective-permute-done.2.refs_8_), channel_id=1, source_target_pairs={{0,32},{16,496},{32,64},{48,16},{64,96},{80,48},{96,128},{112,80},... | collective-permute-start | bytes 835592 | tf_op jit(solution)/shard_map/ppermute | solution.py:227
  44.4 1.9 %collective-permute-start.10 = (bf16[544,256]{1,0:T(8,128)(2,1)S(1)}, bf16[544,256]{1,0:T(8,128)(2,1)S(1)}, u32[]{:S(2)}, u32[]{:S(2)}) collective-permute-start(bf16[544,256]{1,0:T(8,128)(2,1)S(1)} %collective-permute-done.9.refs_9_), channel_id=1, source_target_pairs={{32,0},{496,16},{64,32},{16,48},{96,64},{48,80},{128,96},{80,112},... | collective-permute-start | bytes 835592 | tf_op jit(solution)/shard_map/ppermute | solution.py:231
  47.0 5.3 %collective-permute-start.4 = (bf16[544,256]{1,0:T(8,128)(2,1)S(1)}, bf16[544,256]{1,0:T(8,128)(2,1)S(1)}, u32[]{:S(2)}, u32[]{:S(2)}) collective-permute-start(bf16[544,256]{1,0:T(8,128)(2,1)S(1)} %collective-permute-done.3.refs_10_), channel_id=1, source_target_pairs={{0,32},{16,496},{32,64},{48,16},{64,96},{80,48},{96,128},{112,80},... | collective-permute-start | bytes 835592 | tf_op jit(solution)/shard_map/ppermute | solution.py:227
  52.3 2.9 %collective-permute-done.10.refs_11_ = bf16[544,256]{1,0:T(8,128)(2,1)S(1)} collective-permute-done((bf16[544,256]{1,0:T(8,128)(2,1)S(1)}, bf16[544,256]{1,0:T(8,128)(2,1)S(1)}, u32[]{:S(2)}, u32[]{:S(2)}) %collective-permute-start.10) | collective-permute-done | bytes 278560 | tf_op jit(solution)/shard_map/ppermute | solution.py:231
  55.2 1.9 %collective-permute-start.11 = (bf16[544,256]{1,0:T(8,128)(2,1)S(1)}, bf16[544,256]{1,0:T(8,128)(2,1)S(1)}, u32[]{:S(2)}, u32[]{:S(2)}) collective-permute-start(bf16[544,256]{1,0:T(8,128)(2,1)S(1)} %collective-permute-done.10.refs_11_), channel_id=1, source_target_pairs={{32,0},{496,16},{64,32},{16,48},{96,64},{48,80},{128,96},{80,112},... | collective-permute-start | bytes 835592 | tf_op jit(solution)/shard_map/ppermute | solution.py:231
  57.1 4.9 %collective-permute-start.5 = (bf16[544,256]{1,0:T(8,128)(2,1)S(1)}, bf16[544,256]{1,0:T(8,128)(2,1)S(1)}, u32[]{:S(2)}, u32[]{:S(2)}) collective-permute-start(bf16[544,256]{1,0:T(8,128)(2,1)S(1)} %collective-permute-done.4.refs_12_), channel_id=1, source_target_pairs={{0,32},{16,496},{32,64},{48,16},{64,96},{80,48},{96,128},{112,80},... | collective-permute-start | bytes 835592 | tf_op jit(solution)/shard_map/ppermute | solution.py:227
  62.0 4.5 %collective-permute-done.11.refs_13_ = bf16[544,256]{1,0:T(8,128)(2,1)S(1)} collective-permute-done((bf16[544,256]{1,0:T(8,128)(2,1)S(1)}, bf16[544,256]{1,0:T(8,128)(2,1)S(1)}, u32[]{:S(2)}, u32[]{:S(2)}) %collective-permute-start.11) | collective-permute-done | bytes 278560 | tf_op jit(solution)/shard_map/ppermute | solution.py:231
  68.5 4.9 %collective-permute-start.6 = (bf16[544,256]{1,0:T(8,128)(2,1)S(1)}, bf16[544,256]{1,0:T(8,128)(2,1)}, u32[]{:S(2)}, u32[]{:S(2)}) collective-permute-start(bf16[544,256]{1,0:T(8,128)(2,1)S(1)} %collective-permute-done.5.refs_14_), channel_id=1, source_target_pairs={{0,32},{16,496},{32,64},{48,16},{64,96},{80,48},{96,128},{112,80},... | collective-permute-start | bytes 835592 | tf_op jit(solution)/shard_map/ppermute | solution.py:227
  73.3 3.6 %collective-permute-done.12.refs_5_ = bf16[544,256]{1,0:T(8,128)(2,1)S(1)} collective-permute-done((bf16[544,256]{1,0:T(8,128)(2,1)S(1)}, bf16[544,256]{1,0:T(8,128)(2,1)S(1)}, u32[]{:S(2)}, u32[]{:S(2)}) %collective-permute-start.12) | collective-permute-done | bytes 278560 | tf_op jit(solution)/shard_map/ppermute | solution.py:231
  77.0 1.9 %collective-permute-start.13 = (bf16[544,256]{1,0:T(8,128)(2,1)S(1)}, bf16[544,256]{1,0:T(8,128)(2,1)}, u32[]{:S(2)}, u32[]{:S(2)}) collective-permute-start(bf16[544,256]{1,0:T(8,128)(2,1)S(1)} %collective-permute-done.12.refs_5_), channel_id=1, source_target_pairs={{32,0},{496,16},{64,32},{16,48},{96,64},{48,80},{128,96},{80,112},... | collective-permute-start | bytes 835592 | tf_op jit(solution)/shard_map/ppermute | solution.py:231
  78.9 4.8 %collective-permute-start.7 = (bf16[544,256]{1,0:T(8,128)(2,1)}, bf16[544,256]{1,0:T(8,128)(2,1)S(1)}, u32[]{:S(2)}, u32[]{:S(2)}) collective-permute-start(bf16[544,256]{1,0:T(8,128)(2,1)} %collective-permute-done.6.refs_6_), channel_id=1, source_target_pairs={{0,32},{16,496},{32,64},{48,16},{64,96},{80,48},{96,128},{112,80},... | collective-permute-start | bytes 835592 | tf_op jit(solution)/shard_map/ppermute | solution.py:227
  83.8 9.3 %collective-permute-start = (f32[16,2,160]{2,1,0:T(2,128)S(1)}, f32[16,2,160]{2,1,0:T(2,128)S(1)}, u32[]{:S(2)}, u32[]{:S(2)}) collective-permute-start(f32[16,2,160]{2,1,0:T(2,128)S(1)} %copy-done.18), channel_id=1, source_target_pairs={{0,16},{16,0},{32,48},{48,32},{64,80},{80,64},{96,112},{112,96},{1... | collective-permute-start | bytes 61448 | tf_op jit(solution)/shard_map/ppermute | solution.py:221
  95.3 1.9 %collective-permute-start.14 = (bf16[544,256]{1,0:T(8,128)(2,1)}, bf16[544,256]{1,0:T(8,128)(2,1)}, u32[]{:S(2)}, u32[]{:S(2)}) collective-permute-start(bf16[544,256]{1,0:T(8,128)(2,1)} %collective-permute-done.13.refs_7_), channel_id=1, source_target_pairs={{32,0},{496,16},{64,32},{16,48},{96,64},{48,80},{128,96},{80,112},... | collective-permute-start | bytes 835592 | tf_op jit(solution)/shard_map/ppermute | solution.py:231
  97.2 4.9 %collective-permute-start.15 = (bf16[544,256]{1,0:T(8,128)(2,1)S(1)}, bf16[544,256]{1,0:T(8,128)(2,1)}, u32[]{:S(2)}, u32[]{:S(2)}) collective-permute-start(bf16[544,256]{1,0:T(8,128)(2,1)S(1)} %collective-permute-done.7.refs_5_), channel_id=1, source_target_pairs={{0,32},{16,496},{32,64},{48,16},{64,96},{80,48},{96,128},{112,80},... | collective-permute-start | bytes 835592 | tf_op jit(solution)/shard_map/ppermute | solution.py:227
  103.6 4.7 %shard_map.123 = (bf16[16,512,160]{2,1,0:T(8,128)(2,1)}, bf16[512,128]{1,0:T(8,128)(2,1)}) custom-call(bf16[512,2688]{1,0:T(8,128)(2,1)} %bitcast.38), custom_call_target="tpu_custom_call" | custom-call | bytes 8000000 | tf_op jit(solution)/shard_map/pallas_call | solution.py:236
  108.9 9.8 %shard_map.125 = (f32[3,1184,256]{2,1,0:T(8,128)}, f32[64,256]{1,0:T(8,128)}) custom-call(s32[10]{0:T(128)} %stack.73.refs_0_, bf16[16,512,160]{2,1,0:T(8,128)(2,1)} %get-tuple-element.15.refs_1_, bf16[16,64,160]{2,1,0:T(8,128)(2,1)} %get-tuple-element.16.refs_2_, f32[16,2,160]{2,1,0:T(2,128)} %get-tuple-element.17.refs_3_, f32[16,2,160]{2,1,0:T(2,128)} %copy-done.4, ...), custom_call_target="tpu_custom_call" | custom-call | flops 2909798400 | bytes 8000000 | tf_op jit(solution)/shard_map/pallas_call | solution.py:248
  118.7 7.0 %shard_map.126 = (f32[3,1184,256]{2,1,0:T(8,128)}, f32[64,256]{1,0:T(8,128)}) custom-call(s32[3]{0:T(128)} %pad_add_fusion.1.refs_0_, bf16[16,512,160]{2,1,0:T(8,128)(2,1)} %get-tuple-element.15.refs_1_, bf16[16,64,160]{2,1,0:T(8,128)(2,1)} %get-tuple-element.16.refs_2_, f32[16,2,160]{2,1,0:T(2,128)} %get-tuple-element.17.refs_3_, f32[16,2,160]{2,1,0:T(2,128)} %copy-done.4, ...), custom_call_target="tpu_custom_call" | custom-call | flops 872939520 | bytes 8000000 | tf_op jit(solution)/shard_map/pallas_call | solution.py:248
  125.8 6.7 %shard_map.127 = (f32[1840,256]{1,0:T(8,128)}, bf16[1840,256]{1,0:T(8,128)(2,1)}) custom-call(s32[3]{0:T(128)} %pad_add_fusion.refs_0_, bf16[16,512,160]{2,1,0:T(8,128)(2,1)} %get-tuple-element.15.refs_1_, bf16[16,64,160]{2,1,0:T(8,128)(2,1)} %get-tuple-element.16.refs_2_, f32[16,2,160]{2,1,0:T(2,128)} %get-tuple-element.17.refs_3_, ...), custom_call_target="tpu_custom_call" | custom-call | flops 872939520 | bytes 8000000 | tf_op jit(solution)/shard_map/pallas_call | solution.py:248
  132.5 2.3 %collective-permute-start.16 = (bf16[1840,256]{1,0:T(8,128)(2,1)}, bf16[1840,256]{1,0:T(8,128)(2,1)S(1)}, u32[]{:S(2)}, u32[]{:S(2)}) collective-permute-start(bf16[1840,256]{1,0:T(8,128)(2,1)} %get-tuple-element.24), channel_id=1, source_target_pairs={{0,16},{16,0},{32,48},{48,32},{64,80},{80,64},{96,112},{112,96},{1... | collective-permute-start | bytes 2826248 | tf_op jit(solution)/shard_map/ppermute | solution.py:258
  138.2 4.2 %shard_map.128 = bf16[16,16,128]{2,1,0:T(8,128)(2,1)} custom-call(f32[1840,256]{1,0:T(8,128)} %get-tuple-element.23.own_ref, bf16[1840,256]{1,0:T(8,128)(2,1)} %copy-done.1, bf16[512,128]{1,0:T(8,128)(2,1)} %get-tuple-element.25.tail_ref), custom_call_target="tpu_custom_call" | custom-call | flops 600000000 | bytes 4000000 | tf_op jit(solution)/shard_map/pallas_call | solution.py:261
  142.5 6.7 %all-to-all-start.1 = ((bf16[16,16,128]{2,1,0:T(8,128)(2,1)}), bf16[16,16,128]{2,1,0:T(8,128)(2,1)S(1)}, u32[]{:S(2)}, u32[]{:S(2)}) async-start(bf16[16,16,128]{2,1,0:T(8,128)(2,1)} %shard_map.128), calls=%async_computation.1 | async-start | bytes 131072 | tf_op jit(solution)/shard_map/all_to_all | solution.py:264
  149.3 6.4 %all-to-all-done.1 = bf16[16,16,128]{2,1,0:T(8,128)(2,1)S(1)} async-done(((bf16[16,16,128]{2,1,0:T(8,128)(2,1)}), bf16[16,16,128]{2,1,0:T(8,128)(2,1)S(1)}, u32[]{:S(2)}, u32[]{:S(2)}) %all-to-all-start.1) | async-done | bytes 65568 | tf_op jit(solution)/shard_map/all_to_all | solution.py:264
  155.8 3.2 %all_gather.4 = f32[2,16,128]{2,1,0:T(8,128)S(1)} all-gather(f32[1,16,128]{2,1,0:T(8,128)S(1)} %fusion.2), channel_id=1, replica_groups={{0,16},{32,48},{64,80},{96,112},{128,144},{160,176},{192,208},{224,240}..., dimensions={0}, use_global_device_ids=true | all-gather | bytes 24576 | tf_op jit(solution)/shard_map/all_gather | solution.py:277
  159.7 8.6 %all-to-all-start.2 = ((f32[16,16,128]{2,1,0:T(8,128)}), f32[16,16,128]{2,1,0:T(8,128)S(1)}, u32[]{:S(2)}, u32[]{:S(2)}) async-start(f32[16,16,128]{2,1,0:T(8,128)} %broadcast_in_dim.34), calls=%async_computation.2 | async-start | bytes 262144 | tf_op jit(solution)/shard_map/all_to_all | solution.py:280
  169.0 11.5 %all-to-all-done.2 = f32[16,16,128]{2,1,0:T(8,128)S(1)} async-done(((f32[16,16,128]{2,1,0:T(8,128)}), f32[16,16,128]{2,1,0:T(8,128)S(1)}, u32[]{:S(2)}, u32[]{:S(2)}) %all-to-all-start.2) | async-done | bytes 131104 | tf_op jit(solution)/shard_map/all_to_all | solution.py:280
  (75 shorter events, 16.2 us)
Async XLA Ops:
  4.2 79.6 %copy-start.18 = (f32[16,2,160]{2,1,0:T(2,128)S(1)}, f32[16,2,160]{2,1,0:T(2,128)}, u32[]{:S(2)}) copy-start(f32[16,2,160]{2,1,0:T(2,128)} %get-tuple-element.18) | copy-start | bytes 61444
  4.2 97.9 %all-to-all-start = ((bf16[16,32,2688]{2,1,0:T(8,128)(2,1)}), bf16[16,32,2688]{2,1,0:T(8,128)(2,1)S(1)}, u32[]{:S(2)}, u32[]{:S(2)}) async-start(bf16[16,32,2688]{2,1,0:T(8,128)(2,1)} %get-tuple-element.14), calls=%async_computation | async-start | bytes 5505024 | tf_op jit(solution)/shard_map/all_to_all | solution.py:216
  14.6 14.9 %collective-permute-start.1 = (bf16[544,256]{1,0:T(8,128)(2,1)}, bf16[544,256]{1,0:T(8,128)(2,1)S(1)}, u32[]{:S(2)}, u32[]{:S(2)}) collective-permute-start(bf16[544,256]{1,0:T(8,128)(2,1)} %shard_map.124.refs_5_), channel_id=1, source_target_pairs={{0,32},{16,496},{32,64},{48,16},{64,96},{80,48},{96,128},{112,80},... | collective-permute-start | bytes 835592 | tf_op jit(solution)/shard_map/ppermute | solution.py:227
  25.7 9.0 %collective-permute-start.8 = (bf16[544,256]{1,0:T(8,128)(2,1)}, bf16[544,256]{1,0:T(8,128)(2,1)S(1)}, u32[]{:S(2)}, u32[]{:S(2)}) collective-permute-start(bf16[544,256]{1,0:T(8,128)(2,1)} %shard_map.124.refs_5_), channel_id=1, source_target_pairs={{32,0},{496,16},{64,32},{16,48},{96,64},{48,80},{128,96},{80,112},... | collective-permute-start | bytes 835592 | tf_op jit(solution)/shard_map/ppermute | solution.py:231
  29.5 32.5 %copy-start.9 = (bf16[544,256]{1,0:T(8,128)(2,1)}, bf16[544,256]{1,0:T(8,128)(2,1)S(1)}, u32[]{:S(2)}) copy-start(bf16[544,256]{1,0:T(8,128)(2,1)S(1)} %collective-permute-done.1.refs_6_) | copy-start | bytes 835588
  29.5 8.7 %collective-permute-start.2 = (bf16[544,256]{1,0:T(8,128)(2,1)S(1)}, bf16[544,256]{1,0:T(8,128)(2,1)S(1)}, u32[]{:S(2)}, u32[]{:S(2)}) collective-permute-start(bf16[544,256]{1,0:T(8,128)(2,1)S(1)} %collective-permute-done.1.refs_6_), channel_id=1, source_target_pairs={{0,32},{16,496},{32,64},{48,16},{64,96},{80,48},{96,128},{112,80},... | collective-permute-start | bytes 835592 | tf_op jit(solution)/shard_map/ppermute | solution.py:227
  34.7 44.2 %copy-start.10 = (bf16[544,256]{1,0:T(8,128)(2,1)}, bf16[544,256]{1,0:T(8,128)(2,1)S(1)}, u32[]{:S(2)}) copy-start(bf16[544,256]{1,0:T(8,128)(2,1)S(1)} %collective-permute-done.8.refs_7_) | copy-start | bytes 835588
  34.7 9.7 %collective-permute-start.9 = (bf16[544,256]{1,0:T(8,128)(2,1)S(1)}, bf16[544,256]{1,0:T(8,128)(2,1)S(1)}, u32[]{:S(2)}, u32[]{:S(2)}) collective-permute-start(bf16[544,256]{1,0:T(8,128)(2,1)S(1)} %collective-permute-done.8.refs_7_), channel_id=1, source_target_pairs={{32,0},{496,16},{64,32},{16,48},{96,64},{48,80},{128,96},{80,112},... | collective-permute-start | bytes 835592 | tf_op jit(solution)/shard_map/ppermute | solution.py:231
  38.2 45.6 %copy-start.11 = (bf16[544,256]{1,0:T(8,128)(2,1)}, bf16[544,256]{1,0:T(8,128)(2,1)S(1)}, u32[]{:S(2)}) copy-start(bf16[544,256]{1,0:T(8,128)(2,1)S(1)} %collective-permute-done.2.refs_8_) | copy-start | bytes 835588
  38.2 8.8 %collective-permute-start.3 = (bf16[544,256]{1,0:T(8,128)(2,1)S(1)}, bf16[544,256]{1,0:T(8,128)(2,1)S(1)}, u32[]{:S(2)}, u32[]{:S(2)}) collective-permute-start(bf16[544,256]{1,0:T(8,128)(2,1)S(1)} %collective-permute-done.2.refs_8_), channel_id=1, source_target_pairs={{0,32},{16,496},{32,64},{48,16},{64,96},{80,48},{96,128},{112,80},... | collective-permute-start | bytes 835592 | tf_op jit(solution)/shard_map/ppermute | solution.py:227
  44.4 39.3 %copy-start.12 = (bf16[544,256]{1,0:T(8,128)(2,1)}, bf16[544,256]{1,0:T(8,128)(2,1)S(1)}, u32[]{:S(2)}) copy-start(bf16[544,256]{1,0:T(8,128)(2,1)S(1)} %collective-permute-done.9.refs_9_) | copy-start | bytes 835588
  44.4 10.8 %collective-permute-start.10 = (bf16[544,256]{1,0:T(8,128)(2,1)S(1)}, bf16[544,256]{1,0:T(8,128)(2,1)S(1)}, u32[]{:S(2)}, u32[]{:S(2)}) collective-permute-start(bf16[544,256]{1,0:T(8,128)(2,1)S(1)} %collective-permute-done.9.refs_9_), channel_id=1, source_target_pairs={{32,0},{496,16},{64,32},{16,48},{96,64},{48,80},{128,96},{80,112},... | collective-permute-start | bytes 835592 | tf_op jit(solution)/shard_map/ppermute | solution.py:231
  47.0 36.8 %copy-start.13 = (bf16[544,256]{1,0:T(8,128)(2,1)}, bf16[544,256]{1,0:T(8,128)(2,1)S(1)}, u32[]{:S(2)}) copy-start(bf16[544,256]{1,0:T(8,128)(2,1)S(1)} %collective-permute-done.3.refs_10_) | copy-start | bytes 835588
  47.0 10.2 %collective-permute-start.4 = (bf16[544,256]{1,0:T(8,128)(2,1)S(1)}, bf16[544,256]{1,0:T(8,128)(2,1)S(1)}, u32[]{:S(2)}, u32[]{:S(2)}) collective-permute-start(bf16[544,256]{1,0:T(8,128)(2,1)S(1)} %collective-permute-done.3.refs_10_), channel_id=1, source_target_pairs={{0,32},{16,496},{32,64},{48,16},{64,96},{80,48},{96,128},{112,80},... | collective-permute-start | bytes 835592 | tf_op jit(solution)/shard_map/ppermute | solution.py:227
  55.2 28.6 %copy-start.14 = (bf16[544,256]{1,0:T(8,128)(2,1)}, bf16[544,256]{1,0:T(8,128)(2,1)S(1)}, u32[]{:S(2)}) copy-start(bf16[544,256]{1,0:T(8,128)(2,1)S(1)} %collective-permute-done.10.refs_11_) | copy-start | bytes 835588
  55.2 11.3 %collective-permute-start.11 = (bf16[544,256]{1,0:T(8,128)(2,1)S(1)}, bf16[544,256]{1,0:T(8,128)(2,1)S(1)}, u32[]{:S(2)}, u32[]{:S(2)}) collective-permute-start(bf16[544,256]{1,0:T(8,128)(2,1)S(1)} %collective-permute-done.10.refs_11_), channel_id=1, source_target_pairs={{32,0},{496,16},{64,32},{16,48},{96,64},{48,80},{128,96},{80,112},... | collective-permute-start | bytes 835592 | tf_op jit(solution)/shard_map/ppermute | solution.py:231
  57.1 26.6 %copy-start.15 = (bf16[544,256]{1,0:T(8,128)(2,1)}, bf16[544,256]{1,0:T(8,128)(2,1)S(1)}, u32[]{:S(2)}) copy-start(bf16[544,256]{1,0:T(8,128)(2,1)S(1)} %collective-permute-done.4.refs_12_) | copy-start | bytes 835588
  57.1 11.3 %collective-permute-start.5 = (bf16[544,256]{1,0:T(8,128)(2,1)S(1)}, bf16[544,256]{1,0:T(8,128)(2,1)S(1)}, u32[]{:S(2)}, u32[]{:S(2)}) collective-permute-start(bf16[544,256]{1,0:T(8,128)(2,1)S(1)} %collective-permute-done.4.refs_12_), channel_id=1, source_target_pairs={{0,32},{16,496},{32,64},{48,16},{64,96},{80,48},{96,128},{112,80},... | collective-permute-start | bytes 835592 | tf_op jit(solution)/shard_map/ppermute | solution.py:227
  66.5 10.4 %collective-permute-start.12 = (bf16[544,256]{1,0:T(8,128)(2,1)S(1)}, bf16[544,256]{1,0:T(8,128)(2,1)S(1)}, u32[]{:S(2)}, u32[]{:S(2)}) collective-permute-start(bf16[544,256]{1,0:T(8,128)(2,1)S(1)} %collective-permute-done.11.refs_13_), channel_id=1, source_target_pairs={{32,0},{496,16},{64,32},{16,48},{96,64},{48,80},{128,96},{80,112},... | collective-permute-start | bytes 835592 | tf_op jit(solution)/shard_map/ppermute | solution.py:231
  68.5 10.4 %collective-permute-start.6 = (bf16[544,256]{1,0:T(8,128)(2,1)S(1)}, bf16[544,256]{1,0:T(8,128)(2,1)}, u32[]{:S(2)}, u32[]{:S(2)}) collective-permute-start(bf16[544,256]{1,0:T(8,128)(2,1)S(1)} %collective-permute-done.5.refs_14_), channel_id=1, source_target_pairs={{0,32},{16,496},{32,64},{48,16},{64,96},{80,48},{96,128},{112,80},... | collective-permute-start | bytes 835592 | tf_op jit(solution)/shard_map/ppermute | solution.py:227
  76.9 41.8 %copy-start.2 = (bf16[544,256]{1,0:T(8,128)(2,1)}, bf16[544,256]{1,0:T(8,128)(2,1)S(1)}, u32[]{:S(2)}) copy-start(bf16[544,256]{1,0:T(8,128)(2,1)S(1)} %collective-permute-done.12.refs_5_) | copy-start | bytes 835588
  77.0 18.3 %collective-permute-start.13 = (bf16[544,256]{1,0:T(8,128)(2,1)S(1)}, bf16[544,256]{1,0:T(8,128)(2,1)}, u32[]{:S(2)}, u32[]{:S(2)}) collective-permute-start(bf16[544,256]{1,0:T(8,128)(2,1)S(1)} %collective-permute-done.12.refs_5_), channel_id=1, source_target_pairs={{32,0},{496,16},{64,32},{16,48},{96,64},{48,80},{128,96},{80,112},... | collective-permute-start | bytes 835592 | tf_op jit(solution)/shard_map/ppermute | solution.py:231
  78.9 18.3 %collective-permute-start.7 = (bf16[544,256]{1,0:T(8,128)(2,1)}, bf16[544,256]{1,0:T(8,128)(2,1)S(1)}, u32[]{:S(2)}, u32[]{:S(2)}) collective-permute-start(bf16[544,256]{1,0:T(8,128)(2,1)} %collective-permute-done.6.refs_6_), channel_id=1, source_target_pairs={{0,32},{16,496},{32,64},{48,16},{64,96},{80,48},{96,128},{112,80},... | collective-permute-start | bytes 835592 | tf_op jit(solution)/shard_map/ppermute | solution.py:227
  83.8 24.5 %collective-permute-start = (f32[16,2,160]{2,1,0:T(2,128)S(1)}, f32[16,2,160]{2,1,0:T(2,128)S(1)}, u32[]{:S(2)}, u32[]{:S(2)}) collective-permute-start(f32[16,2,160]{2,1,0:T(2,128)S(1)} %copy-done.18), channel_id=1, source_target_pairs={{0,16},{16,0},{32,48},{48,32},{64,80},{80,64},{96,112},{112,96},{1... | collective-permute-start | bytes 61448 | tf_op jit(solution)/shard_map/ppermute | solution.py:221
  95.3 30.5 %collective-permute-start.14 = (bf16[544,256]{1,0:T(8,128)(2,1)}, bf16[544,256]{1,0:T(8,128)(2,1)}, u32[]{:S(2)}, u32[]{:S(2)}) collective-permute-start(bf16[544,256]{1,0:T(8,128)(2,1)} %collective-permute-done.13.refs_7_), channel_id=1, source_target_pairs={{32,0},{496,16},{64,32},{16,48},{96,64},{48,80},{128,96},{80,112},... | collective-permute-start | bytes 835592 | tf_op jit(solution)/shard_map/ppermute | solution.py:231
  97.2 28.6 %copy-start.3 = (bf16[544,256]{1,0:T(8,128)(2,1)}, bf16[544,256]{1,0:T(8,128)(2,1)S(1)}, u32[]{:S(2)}) copy-start(bf16[544,256]{1,0:T(8,128)(2,1)S(1)} %collective-permute-done.7.refs_5_) | copy-start | bytes 835588
  97.2 28.6 %collective-permute-start.15 = (bf16[544,256]{1,0:T(8,128)(2,1)S(1)}, bf16[544,256]{1,0:T(8,128)(2,1)}, u32[]{:S(2)}, u32[]{:S(2)}) collective-permute-start(bf16[544,256]{1,0:T(8,128)(2,1)S(1)} %collective-permute-done.7.refs_5_), channel_id=1, source_target_pairs={{0,32},{16,496},{32,64},{48,16},{64,96},{80,48},{96,128},{112,80},... | collective-permute-start | bytes 835592 | tf_op jit(solution)/shard_map/ppermute | solution.py:227
  125.8 23.4 %copy-start.19 = (f32[1,64]{1,0:T(1,128)S(1)}, f32[1,64]{1,0:T(1,128)}, u32[]{:S(2)}) copy-start(f32[1,64]{1,0:T(1,128)} %param.17) | copy-start | bytes 772
  132.5 48.1 %copy-start.6 = (f32[32,64]{1,0:T(8,128)S(1)}, f32[32,64]{1,0:T(8,128)}, u32[]{:S(2)}) copy-start(f32[32,64]{1,0:T(8,128)} %param.12) | copy-start | bytes 24580
  132.5 4.7 %collective-permute-start.16 = (bf16[1840,256]{1,0:T(8,128)(2,1)}, bf16[1840,256]{1,0:T(8,128)(2,1)S(1)}, u32[]{:S(2)}, u32[]{:S(2)}) collective-permute-start(bf16[1840,256]{1,0:T(8,128)(2,1)} %get-tuple-element.24), channel_id=1, source_target_pairs={{0,16},{16,0},{32,48},{48,32},{64,80},{80,64},{96,112},{112,96},{1... | collective-permute-start | bytes 2826248 | tf_op jit(solution)/shard_map/ppermute | solution.py:258
  142.5 13.2 %all-to-all-start.1 = ((bf16[16,16,128]{2,1,0:T(8,128)(2,1)}), bf16[16,16,128]{2,1,0:T(8,128)(2,1)S(1)}, u32[]{:S(2)}, u32[]{:S(2)}) async-start(bf16[16,16,128]{2,1,0:T(8,128)(2,1)} %shard_map.128), calls=%async_computation.1 | async-start | bytes 131072 | tf_op jit(solution)/shard_map/all_to_all | solution.py:264
  159.7 20.8 %all-to-all-start.2 = ((f32[16,16,128]{2,1,0:T(8,128)}), f32[16,16,128]{2,1,0:T(8,128)S(1)}, u32[]{:S(2)}, u32[]{:S(2)}) async-start(f32[16,16,128]{2,1,0:T(8,128)} %broadcast_in_dim.34), calls=%async_computation.2 | async-start | bytes 262144 | tf_op jit(solution)/shard_map/all_to_all | solution.py:280
  (8 other events, 67.2 us)

commit v2 on v1

v2 whole, which is shorter than its diff:
```python
import functools
import math

import jax
import jax.numpy as jnp
from jax import lax
from jax.experimental import pallas as pl
from jax.experimental.pallas import tpu as pltpu
from jax.sharding import PartitionSpec as P

HEAD = 128
NT = 1000
F32 = jnp.float32
BF16 = jnp.bfloat16
KEPT = 14.0


def sigma_of(level_ids):
    fraction = (level_ids.astype(F32) + 1.0) / NT
    return 5.0 * fraction / (1.0 + 4.0 * fraction)


def dot_nt(a, b):
    return lax.dot_general(a, b, (((1,), (1,)), ((), ())), preferred_element_type=F32)


def dot_nn(a, b):
    return lax.dot_general(a, b, (((1,), (0,)), ((), ())), preferred_element_type=F32)


def split_two(value):
    high = value.astype(BF16)
    return high, (value - high.astype(F32)).astype(BF16)


def kernel_call(body, out_shape, n_in, n_smem=0, flops=0, moved=0, limit=24):
    one = pl.BlockSpec(memory_space=pltpu.VMEM)
    scalar = pl.BlockSpec(memory_space=pltpu.SMEM)
    many = isinstance(out_shape, (tuple, list))
    return pl.pallas_call(
        body,
        out_shape=out_shape,
        in_specs=[scalar] * n_smem + [one] * n_in,
        out_specs=[one] * len(out_shape) if many else one,
        compiler_params=pltpu.CompilerParams(vmem_limit_bytes=limit * 1024 * 1024),
        cost_estimate=pl.CostEstimate(flops=flops, bytes_accessed=moved, transcendentals=0),
    )


def pack_weights(qkv_ref, out_ref, head_ref, chunk_ref, share_ref):
    count, rows, cols = qkv_ref.shape
    row = lax.broadcasted_iota(jnp.int32, (16, cols), 0)
    meta = jnp.zeros((16, cols), F32)
    for i in range(count):
        weight = qkv_ref[i].astype(F32)
        peak = jnp.maximum(jnp.max(jnp.abs(weight), axis=0, keepdims=True), 1e-30)
        power = jnp.floor(-jnp.log2(peak))
        whole = jnp.round(weight * jnp.exp2(power + KEPT))
        chunk_ref[i * rows : (i + 1) * rows, :] = whole.astype(jnp.int32).astype(jnp.int16)
        meta = jnp.where(row == i, power, meta)
    chunk_ref[count * rows :, :] = meta.astype(jnp.int32).astype(jnp.int16)
    share_ref[...] = dot_nt(head_ref[...], out_ref[...]).astype(BF16)


def pack_context(rows, core_ref, states_ref, embed_ref, context_ref, mods_ref, payload_ref, embed_out, mine_ref, other_ref):
    peers, tokens, _ = payload_ref.shape
    channels, width = embed_ref.shape
    half = embed_out.shape[1]
    chips = half // rows
    second = core_ref[0] == 1
    latent = states_ref[...].astype(BF16)
    context = context_ref[...].astype(F32)

    def halves(value):
        moved = pltpu.roll(value, width - rows, 1)
        return jnp.where(second, moved, value), jnp.where(second, value, moved)

    def blocks(value, put):
        for j in range(chips):
            put(slice(j * rows, (j + 1) * rows), value[:, 2 * j * rows : (2 * j + 1) * rows])

    def put_context(at, value):
        payload_ref[0, :, at] = value.astype(BF16)

    def put_embed(at, value):
        embed_out[:, at] = value.astype(BF16)

    def put_mine(at, value):
        mine_ref[:, at] = value

    def put_other(at, value):
        other_ref[:, at] = value

    blocks(halves(context)[0], put_context)
    hidden = dot_nn(latent, embed_ref[...]) + context
    scale = lax.rsqrt(jnp.mean(hidden * hidden, axis=-1, keepdims=True) + 1e-06)
    high, low = split_two(scale)
    lane = lax.broadcasted_iota(jnp.int32, (tokens, 128), 1)
    tail = jnp.concatenate([latent.astype(F32), jnp.zeros((tokens, 128 - channels), F32)], axis=1)
    tail = jnp.where(lane == channels, high.astype(F32), tail)
    tail = jnp.where(lane == channels + 1, low.astype(F32), tail)
    payload_ref[0, :, half:] = tail.astype(BF16)
    for p in range(1, peers):
        payload_ref[p] = payload_ref[0]
    blocks(halves(embed_ref[...].astype(F32))[0], put_embed)
    mine, other = halves(mods_ref[...])
    blocks(mine, put_mine)
    blocks(other, put_other)


def project(rows, context_ref, embed_ref, mine_ref, other_ref, chunk_ref, own_ref, send_ref, sums_ref):
    at = pl.program_id(0)
    group = chunk_ref.shape[0]
    count, double, _ = sums_ref.shape
    half = double // 2
    context = context_ref[...].astype(F32)
    embed = embed_ref[...].astype(F32)
    row = lax.broadcasted_iota(jnp.int32, (16, group * rows), 0)
    parts = []
    for mods_ref in (mine_ref, other_ref):
        gain = 1.0 + mods_ref[1:2, :]
        parts.append((context * gain).astype(BF16))
        parts.append((embed * gain).astype(BF16))
        parts.append(jnp.where(row == 0, mods_ref[0:1, :], 0.0).astype(BF16))
    left = jnp.concatenate(parts, axis=0)
    metas = [chunk_ref[n, count * rows :, :].astype(F32) for n in range(group)]
    for i in range(count):
        pieces = []
        for n in range(group):
            back = jnp.exp2(-(metas[n][i : i + 1] + KEPT))
            pieces.append((chunk_ref[n, i * rows : (i + 1) * rows, :].astype(F32) * back).astype(BF16))
        term = dot_nn(left, jnp.concatenate(pieces, axis=0))

        @pl.when(at == 0)
        def _(i=i, term=term):
            sums_ref[i] = term

        @pl.when(at > 0)
        def _(i=i, term=term):
            sums_ref[i] += term

    @pl.when(at == pl.num_programs(0) - 1)
    def _():
        for i in range(count):
            own_ref[i * half : (i + 1) * half, :] = sums_ref[i, :half]
            send_ref[i * half : (i + 1) * half, :] = sums_ref[i, half:].astype(BF16)


def attend(own_ref, got_ref, full_ref, shares_ref, out_ref):
    peers, pair_rows, lanes = out_ref.shape
    channels = lanes // 2
    tokens = full_ref.shape[0]
    tail_ref = full_ref
    half = tokens + channels + 16
    latent = tail_ref[:, :channels]
    scale = tail_ref[:, channels : channels + 1].astype(F32) + tail_ref[:, channels + 1 : channels + 2].astype(F32)
    made = []
    for i in range(3):
        at = i * half
        body = own_ref[at : at + tokens, :] + got_ref[at : at + tokens, :].astype(F32)
        at += tokens
        embed = own_ref[at : at + channels, :] + got_ref[at : at + channels, :].astype(F32)
        at += channels
        shift = own_ref[at : at + 16, :] + got_ref[at : at + 16, :].astype(F32)
        high, low = split_two(embed)
        body = body + dot_nn(latent, high) + dot_nn(latent, low)
        made.append((body * scale + shift[0:1]).astype(BF16))
    queries, keys, values = made
    outs = []
    for h in range(queries.shape[1] // HEAD):
        cols = slice(h * HEAD, (h + 1) * HEAD)
        scores = dot_nt(queries[:, cols], keys[:, cols]) * (1.0 / math.sqrt(HEAD))
        weights = jnp.exp(scores - jnp.max(scores, axis=-1, keepdims=True))
        total = jnp.sum(weights, axis=-1, keepdims=True)
        outs.append((dot_nn(weights.astype(BF16), values[:, cols]) / total).astype(BF16))
    attended = jnp.concatenate(outs, axis=1)
    heads = jnp.sum(shares_ref[...].astype(F32), axis=0)
    high, low = split_two(heads)
    result = dot_nt(attended, high) + dot_nt(attended, low)
    for p in range(peers):
        at = 2 * p * pair_rows
        block = jnp.concatenate([result[at : at + pair_rows], result[at + pair_rows : at + 2 * pair_rows]], axis=1)
        out_ref[p] = block.astype(BF16)


def per_device(
    states, initial, noise_draws, timesteps, context, modulation, out_gate, embed_weight, qkv_weight, out_weight, head_weight
):
    steps, peers = lax.axis_size("tm"), lax.axis_size("seq")
    chips = steps // 2
    mine = lax.axis_index("tm")
    z, core = mine // 2, mine % 2
    tokens_here, channels = initial.shape
    width = context.shape[1]
    rows = qkv_weight.shape[1]
    cols = qkv_weight.shape[2]
    tokens = tokens_here * peers
    half = tokens + channels + 16
    shape = jax.ShapeDtypeStruct

    flip = [(i, i ^ 1) for i in range(steps)]
    same_core = [list(range(0, steps, 2)), list(range(1, steps, 2))]
    reach = chips * rows

    payload, embed_half, mods_mine, mods_other = kernel_call(
        functools.partial(pack_context, rows),
        (
            shape((peers, tokens_here, reach + 128), BF16),
            shape((channels, reach), BF16),
            shape((2, reach), F32),
            shape((2, reach), F32),
        ),
        4,
        1,
        flops=2 * tokens_here * channels * width,
        moved=5000000,
    )(core[None], states[0], embed_weight, context, modulation[0])
    gathered = lax.all_to_all(payload, "seq", 0, 0).reshape(tokens, reach + 128)
    mods_sibling = lax.ppermute(mods_other, "tm", flip)

    chunk, share = kernel_call(
        pack_weights,
        (shape((3 * rows + 16, cols), jnp.int16), shape((channels, cols), BF16)),
        3,
        flops=2 * channels * rows * cols,
        moved=700000,
    )(qkv_weight, out_weight, head_weight)
    head_shares = lax.all_gather(share, "tm")
    chunks = lax.all_gather(chunk, "tm", axis_index_groups=same_core)

    group = min(4, chips)
    span = group * rows
    own, send = pl.pallas_call(
        functools.partial(project, rows),
        grid=(chips // group,),
        out_shape=(shape((3 * half, cols), F32), shape((3 * half, cols), BF16)),
        in_specs=[
            pl.BlockSpec((tokens, span), lambda k: (0, k)),
            pl.BlockSpec((channels, span), lambda k: (0, k)),
            pl.BlockSpec((2, span), lambda k: (0, k)),
            pl.BlockSpec((2, span), lambda k: (0, k)),
            pl.BlockSpec((group, 3 * rows + 16, cols), lambda k: (k, 0, 0)),
        ],
        out_specs=[pl.BlockSpec((3 * half, cols), lambda k: (0, 0))] * 2,
        scratch_shapes=[pltpu.VMEM((3, 2 * half, cols), F32)],
        compiler_params=pltpu.CompilerParams(vmem_limit_bytes=36 * 1024 * 1024),
        cost_estimate=pl.CostEstimate(flops=8000000000, bytes_accessed=10000000, transcendentals=0),
    )(gathered, embed_half, mods_mine, mods_sibling, chunks)
    got = lax.ppermute(send, "tm", flip)

    pair_rows = tokens_here // 2
    whole = lambda *dims: pl.BlockSpec(dims, lambda k: (0,) * len(dims))
    shares = pl.pallas_call(
        attend,
        grid=(1,),
        out_shape=shape((peers, pair_rows, 2 * channels), BF16),
        in_specs=[
            whole(3 * half, cols),
            whole(3 * half, cols),
            pl.BlockSpec((tokens, 128), lambda k: (0, reach // 128)),
            whole(steps, channels, cols),
        ],
        out_specs=whole(peers, pair_rows, 2 * channels),
        compiler_params=pltpu.CompilerParams(vmem_limit_bytes=32 * 1024 * 1024),
        cost_estimate=pl.CostEstimate(flops=600000000, bytes_accessed=4000000, transcendentals=0),
    )(own, got, gathered, head_shares)
    shares = lax.all_to_all(shares, "seq", 0, 0)
    mixed = jnp.sum(shares.astype(F32), axis=0)

    def pairs(value):
        return jnp.concatenate([value[:pair_rows], value[pair_rows:]], axis=1)

    def unpairs(value):
        return jnp.concatenate([value[:, :channels], value[:, channels:]], axis=0)

    gate = jnp.concatenate([out_gate, out_gate], axis=1)
    velocity_f = (1.0 + gate) * mixed
    step_size = sigma_of(timesteps[0, 1]) - sigma_of(timesteps[0, 0])
    drift = step_size * velocity_f + jnp.sqrt(-step_size) * pairs(noise_draws[0])
    both = lax.all_gather(drift, "tm", axis_index_groups=[[2 * i, 2 * i + 1] for i in range(chips)])
    spread = jnp.broadcast_to((both[0] + both[1])[None], (chips, pair_rows, 2 * channels))
    everyone = lax.all_to_all(spread, "tm", 0, 0, axis_index_groups=same_core)
    earlier = lax.broadcasted_iota(jnp.int32, (chips, 1, 1), 0) < z
    before = jnp.sum(jnp.where(earlier, everyone, 0.0), axis=0) + jnp.where(core == 1, both[0], 0.0)
    new_states = initial + unpairs(before)
    return (new_states[None], unpairs(velocity_f).astype(BF16)[None])


def solution(mesh):
    in_specs = (
        P("tm", "seq", None),
        P("seq", None),
        P("tm", "seq", None),
        P("tm", None),
        P("seq", None),
        P("tm", None, None),
        P("tm", None),
        P(),
        P(None, "tm", "seq"),
        P("seq", "tm"),
        P(None, "tm"),
    )
    out_specs = (P("tm", "seq", None), P("tm", "seq", None))
    return jax.shard_map(per_device, mesh=mesh, in_specs=in_specs, out_specs=out_specs, check_vma=False)
```

time: 183 us -> 170 us (0.929)
  blocking collectives: 3.2 us -> 66.7 us
  starting transfers between devices: 94.4 us -> 32 us
  Pallas kernels: 37.9 us -> 19.8 us
  waiting for transfers between devices: 34.3 us -> 18.2 us
  between operations: 2.54 us -> 15.6 us
  local copies, waits for them, and re-layouts: 6.09 us -> 14.5 us
    all_gather x0 -> x1, blocking collectives: none -> 63.4 us  [per_device(): chunks = lax.all_gather(chunk, 'tm', axis_index_groups=same_core)]
    ppermute x15 -> x0, starting transfers between devices: 59.7 us -> none  [the longest x8 46.3 us: per_device(): ahead = lax.ppermute(ahead, 'tm', forth)]
    pallas_call x7 -> x4, Pallas kernels: 37.9 us -> 19.8 us  [the longest x1 14.3 us: per_device(): pl.pallas_call(functools.partial(project, rows), grid=(chips // group,),...]
    ppermute x15 -> x0, waiting for transfers between devices: 16 us -> none  [the longest x7 12 us: per_device(): behind = lax.ppermute(behind, 'tm', back)]
    unnamed x41 -> x37, local copies, waits for them, and re-layouts: 3.95 us -> 13.1 us
    ppermute x1, starting transfers between devices: 9.32 us -> 4.93 us  [per_device(): mods_sibling = lax.ppermute(mods_other, 'tm', flip)]
    all_to_all x1, starting transfers between devices: 8.62 us -> 5.55 us  [per_device(): everyone = lax.all_to_all(spread, 'tm', 0, 0, axis_index_groups=same_core)]
    ppermute x1, starting transfers between devices: 2.32 us -> 5.19 us  [per_device(): got = lax.ppermute(send, 'tm', flip)]
  transfers between devices with their start and end apart: 20 -> 6, of which waited for: 10 -> 3; matrix products, arithmetic and copies ran while one was open for 2% -> 1% of each run, Pallas kernels for 13% -> 9%
where the time goes in v2:
time: 170 us; the launch traced here: 168 us
  blocking collectives  66.7 us (39%)
  starting transfers between devices  32 us (19%)
  Pallas kernels  19.8 us (12%)
  waiting for transfers between devices  18.2 us (11%)
  between operations  15.6 us (9%)
  local copies, waits for them, and re-layouts  14.5 us (9%)
    all_gather x1, blocking collectives, per_device(): chunks = lax.all_gather(chunk, 'tm', axis_index_groups=same_core)  63.4 us
    pallas_call x1, Pallas kernels, per_device(): pl.pallas_call(functools.partial(project, rows), grid=(chips // group,),...  14.3 us
    unnamed x37, local copies, waits for them, and re-layouts  13.1 us
    all_to_all x1, waiting for transfers between devices, per_device(): everyone = lax.all_to_all(spread, 'tm', 0, 0, axis_index_groups=same_core)  11.5 us
    all_to_all x1, starting transfers between devices, per_device(): shares = lax.all_to_all(shares, 'seq', 0, 0)  8.56 us
    all_to_all x1, starting transfers between devices, per_device(): gathered = lax.all_to_all(payload, 'seq', 0, 0).reshape(tokens, reach + 128)  7.71 us
    all_to_all x1, waiting for transfers between devices, per_device(): shares = lax.all_to_all(shares, 'seq', 0, 0)  6.5 us
    all_to_all x1, starting transfers between devices, per_device(): everyone = lax.all_to_all(spread, 'tm', 0, 0, axis_index_groups=same_core)  5.55 us
  transfers between devices with their start and end apart: 6, of which 3 were waited for; matrix products, arithmetic and copies ran while one was open for 1% of the time, Pallas kernels for 9%

profile of v2, /device:TPU:1, one launch (start us, length us, event | category | flops | bytes accessed | tf_op | source)
XLA Modules:
  0.0 168.3 jit_solution(4169740731442761904)
XLA Ops:
  7.2 1.1 copy-done.5
  8.3 1.0 copy-done.6
  9.2 0.8 copy-done.8
  10.0 0.7 copy-done.10
  10.7 0.9 shard_map.122
  11.7 1.6 copy-done.1
  13.2 0.8 copy-done.11
  14.0 7.7 %all-to-all-start = ((bf16[16,32,2688]{2,1,0:T(8,128)(2,1)}), bf16[16,32,2688]{2,1,0:T(8,128)(2,1)S(1)}, u32[]{:S(2)}, u32[]{:S(2)}) async-start(bf16[16,32,2688]{2,1,0:T(8,128)(2,1)} %copy-done.1), calls=%async_computation | async-start | bytes 5505024 | tf_op jit(solution)/shard_map/all_to_all | solution.py:218
  21.8 4.9 %collective-permute-start = (f32[2,2560]{1,0:T(2,128)S(1)}, f32[2,2560]{1,0:T(2,128)S(1)}, u32[]{:S(2)}, u32[]{:S(2)}) collective-permute-start(f32[2,2560]{1,0:T(2,128)S(1)} %get-tuple-element.13), channel_id=1, source_target_pairs={{0,16},{16,0},{32,48},{48,32},{64,80},{80,64},{96,112},{112,96},{1... | collective-permute-start | bytes 61448 | tf_op jit(solution)/shard_map/ppermute | solution.py:219
  26.7 0.1 copy.15.out_ref
  26.8 0.8 shard_map.123
  27.7 63.4 %all-gather.6 = s16[7936,256]{1,0:T(8,128)(2,1)} all-gather(s16[496,256]{1,0:T(8,128)(2,1)S(1)} %get-tuple-element.14), channel_id=2, replica_groups={{0,32,64,96,128,160,192,224,256,288,320,352,384,416,448,480},{16,48,80,..., dimensions={0}, use_global_device_ids=true | all-gather | bytes 4317184 | tf_op jit(solution)/shard_map/all_gather | solution.py:229
  91.1 2.2 %copy-done = s16[7936,256]{1,0:T(8,128)(2,1)S(1)} copy-done((s16[7936,256]{1,0:T(8,128)(2,1)S(1)}, s16[7936,256]{1,0:T(8,128)(2,1)}, u32[]{:S(2)}) %copy-start) | copy-done | bytes 4063256
  93.2 1.0 copy-done.12
  94.2 14.3 %shard_map.124 = (f32[1776,256]{1,0:T(8,128)S(1)}, bf16[1776,256]{1,0:T(8,128)(2,1)}) custom-call(bf16[512,2688]{1,0:T(8,128)(2,1)S(1)} %bitcast.24, bf16[64,2560]{1,0:T(8,128)(2,1)S(1)} %copy-done.12, f32[2,2560]{1,0:T(2,128)S(1)} %get-tuple-element.12.mine_ref, f32[2,2560]{1,0:T(2,128)S(1)} %collective-permute-done.other_ref, s16[16,496,256]{2,1,0:T(8,128)(2,1)S(1)} %bitcast.26), custom_call_target="tpu_custom_call" | custom-call | flops 8000000000 | bytes 10000000 | tf_op jit(solution)/shard_map/pallas_call | solution.py:233
  108.5 1.2 copy-done.2
  109.7 5.2 %collective-permute-start.1 = (bf16[1776,256]{1,0:T(8,128)(2,1)}, bf16[1776,256]{1,0:T(8,128)(2,1)}, u32[]{:S(2)}, u32[]{:S(2)}) collective-permute-start(bf16[1776,256]{1,0:T(8,128)(2,1)} %get-tuple-element.16), channel_id=1, source_target_pairs={{0,16},{16,0},{32,48},{48,32},{64,80},{80,64},{96,112},{112,96},{1... | collective-permute-start | bytes 2727944 | tf_op jit(solution)/shard_map/ppermute | solution.py:249
  115.0 0.6 fusion.6
  117.1 0.2 collective-permute-done.1.got_ref
  117.4 1.5 copy-done.3
  118.8 1.2 copy-done.4
  120.1 3.7 %shard_map.125 = bf16[16,16,128]{2,1,0:T(8,128)(2,1)} custom-call(f32[1776,256]{1,0:T(8,128)S(1)} %copy-done.3, bf16[1776,256]{1,0:T(8,128)(2,1)} %collective-permute-done.1.got_ref, bf16[512,2688]{1,0:T(8,128)(2,1)S(1)} %bitcast.25, bf16[32,64,256]{2,1,0:T(8,128)(2,1)S(1)} %bitcast.27), custom_call_target="tpu_custom_call" | custom-call | flops 600000000 | bytes 4000000 | tf_op jit(solution)/shard_map/pallas_call | solution.py:253
  123.8 8.6 %all-to-all-start.1 = ((bf16[16,16,128]{2,1,0:T(8,128)(2,1)}), bf16[16,16,128]{2,1,0:T(8,128)(2,1)S(1)}, u32[]{:S(2)}, u32[]{:S(2)}) async-start(bf16[16,16,128]{2,1,0:T(8,128)(2,1)} %shard_map.125), calls=%async_computation.1 | async-start | bytes 131072 | tf_op jit(solution)/shard_map/all_to_all | solution.py:267
  132.4 6.5 %all-to-all-done.1 = bf16[16,16,128]{2,1,0:T(8,128)(2,1)S(1)} async-done(((bf16[16,16,128]{2,1,0:T(8,128)(2,1)}), bf16[16,16,128]{2,1,0:T(8,128)(2,1)S(1)}, u32[]{:S(2)}, u32[]{:S(2)}) %all-to-all-start.1) | async-done | bytes 65568 | tf_op jit(solution)/shard_map/all_to_all | solution.py:267
  138.9 0.1 fusion.2
  139.0 3.3 %all_gather.20 = f32[2,16,128]{2,1,0:T(8,128)S(1)} all-gather(f32[1,16,128]{2,1,0:T(8,128)S(1)} %fusion.2), channel_id=1, replica_groups={{0,16},{32,48},{64,80},{96,112},{128,144},{160,176},{192,208},{224,240}..., dimensions={0}, use_global_device_ids=true | all-gather | bytes 24576 | tf_op jit(solution)/shard_map/all_gather | solution.py:280
  142.3 0.7 broadcast_in_dim.34
  143.0 5.6 %all-to-all-start.2 = ((f32[16,16,128]{2,1,0:T(8,128)}), f32[16,16,128]{2,1,0:T(8,128)S(1)}, u32[]{:S(2)}, u32[]{:S(2)}) async-start(f32[16,16,128]{2,1,0:T(8,128)} %broadcast_in_dim.34), calls=%async_computation.2 | async-start | bytes 262144 | tf_op jit(solution)/shard_map/all_to_all | solution.py:282
  148.6 0.6 pad_maximum_fusion
  149.2 11.5 %all-to-all-done.2 = f32[16,16,128]{2,1,0:T(8,128)S(1)} async-done(((f32[16,16,128]{2,1,0:T(8,128)}), f32[16,16,128]{2,1,0:T(8,128)S(1)}, u32[]{:S(2)}, u32[]{:S(2)}) %all-to-all-start.2) | async-done | bytes 131104 | tf_op jit(solution)/shard_map/all_to_all | solution.py:282
  160.7 0.1 select_reduce_fusion
  160.8 0.6 fusion
  (39 shorter events, 0.4 us)
Async XLA Ops:
  7.2 1.1 copy-start.5
  8.3 1.0 copy-start.6
  9.2 0.8 copy-start.8
  10.0 0.7 copy-start.10
  11.7 1.6 copy-start.1
  13.2 0.8 copy-start.11
  14.0 12.7 %copy-start.13 = (bf16[256,160]{0,1:T(8,128)(2,1)S(1)}, bf16[256,160]{0,1:T(8,128)(2,1)}, u32[]{:S(2)}) copy-start(bf16[256,160]{0,1:T(8,128)(2,1)} %param.20) | copy-start | bytes 245764
  14.0 12.8 %copy-start.7 = (bf16[3,160,256]{2,1,0:T(8,128)(2,1)S(1)}, bf16[3,160,256]{2,1,0:T(8,128)(2,1)}, u32[]{:S(2)}) copy-start(bf16[3,160,256]{2,1,0:T(8,128)(2,1)} %qkv_ref.1) | copy-start | bytes 737284
  14.0 12.8 %copy-start.9 = (bf16[64,160]{1,0:T(8,128)(2,1)S(1)}, bf16[64,160]{1,0:T(8,128)(2,1)}, u32[]{:S(2)}) copy-start(bf16[64,160]{1,0:T(8,128)(2,1)} %head_ref.1) | copy-start | bytes 61444
  14.0 77.1 %all-to-all-start = ((bf16[16,32,2688]{2,1,0:T(8,128)(2,1)}), bf16[16,32,2688]{2,1,0:T(8,128)(2,1)S(1)}, u32[]{:S(2)}, u32[]{:S(2)}) async-start(bf16[16,32,2688]{2,1,0:T(8,128)(2,1)} %copy-done.1), calls=%async_computation | async-start | bytes 5505024 | tf_op jit(solution)/shard_map/all_to_all | solution.py:218
  21.7 95.4 %all-gather.5.cloned.1.call-start = ((), (), s32[]{:S(2)}) async-start(), calls=%async_computation.3 | async-start | bytes 1081344 | tf_op jit(solution)/shard_map/all_gather | solution.py:228
  21.8 69.3 %collective-permute-start = (f32[2,2560]{1,0:T(2,128)S(1)}, f32[2,2560]{1,0:T(2,128)S(1)}, u32[]{:S(2)}, u32[]{:S(2)}) collective-permute-start(f32[2,2560]{1,0:T(2,128)S(1)} %get-tuple-element.13), channel_id=1, source_target_pairs={{0,16},{16,0},{32,48},{48,32},{64,80},{80,64},{96,112},{112,96},{1... | collective-permute-start | bytes 61448 | tf_op jit(solution)/shard_map/ppermute | solution.py:219
  91.1 2.2 %copy-start = (s16[7936,256]{1,0:T(8,128)(2,1)S(1)}, s16[7936,256]{1,0:T(8,128)(2,1)}, u32[]{:S(2)}) copy-start(s16[7936,256]{1,0:T(8,128)(2,1)} %all-gather.6) | copy-start | bytes 12189700
  93.2 1.0 copy-start.12
  94.2 20.7 %copy-start.16 = (s32[1,2]{1,0:T(1,128)S(1)}, s32[1,2]{1,0:T(1,128)}, u32[]{:S(2)}) copy-start(s32[1,2]{1,0:T(1,128)} %param.14) | copy-start | bytes 28
  94.2 22.8 %copy-start.17 = (f32[1,64]{1,0:T(1,128)S(1)}, f32[1,64]{1,0:T(1,128)}, u32[]{:S(2)}) copy-start(f32[1,64]{1,0:T(1,128)} %param.17) | copy-start | bytes 772
  94.2 22.9 %copy-start.15 = (f32[1,32,64]{2,1,0:T(8,128)S(1)}, f32[1,32,64]{2,1,0:T(8,128)}, u32[]{:S(2)}) copy-start(f32[1,32,64]{2,1,0:T(8,128)} %param.13) | copy-start | bytes 24580
  108.5 1.2 copy-start.2
  109.7 7.6 %collective-permute-start.1 = (bf16[1776,256]{1,0:T(8,128)(2,1)}, bf16[1776,256]{1,0:T(8,128)(2,1)}, u32[]{:S(2)}, u32[]{:S(2)}) collective-permute-start(bf16[1776,256]{1,0:T(8,128)(2,1)} %get-tuple-element.16), channel_id=1, source_target_pairs={{0,16},{16,0},{32,48},{48,32},{64,80},{80,64},{96,112},{112,96},{1... | collective-permute-start | bytes 2727944 | tf_op jit(solution)/shard_map/ppermute | solution.py:249
  117.3 1.5 copy-start.3
  118.8 1.2 copy-start.4
  120.1 40.8 %copy-start.14 = (f32[32,64]{1,0:T(8,128)S(1)}, f32[32,64]{1,0:T(8,128)}, u32[]{:S(2)}) copy-start(f32[32,64]{1,0:T(8,128)} %param.12) | copy-start | bytes 24580
  123.8 15.1 %all-to-all-start.1 = ((bf16[16,16,128]{2,1,0:T(8,128)(2,1)}), bf16[16,16,128]{2,1,0:T(8,128)(2,1)S(1)}, u32[]{:S(2)}, u32[]{:S(2)}) async-start(bf16[16,16,128]{2,1,0:T(8,128)(2,1)} %shard_map.125), calls=%async_computation.1 | async-start | bytes 131072 | tf_op jit(solution)/shard_map/all_to_all | solution.py:267
  143.0 17.7 %all-to-all-start.2 = ((f32[16,16,128]{2,1,0:T(8,128)}), f32[16,16,128]{2,1,0:T(8,128)S(1)}, u32[]{:S(2)}, u32[]{:S(2)}) async-start(f32[16,16,128]{2,1,0:T(8,128)} %broadcast_in_dim.34), calls=%async_computation.2 | async-start | bytes 262144 | tf_op jit(solution)/shard_map/all_to_all | solution.py:282
Sparse Core Ops, SparseCore 0:
  27.8 73.9 all-gather.4

commit v3 on v2

--- a/solution.py
+++ b/solution.py
@@ -33,7 +33,7 @@
     return high, (value - high.astype(F32)).astype(BF16)
 
 
-def kernel_call(body, out_shape, n_in, n_smem=0, flops=0, moved=0, limit=24):
+def kernel_call(body, out_shape, n_in, n_smem=0, flops=0, moved=0, limit=56):
     one = pl.BlockSpec(memory_space=pltpu.VMEM)
     scalar = pl.BlockSpec(memory_space=pltpu.SMEM)
     many = isinstance(out_shape, (tuple, list))
@@ -47,22 +47,46 @@
     )
 
 
-def pack_weights(qkv_ref, out_ref, head_ref, chunk_ref, share_ref):
+def grid_call(body, steps, out_shape, in_specs, out_specs, scratch, flops):
+    return pl.pallas_call(
+        body,
+        grid=(steps,),
+        out_shape=out_shape,
+        in_specs=in_specs,
+        out_specs=out_specs,
+        scratch_shapes=scratch,
+        compiler_params=pltpu.CompilerParams(vmem_limit_bytes=56 * 1024 * 1024),
+        cost_estimate=pl.CostEstimate(flops=flops, bytes_accessed=5000000, transcendentals=0),
+    )
+
+
+def to_whole(weight):
+    peak = jnp.maximum(jnp.max(jnp.abs(weight), axis=0, keepdims=True), 1e-30)
+    power = jnp.floor(-jnp.log2(peak))
+    whole = jnp.round(weight * jnp.exp2(power + KEPT))
+    return whole.astype(jnp.int32).astype(jnp.int16), power
+
+
+def from_whole(whole, power):
+    return whole.astype(F32) * jnp.exp2(-(power + KEPT))
+
+
+def pack_weights(qkv_ref, out_ref, head_ref, chunk_ref):
     count, rows, cols = qkv_ref.shape
+    channels = head_ref.shape[0]
     row = lax.broadcasted_iota(jnp.int32, (16, cols), 0)
     meta = jnp.zeros((16, cols), F32)
     for i in range(count):
-        weight = qkv_ref[i].astype(F32)
-        peak = jnp.maximum(jnp.max(jnp.abs(weight), axis=0, keepdims=True), 1e-30)
-        power = jnp.floor(-jnp.log2(peak))
-        whole = jnp.round(weight * jnp.exp2(power + KEPT))
-        chunk_ref[i * rows : (i + 1) * rows, :] = whole.astype(jnp.int32).astype(jnp.int16)
+        chunk_ref[i * rows : (i + 1) * rows, :], power = to_whole(qkv_ref[i].astype(F32))
         meta = jnp.where(row == i, power, meta)
-    chunk_ref[count * rows :, :] = meta.astype(jnp.int32).astype(jnp.int16)
-    share_ref[...] = dot_nt(head_ref[...], out_ref[...]).astype(BF16)
-
-
-def pack_context(rows, core_ref, states_ref, embed_ref, context_ref, mods_ref, payload_ref, embed_out, mine_ref, other_ref):
+    at = count * rows
+    chunk_ref[at : at + channels, :], power = to_whole(dot_nn(head_ref[...], out_ref[...]))
+    meta = jnp.where(row == count, power, meta)
+    chunk_ref[at + channels :, :] = meta.astype(jnp.int32).astype(jnp.int16)
+
+
+def pack(rows, core_ref, states_ref, embed_ref, context_ref, mods_ref, *refs):
+    weight_refs, (payload_ref, embed_out, mine_ref, other_ref, chunk_ref) = refs[:3], refs[3:]
     peers, tokens, _ = payload_ref.shape
     channels, width = embed_ref.shape
     half = embed_out.shape[1]
@@ -106,47 +130,53 @@
     mine, other = halves(mods_ref[...])
     blocks(mine, put_mine)
     blocks(other, put_other)
-
-
-def project(rows, context_ref, embed_ref, mine_ref, other_ref, chunk_ref, own_ref, send_ref, sums_ref):
-    at = pl.program_id(0)
-    group = chunk_ref.shape[0]
-    count, double, _ = sums_ref.shape
-    half = double // 2
-    context = context_ref[...].astype(F32)
-    embed = embed_ref[...].astype(F32)
-    row = lax.broadcasted_iota(jnp.int32, (16, group * rows), 0)
-    parts = []
-    for mods_ref in (mine_ref, other_ref):
-        gain = 1.0 + mods_ref[1:2, :]
-        parts.append((context * gain).astype(BF16))
-        parts.append((embed * gain).astype(BF16))
-        parts.append(jnp.where(row == 0, mods_ref[0:1, :], 0.0).astype(BF16))
-    left = jnp.concatenate(parts, axis=0)
-    metas = [chunk_ref[n, count * rows :, :].astype(F32) for n in range(group)]
-    for i in range(count):
-        pieces = []
-        for n in range(group):
-            back = jnp.exp2(-(metas[n][i : i + 1] + KEPT))
-            pieces.append((chunk_ref[n, i * rows : (i + 1) * rows, :].astype(F32) * back).astype(BF16))
-        term = dot_nn(left, jnp.concatenate(pieces, axis=0))
-
-        @pl.when(at == 0)
-        def _(i=i, term=term):
-            sums_ref[i] = term
-
-        @pl.when(at > 0)
-        def _(i=i, term=term):
-            sums_ref[i] += term
-
-    @pl.when(at == pl.num_programs(0) - 1)
+    pack_weights(*weight_refs, chunk_ref)
+
+
+def scale_rows(left_ref, context_ref, embed_ref, mods_ref):
+    tokens, channels = context_ref.shape[0], embed_ref.shape[0]
+    gain = 1.0 + mods_ref[1:2, :]
+    left_ref[:tokens, :] = (context_ref[...].astype(F32) * gain).astype(BF16)
+    left_ref[tokens : tokens + channels, :] = (embed_ref[...].astype(F32) * gain).astype(BF16)
+    row = lax.broadcasted_iota(jnp.int32, (16, gain.shape[1]), 0)
+    left_ref[tokens + channels :, :] = jnp.where(row == 0, mods_ref[0:1, :], 0.0).astype(BF16)
+
+
+def project_sibling(context_ref, embed_ref, mods_ref, chunk_ref, extra_ref, send_ref, weight_ref, heads_ref, left_ref):
+    i = pl.program_id(0)
+    chips, rows, _ = chunk_ref.shape
+    channels = heads_ref.shape[0]
+    half = left_ref.shape[0]
+
+    @pl.when(i == 0)
     def _():
-        for i in range(count):
-            own_ref[i * half : (i + 1) * half, :] = sums_ref[i, :half]
-            send_ref[i * half : (i + 1) * half, :] = sums_ref[i, half:].astype(BF16)
-
-
-def attend(own_ref, got_ref, full_ref, shares_ref, out_ref):
+        scale_rows(left_ref, context_ref, embed_ref, mods_ref)
+        heads = None
+        for n in range(chips):
+            power = extra_ref[n, channels:, :].astype(F32)[3:4]
+            share = from_whole(extra_ref[n, :channels, :], power)
+            heads = share if heads is None else heads + share
+        heads_ref[...] = heads
+        send_ref[3 * half :, :] = heads.astype(BF16)
+
+    row = lax.broadcasted_iota(jnp.int32, (16, heads_ref.shape[1]), 0)
+    for n in range(chips):
+        meta = extra_ref[n, channels:, :].astype(F32)
+        power = jnp.sum(jnp.where(row == i, meta, 0.0), axis=0, keepdims=True)
+        weight_ref[0, n * rows : (n + 1) * rows, :] = from_whole(chunk_ref[n], power).astype(BF16)
+    result = dot_nn(left_ref[...], weight_ref[0])
+    send_ref[pl.ds(pl.multiple_of(i * half, 16), half), :] = result.astype(BF16)
+
+
+def project_own(context_ref, embed_ref, mods_ref, weight_ref, own_ref, left_ref):
+    @pl.when(pl.program_id(0) == 0)
+    def _():
+        scale_rows(left_ref, context_ref, embed_ref, mods_ref)
+
+    own_ref[...] = dot_nn(left_ref[...], weight_ref[0])
+
+
+def attend(own_ref, got_ref, full_ref, heads_ref, out_ref):
     peers, pair_rows, lanes = out_ref.shape
     channels = lanes // 2
     tokens = full_ref.shape[0]
@@ -174,7 +204,7 @@
         total = jnp.sum(weights, axis=-1, keepdims=True)
         outs.append((dot_nn(weights.astype(BF16), values[:, cols]) / total).astype(BF16))
     attended = jnp.concatenate(outs, axis=1)
-    heads = jnp.sum(shares_ref[...].astype(F32), axis=0)
+    heads = heads_ref[...] + got_ref[3 * half :, :].astype(F32)
     high, low = split_two(heads)
     result = dot_nt(attended, high) + dot_nt(attended, low)
     for p in range(peers):
@@ -202,68 +232,69 @@
     same_core = [list(range(0, steps, 2)), list(range(1, steps, 2))]
     reach = chips * rows
 
-    payload, embed_half, mods_mine, mods_other = kernel_call(
-        functools.partial(pack_context, rows),
+    payload, embed_half, mods_mine, mods_other, chunk = kernel_call(
+        functools.partial(pack, rows),
         (
             shape((peers, tokens_here, reach + 128), BF16),
             shape((channels, reach), BF16),
             shape((2, reach), F32),
             shape((2, reach), F32),
+            shape((3 * rows + channels + 16, cols), jnp.int16),
         ),
-        4,
+        7,
         1,
         flops=2 * tokens_here * channels * width,
         moved=5000000,
-    )(core[None], states[0], embed_weight, context, modulation[0])
+    )(core[None], states[0], embed_weight, context, modulation[0], qkv_weight, out_weight.T, head_weight)
     gathered = lax.all_to_all(payload, "seq", 0, 0).reshape(tokens, reach + 128)
     mods_sibling = lax.ppermute(mods_other, "tm", flip)
-
-    chunk, share = kernel_call(
-        pack_weights,
-        (shape((3 * rows + 16, cols), jnp.int16), shape((channels, cols), BF16)),
+    chunks = lax.all_gather(chunk, "tm", axis_index_groups=same_core)
+
+    def whole(*dims):
+        return pl.BlockSpec(dims, lambda i: (0,) * len(dims))
+
+    extra = channels + 16
+    common = [whole(tokens, reach), whole(channels, reach), whole(2, reach)]
+    left = [pltpu.VMEM((half, reach), BF16)]
+    send, weights, heads = grid_call(
+        project_sibling,
         3,
-        flops=2 * channels * rows * cols,
-        moved=700000,
-    )(qkv_weight, out_weight, head_weight)
-    head_shares = lax.all_gather(share, "tm")
-    chunks = lax.all_gather(chunk, "tm", axis_index_groups=same_core)
-
-    group = min(4, chips)
-    span = group * rows
-    own, send = pl.pallas_call(
-        functools.partial(project, rows),
-        grid=(chips // group,),
-        out_shape=(shape((3 * half, cols), F32), shape((3 * half, cols), BF16)),
-        in_specs=[
-            pl.BlockSpec((tokens, span), lambda k: (0, k)),
-            pl.BlockSpec((channels, span), lambda k: (0, k)),
-            pl.BlockSpec((2, span), lambda k: (0, k)),
-            pl.BlockSpec((2, span), lambda k: (0, k)),
-            pl.BlockSpec((group, 3 * rows + 16, cols), lambda k: (k, 0, 0)),
+        (shape((3 * half + channels, cols), BF16), shape((3, reach, cols), BF16), shape((channels, cols), F32)),
+        common
+        + [
+            pl.BlockSpec((chips, rows, cols), lambda i: (0, i, 0)),
+            pl.BlockSpec((chips, extra, cols), lambda i: (0, 3 * rows // extra, 0)),
         ],
-        out_specs=[pl.BlockSpec((3 * half, cols), lambda k: (0, 0))] * 2,
-        scratch_shapes=[pltpu.VMEM((3, 2 * half, cols), F32)],
-        compiler_params=pltpu.CompilerParams(vmem_limit_bytes=36 * 1024 * 1024),
-        cost_estimate=pl.CostEstimate(flops=8000000000, bytes_accessed=10000000, transcendentals=0),
-    )(gathered, embed_half, mods_mine, mods_sibling, chunks)
+        [whole(3 * half + channels, cols), pl.BlockSpec((1, reach, cols), lambda i: (i, 0, 0)), whole(channels, cols)],
+        left,
+        4000000000,
+    )(gathered, embed_half, mods_sibling, chunks, chunks)
     got = lax.ppermute(send, "tm", flip)
+    own = grid_call(
+        project_own,
+        3,
+        shape((3 * half, cols), F32),
+        common + [pl.BlockSpec((1, reach, cols), lambda i: (i, 0, 0))],
+        pl.BlockSpec((half, cols), lambda i: (i, 0)),
+        left,
+        4000000000,
+    )(gathered, embed_half, mods_mine, weights)
 
     pair_rows = tokens_here // 2
-    whole = lambda *dims: pl.BlockSpec(dims, lambda k: (0,) * len(dims))
-    shares = pl.pallas_call(
+    shares = grid_call(
         attend,
-        grid=(1,),
-        out_shape=shape((peers, pair_rows, 2 * channels), BF16),
-        in_specs=[
+        1,
+        shape((peers, pair_rows, 2 * channels), BF16),
+        [
             whole(3 * half, cols),
-            whole(3 * half, cols),
-            pl.BlockSpec((tokens, 128), lambda k: (0, reach // 128)),
-            whole(steps, channels, cols),
+            whole(3 * half + channels, cols),
+            pl.BlockSpec((tokens, 128), lambda i: (0, reach // 128)),
+            whole(channels, cols),
         ],
-        out_specs=whole(peers, pair_rows, 2 * channels),
-        compiler_params=pltpu.CompilerParams(vmem_limit_bytes=32 * 1024 * 1024),
-        cost_estimate=pl.CostEstimate(flops=600000000, bytes_accessed=4000000, transcendentals=0),
-    )(own, got, gathered, head_shares)
+        whole(peers, pair_rows, 2 * channels),
+        [],
+        600000000,
+    )(own, got, gathered, heads)
     shares = lax.all_to_all(shares, "seq", 0, 0)
     mixed = jnp.sum(shares.astype(F32), axis=0)
 

time: 170 us -> 150 us (0.88)
  between operations: 15.6 us -> 2.13 us
  local copies, waits for them, and re-layouts: 14.5 us -> 3.95 us
  Pallas kernels: 19.8 us -> 22.5 us
  starting transfers between devices: 32 us -> 34.3 us
    unnamed x37 -> x18, local copies, waits for them, and re-layouts: 13.1 us -> 2.58 us
    pallas_call x4, Pallas kernels: 19.8 us -> 22.5 us  [the longest x1 7.6 us: per_device(): grid_call(project_sibling, 3, (shape((3 * half + channels, cols), BF16),...]
    ppermute x1, starting transfers between devices: 5.19 us -> 7.48 us  [per_device(): got = lax.ppermute(send, 'tm', flip)]
  transfers between devices with their start and end apart: 6 -> 5, of which waited for: 3 -> 2; matrix products, arithmetic and copies ran while one was open for 1% -> 1% of each run, Pallas kernels for 9% -> 5%
where the time goes in v3:
time: 150 us; the launch traced here: 149 us
  blocking collectives  66.5 us (44%)
  starting transfers between devices  34.3 us (23%)
  Pallas kernels  22.5 us (15%)
  waiting for transfers between devices  18 us (12%)
  local copies, waits for them, and re-layouts  3.95 us (3%)
  between operations  2.13 us (1%)
  other arithmetic  1.5 us (1%)
    all_gather x1, blocking collectives, per_device(): chunks = lax.all_gather(chunk, 'tm', axis_index_groups=same_core)  63.6 us
    all_to_all x1, waiting for transfers between devices, per_device(): everyone = lax.all_to_all(spread, 'tm', 0, 0, axis_index_groups=same_core)  11.5 us
    all_to_all x1, starting transfers between devices, per_device(): gathered = lax.all_to_all(payload, 'seq', 0, 0).reshape(tokens, reach + 128)  7.73 us
    pallas_call x1, Pallas kernels, per_device(): grid_call(project_sibling, 3, (shape((3 * half + channels, cols), BF16),...  7.6 us
    ppermute x1, starting transfers between devices, per_device(): got = lax.ppermute(send, 'tm', flip)  7.48 us
    all_to_all x1, starting transfers between devices, per_device(): everyone = lax.all_to_all(spread, 'tm', 0, 0, axis_index_groups=same_core)  7.2 us
    pallas_call x1, Pallas kernels, per_device(): grid_call(project_own, 3, shape((3 * half, cols), F32), common + [pl.Bloc...  7.03 us
    all_to_all x1, starting transfers between devices, per_device(): shares = lax.all_to_all(shares, 'seq', 0, 0)  6.93 us
  transfers between devices with their start and end apart: 5, of which 2 were waited for; matrix products, arithmetic and copies ran while one was open for 1% of the time, Pallas kernels for 5%

profile of v3, /device:TPU:1, one launch (start us, length us, event | category | flops | bytes accessed | tf_op | source)
XLA Modules:
  0.0 148.8 jit_solution(8171837687172105377)
XLA Ops:
  0.6 3.7 %shard_map.122 = (bf16[16,32,2688]{2,1,0:T(8,128)(2,1)}, bf16[64,2560]{1,0:T(8,128)(2,1)}, f32[2,2560]{1,0:T(2,128)}, f32[2,2560]{1,0:T(2,128)}, s16[560,256]{1,0:T(8,128)(2,1)}) custom-call(s32[1]{0:T(128)} %bitcast.2.core_ref, f32[32,64]{1,0:T(8,128)} %bitcast.31, bf16[64,5120]{1,0:T(8,128)(2,1)} %embed_ref.1, bf16[32,5120]{1,0:T(8,128)(2,1)} %context_ref.1, ...), custom_call_target="tpu_custom_call" | custom-call | flops 20971520 | bytes 5000000 | tf_op jit(solution)/shard_map/pallas_call | solution.py:235
  4.3 7.7 %all-to-all-start = ((bf16[16,32,2688]{2,1,0:T(8,128)(2,1)}), bf16[16,32,2688]{2,1,0:T(8,128)(2,1)S(1)}, u32[]{:S(2)}, u32[]{:S(2)}) async-start(bf16[16,32,2688]{2,1,0:T(8,128)(2,1)} %get-tuple-element.10), calls=%async_computation | async-start | bytes 5505024 | tf_op jit(solution)/shard_map/all_to_all | solution.py:249
  12.1 0.0 copy-done.6
  12.1 4.9 %collective-permute-start = (f32[2,2560]{1,0:T(2,128)S(1)}, f32[2,2560]{1,0:T(2,128)S(1)}, u32[]{:S(2)}, u32[]{:S(2)}) collective-permute-start(f32[2,2560]{1,0:T(2,128)S(1)} %copy-done.6), channel_id=1, source_target_pairs={{0,16},{16,0},{32,48},{48,32},{64,80},{80,64},{96,112},{112,96},{1... | collective-permute-start | bytes 61448 | tf_op jit(solution)/shard_map/ppermute | solution.py:250
  17.0 0.0 copy-done.2
  17.0 63.6 %all-gather.2 = s16[8960,256]{1,0:T(8,128)(2,1)} all-gather(s16[560,256]{1,0:T(8,128)(2,1)S(1)} %copy-done.2), channel_id=2, replica_groups={{0,32,64,96,128,160,192,224,256,288,320,352,384,416,448,480},{16,48,80,..., dimensions={0}, use_global_device_ids=true | all-gather | bytes 4874240 | tf_op jit(solution)/shard_map/all_gather | solution.py:251
  80.6 0.0 collective-permute-done.mods_ref
  80.6 0.0 all-to-all-done
  80.6 0.6 copy-done.7
  81.2 1.0 copy-done
  82.2 7.6 %shard_map.123 = (bf16[1840,256]{1,0:T(8,128)(2,1)}, bf16[3,2560,256]{2,1,0:T(8,128)(2,1)}, f32[64,256]{1,0:T(8,128)}) custom-call(bf16[512,2688]{1,0:T(8,128)(2,1)} %bitcast.24, bf16[64,2560]{1,0:T(8,128)(2,1)} %get-tuple-element.11.embed_ref, f32[2,2560]{1,0:T(2,128)} %copy-done.7, s16[16,560,256]{2,1,0:T(8,128)(2,1)} %bitcast.27, ...), custom_call_target="tpu_custom_call" | custom-call | flops 4000000000 | bytes 5000000 | tf_op jit(solution)/shard_map/pallas_call | solution.py:259
  89.8 7.5 %collective-permute-start.1 = (bf16[1840,256]{1,0:T(8,128)(2,1)}, bf16[1840,256]{1,0:T(8,128)(2,1)S(1)}, u32[]{:S(2)}, u32[]{:S(2)}) collective-permute-start(bf16[1840,256]{1,0:T(8,128)(2,1)} %get-tuple-element.16), channel_id=1, source_target_pairs={{0,16},{16,0},{32,48},{48,32},{64,80},{80,64},{96,112},{112,96},{1... | collective-permute-start | bytes 2826248 | tf_op jit(solution)/shard_map/ppermute | solution.py:272
  97.3 0.0 copy-done.5
  97.3 0.6 fusion.6
  99.2 0.1 maximum_add_fusion.1
  99.3 0.0 copy-done.4
  99.3 7.0 %shard_map.124.own_ref = f32[1776,256]{1,0:T(8,128)} custom-call(bf16[512,2688]{1,0:T(8,128)(2,1)} %bitcast.25, bf16[64,2560]{1,0:T(8,128)(2,1)} %get-tuple-element.11.embed_ref, f32[2,2560]{1,0:T(2,128)} %get-tuple-element.12.mods_ref, bf16[3,2560,256]{2,1,0:T(8,128)(2,1)} %get-tuple-element.15.weight_ref), custom_call_target="tpu_custom_call" | custom-call | flops 4000000000 | bytes 5000000 | tf_op jit(solution)/shard_map/pallas_call | solution.py:273
  106.4 0.0 collective-permute-done.1.got_ref
  106.4 0.9 copy-done.1
  107.3 4.2 %shard_map.125 = bf16[16,16,128]{2,1,0:T(8,128)(2,1)} custom-call(f32[1776,256]{1,0:T(8,128)} %shard_map.124.own_ref, bf16[1840,256]{1,0:T(8,128)(2,1)} %copy-done.1, bf16[512,2688]{1,0:T(8,128)(2,1)} %bitcast.26, f32[64,256]{1,0:T(8,128)} %get-tuple-element.17.heads_ref), custom_call_target="tpu_custom_call" | custom-call | flops 600000000 | bytes 5000000 | tf_op jit(solution)/shard_map/pallas_call | solution.py:284
  111.5 6.9 %all-to-all-start.1 = ((bf16[16,16,128]{2,1,0:T(8,128)(2,1)}), bf16[16,16,128]{2,1,0:T(8,128)(2,1)S(1)}, u32[]{:S(2)}, u32[]{:S(2)}) async-start(bf16[16,16,128]{2,1,0:T(8,128)(2,1)} %shard_map.125), calls=%async_computation.1 | async-start | bytes 131072 | tf_op jit(solution)/shard_map/all_to_all | solution.py:298
  118.5 6.5 %all-to-all-done.1 = bf16[16,16,128]{2,1,0:T(8,128)(2,1)S(1)} async-done(((bf16[16,16,128]{2,1,0:T(8,128)(2,1)}), bf16[16,16,128]{2,1,0:T(8,128)(2,1)S(1)}, u32[]{:S(2)}, u32[]{:S(2)}) %all-to-all-start.1) | async-done | bytes 65568 | tf_op jit(solution)/shard_map/all_to_all | solution.py:298
  125.0 0.1 fusion.2
  125.1 2.9 %all_gather.12 = f32[2,16,128]{2,1,0:T(8,128)S(1)} all-gather(f32[1,16,128]{2,1,0:T(8,128)S(1)} %fusion.2), channel_id=1, replica_groups={{0,16},{32,48},{64,80},{96,112},{128,144},{160,176},{192,208},{224,240}..., dimensions={0}, use_global_device_ids=true | all-gather | bytes 24576 | tf_op jit(solution)/shard_map/all_gather | solution.py:311
  128.0 0.7 broadcast_in_dim.34
  128.7 7.2 %all-to-all-start.2 = ((f32[16,16,128]{2,1,0:T(8,128)}), f32[16,16,128]{2,1,0:T(8,128)S(1)}, u32[]{:S(2)}, u32[]{:S(2)}) async-start(f32[16,16,128]{2,1,0:T(8,128)} %broadcast_in_dim.34), calls=%async_computation.2 | async-start | bytes 262144 | tf_op jit(solution)/shard_map/all_to_all | solution.py:313
  135.9 0.1 slice_bitcast_fusion.1
  136.0 0.6 pad_maximum_fusion
  136.6 11.5 %all-to-all-done.2 = f32[16,16,128]{2,1,0:T(8,128)S(1)} async-done(((f32[16,16,128]{2,1,0:T(8,128)}), f32[16,16,128]{2,1,0:T(8,128)S(1)}, u32[]{:S(2)}, u32[]{:S(2)}) %all-to-all-start.2) | async-done | bytes 131104 | tf_op jit(solution)/shard_map/all_to_all | solution.py:313
  148.0 0.1 select_reduce_fusion
  148.1 0.1 fusion.5
  148.2 0.6 fusion
  (17 shorter events, 0.1 us)
Async XLA Ops:
  4.3 7.7 %copy-start.6 = (f32[2,2560]{1,0:T(2,128)S(1)}, f32[2,2560]{1,0:T(2,128)}, u32[]{:S(2)}) copy-start(f32[2,2560]{1,0:T(2,128)} %get-tuple-element.13) | copy-start | bytes 61444
  4.3 12.7 %copy-start.2 = (s16[560,256]{1,0:T(8,128)(2,1)S(1)}, s16[560,256]{1,0:T(8,128)(2,1)}, u32[]{:S(2)}) copy-start(s16[560,256]{1,0:T(8,128)(2,1)} %get-tuple-element.14) | copy-start | bytes 860164
  4.3 76.3 %all-to-all-start = ((bf16[16,32,2688]{2,1,0:T(8,128)(2,1)}), bf16[16,32,2688]{2,1,0:T(8,128)(2,1)S(1)}, u32[]{:S(2)}, u32[]{:S(2)}) async-start(bf16[16,32,2688]{2,1,0:T(8,128)(2,1)} %get-tuple-element.10), calls=%async_computation | async-start | bytes 5505024 | tf_op jit(solution)/shard_map/all_to_all | solution.py:249
  12.1 68.5 %collective-permute-start = (f32[2,2560]{1,0:T(2,128)S(1)}, f32[2,2560]{1,0:T(2,128)S(1)}, u32[]{:S(2)}, u32[]{:S(2)}) collective-permute-start(f32[2,2560]{1,0:T(2,128)S(1)} %copy-done.6), channel_id=1, source_target_pairs={{0,16},{16,0},{32,48},{48,32},{64,80},{80,64},{96,112},{112,96},{1... | collective-permute-start | bytes 61448 | tf_op jit(solution)/shard_map/ppermute | solution.py:250
  80.6 0.6 copy-start.7
  80.6 1.6 %copy-start = (bf16[16,32,2688]{2,1,0:T(8,128)(2,1)}, bf16[16,32,2688]{2,1,0:T(8,128)(2,1)S(1)}, u32[]{:S(2)}) copy-start(bf16[16,32,2688]{2,1,0:T(8,128)(2,1)S(1)} %all-to-all-done) | copy-start | bytes 8257540
  82.2 15.1 %copy-start.5 = (s32[1,2]{1,0:T(1,128)S(1)}, s32[1,2]{1,0:T(1,128)}, u32[]{:S(2)}) copy-start(s32[1,2]{1,0:T(1,128)} %param.14) | copy-start | bytes 28
  82.2 17.0 %copy-start.8 = (f32[1,64]{1,0:T(1,128)S(1)}, f32[1,64]{1,0:T(1,128)}, u32[]{:S(2)}) copy-start(f32[1,64]{1,0:T(1,128)} %param.17) | copy-start | bytes 772
  82.2 17.1 %copy-start.4 = (f32[1,32,64]{2,1,0:T(8,128)S(1)}, f32[1,32,64]{2,1,0:T(8,128)}, u32[]{:S(2)}) copy-start(f32[1,32,64]{2,1,0:T(8,128)} %param.13) | copy-start | bytes 24580
  89.8 16.5 %collective-permute-start.1 = (bf16[1840,256]{1,0:T(8,128)(2,1)}, bf16[1840,256]{1,0:T(8,128)(2,1)S(1)}, u32[]{:S(2)}, u32[]{:S(2)}) collective-permute-start(bf16[1840,256]{1,0:T(8,128)(2,1)} %get-tuple-element.16), channel_id=1, source_target_pairs={{0,16},{16,0},{32,48},{48,32},{64,80},{80,64},{96,112},{112,96},{1... | collective-permute-start | bytes 2826248 | tf_op jit(solution)/shard_map/ppermute | solution.py:272
  106.4 0.9 copy-start.1
  107.3 40.9 %copy-start.3 = (f32[32,64]{1,0:T(8,128)S(1)}, f32[32,64]{1,0:T(8,128)}, u32[]{:S(2)}) copy-start(f32[32,64]{1,0:T(8,128)} %param.12) | copy-start | bytes 24580
  111.5 13.5 %all-to-all-start.1 = ((bf16[16,16,128]{2,1,0:T(8,128)(2,1)}), bf16[16,16,128]{2,1,0:T(8,128)(2,1)S(1)}, u32[]{:S(2)}, u32[]{:S(2)}) async-start(bf16[16,16,128]{2,1,0:T(8,128)(2,1)} %shard_map.125), calls=%async_computation.1 | async-start | bytes 131072 | tf_op jit(solution)/shard_map/all_to_all | solution.py:298
  128.7 19.4 %all-to-all-start.2 = ((f32[16,16,128]{2,1,0:T(8,128)}), f32[16,16,128]{2,1,0:T(8,128)S(1)}, u32[]{:S(2)}, u32[]{:S(2)}) async-start(f32[16,16,128]{2,1,0:T(8,128)} %broadcast_in_dim.34), calls=%async_computation.2 | async-start | bytes 262144 | tf_op jit(solution)/shard_map/all_to_all | solution.py:313

commit v4 on v3

v4 whole, which is shorter than its diff:
```python
import functools
import math

import jax
import jax.numpy as jnp
from jax import lax
from jax.experimental import pallas as pl
from jax.experimental.pallas import tpu as pltpu
from jax.sharding import PartitionSpec as P

HEAD = 128
NT = 1000
F32 = jnp.float32
BF16 = jnp.bfloat16
KEPT = 14.0
LIMIT = 56 * 1024 * 1024


def sigma_of(level_ids):
    fraction = (level_ids.astype(F32) + 1.0) / NT
    return 5.0 * fraction / (1.0 + 4.0 * fraction)


def dot_nt(a, b):
    return lax.dot_general(a, b, (((1,), (1,)), ((), ())), preferred_element_type=F32)


def dot_nn(a, b):
    return lax.dot_general(a, b, (((1,), (0,)), ((), ())), preferred_element_type=F32)


def split_two(value):
    high = value.astype(BF16)
    return high, (value - high.astype(F32)).astype(BF16)


def to_whole(weight):
    peak = jnp.maximum(jnp.max(jnp.abs(weight), axis=0, keepdims=True), 1e-30)
    power = jnp.floor(-jnp.log2(peak))
    return jnp.round(weight * jnp.exp2(power + KEPT)), power


def from_whole(whole, power):
    return whole.astype(F32) * jnp.exp2(-(power + KEPT))


def whole_block(*dims):
    return pl.BlockSpec(dims, lambda i: (0,) * len(dims))


def grid_call(body, steps, out_shape, in_specs, out_specs, scratch, flops):
    return pl.pallas_call(
        body,
        grid=(steps,),
        out_shape=out_shape,
        in_specs=in_specs,
        out_specs=out_specs,
        scratch_shapes=scratch,
        compiler_params=pltpu.CompilerParams(vmem_limit_bytes=LIMIT),
        cost_estimate=pl.CostEstimate(flops=flops, bytes_accessed=5000000, transcendentals=0),
    )


def pack_weights(odd, qkv_ref, out_ref, head_ref, mine_ref, theirs_ref):
    count, rows, _ = qkv_ref.shape
    channels = head_ref.shape[0]

    def put(at, size, value):
        first, second = value[:, :HEAD], value[:, HEAD:]
        mine_ref[at : at + size, :] = jnp.where(odd, second, first).astype(jnp.int32).astype(jnp.int16)
        theirs_ref[at : at + size, :] = jnp.where(odd, first, second).astype(jnp.int32).astype(jnp.int16)

    row = lax.broadcasted_iota(jnp.int32, (16, 2 * HEAD), 0)
    meta = jnp.zeros((16, 2 * HEAD), F32)
    for i in range(count):
        value, power = to_whole(qkv_ref[i].astype(F32))
        put(i * rows, rows, value)
        meta = jnp.where(row == i, power, meta)
    value, power = to_whole(dot_nn(head_ref[...], out_ref[...]))
    put(count * rows, channels, value)
    put(count * rows + channels, 16, jnp.where(row == count, power, meta))


def pack(rows, place_ref, times_ref, states_ref, gate_ref, embed_ref, context_ref, mods_ref, *refs):
    weight_refs, (payload_ref, embed_out, mods_out, mine_ref, theirs_ref) = refs[:3], refs[3:]
    peers, tokens, _ = payload_ref.shape
    channels, width = embed_ref.shape
    reach = embed_out.shape[1]
    chips = reach // rows
    second, odd = place_ref[0] == 1, place_ref[1] == 1
    latent = states_ref[...].astype(BF16)
    context = context_ref[...].astype(F32)

    def moved(value):
        return pltpu.roll(value, width - rows, 1)

    def blocks(value, put):
        for j in range(chips):
            put(slice(j * rows, (j + 1) * rows), value[:, 2 * j * rows : (2 * j + 1) * rows])

    def mine_of(value):
        return jnp.where(second, moved(value), value)

    def put_context(at, value):
        payload_ref[0, :, at] = value.astype(BF16)

    def put_embed(at, value):
        embed_out[:, at] = value.astype(BF16)

    blocks(mine_of(context), put_context)
    hidden = dot_nn(latent, embed_ref[...]) + context
    scale = lax.rsqrt(jnp.mean(hidden * hidden, axis=-1, keepdims=True) + 1e-06)
    high, low = split_two(scale)
    lane = lax.broadcasted_iota(jnp.int32, (tokens, 128), 1)
    tail = jnp.concatenate([latent.astype(F32), jnp.zeros((tokens, 128 - channels), F32)], axis=1)
    tail = jnp.where(lane == channels, high.astype(F32), tail)
    tail = jnp.where(lane == channels + 1, low.astype(F32), tail)
    payload_ref[0, :, reach:] = tail.astype(BF16)
    for p in range(1, peers):
        payload_ref[p] = payload_ref[0]
    blocks(mine_of(embed_ref[...].astype(F32)), put_embed)
    now = jnp.full((1, channels), times_ref[0, 0], jnp.int32)
    later = jnp.full((1, channels), times_ref[0, 1], jnp.int32)
    factor = (sigma_of(later) - sigma_of(now)) * (1.0 + gate_ref[...])
    for core in range(2):
        value = moved(mods_ref[...]) if core else mods_ref[...]

        def put_mods(at, part, core=core):
            mods_out[core, 0:2, at] = part
            mods_out[core + 2, 0:2, at] = part

        blocks(value, put_mods)
        for p in (core, core + 2):
            mods_out[p, 2:4, :] = jnp.zeros((2, reach), F32)
            mods_out[p, 2:3, :channels] = factor
    pack_weights(odd, *weight_refs, mine_ref, theirs_ref)


def scale_rows(left_ref, context_ref, embed_ref, mods):
    tokens, channels = context_ref.shape[0], embed_ref.shape[0]
    gain = 1.0 + mods[1:2, :]
    left_ref[:tokens, :] = (context_ref[...].astype(F32) * gain).astype(BF16)
    left_ref[tokens : tokens + channels, :] = (embed_ref[...].astype(F32) * gain).astype(BF16)
    row = lax.broadcasted_iota(jnp.int32, (16, gain.shape[1]), 0)
    left_ref[tokens + channels :, :] = jnp.where(row == 0, mods[0:1, :], 0.0).astype(BF16)


def project_sent(rows, place_ref, context_ref, embed_ref, mods_ref, chunk_ref, send_ref, weight_ref, heads_ref, left_ref):
    at = pl.program_id(0)
    odd = place_ref[1]
    channels = heads_ref.shape[0]
    half = left_ref.shape[0]
    scale_rows(left_ref, context_ref, embed_ref, mods_ref[place_ref[2 + at]])

    @pl.when(at == 0)
    def _():
        heads = None
        for q in range(2 * chunk_ref.shape[0]):
            block = chunk_ref[q // 2, (q % 2 + odd) % 2]
            meta = block[3 * rows + channels :, :].astype(F32)
            for i in range(3):
                part = from_whole(block[i * rows : (i + 1) * rows, :], meta[i : i + 1])
                weight_ref[q * rows : (q + 1) * rows, i * HEAD : (i + 1) * HEAD] = part.astype(BF16)
            share = from_whole(block[3 * rows : 3 * rows + channels, :], meta[3:4])
            heads = share if heads is None else heads + share
        heads_ref[...] = heads
        send_ref[2 * half :, :HEAD] = heads.astype(BF16)
        send_ref[2 * half :, HEAD:] = jnp.zeros((channels, 2 * HEAD), BF16)

    result = dot_nn(left_ref[...], weight_ref[...])
    send_ref[pl.ds(pl.multiple_of(at * half, 16), half), :] = result.astype(BF16)


def project_kept(place_ref, context_ref, embed_ref, mods_ref, weight_ref, own_ref, left_ref):
    scale_rows(left_ref, context_ref, embed_ref, mods_ref[place_ref[4 + pl.program_id(0)]])
    own_ref[...] = dot_nn(left_ref[...], weight_ref[...])


def attend(own_ref, got_ref, tail_ref, other_ref, heads_ref, out_ref):
    peers, tokens_here, lanes = out_ref.shape
    channels = lanes // 2
    tokens = tail_ref.shape[0]
    half = tokens + channels + 16
    heads = heads_ref[...] + got_ref[2 * half :, :HEAD].astype(F32)
    heads_high, heads_low = split_two(heads)
    results = []
    for step, ref in enumerate((tail_ref, other_ref)):
        latent = ref[:, :channels]
        scale = ref[:, channels : channels + 1].astype(F32) + ref[:, channels + 1 : channels + 2].astype(F32)
        at = step * half
        body = own_ref[at : at + tokens, :] + got_ref[at : at + tokens, :].astype(F32)
        at += tokens
        high, low = split_two(own_ref[at : at + channels, :] + got_ref[at : at + channels, :].astype(F32))
        at += channels
        shift = own_ref[at : at + 16, :] + got_ref[at : at + 16, :].astype(F32)
        body = body + dot_nn(latent, high) + dot_nn(latent, low)
        made = (body * scale + shift[0:1]).astype(BF16)
        queries, keys, values = (made[:, i * HEAD : (i + 1) * HEAD] for i in range(3))
        scores = dot_nt(queries, keys) * (1.0 / math.sqrt(HEAD))
        weights = jnp.exp(scores - jnp.max(scores, axis=-1, keepdims=True))
        total = jnp.sum(weights, axis=-1, keepdims=True)
        attended = (dot_nn(weights.astype(BF16), values) / total).astype(BF16)
        results.append(dot_nt(attended, heads_high) + dot_nt(attended, heads_low))
    result = jnp.concatenate(results, axis=1).astype(BF16)
    for p in range(peers):
        out_ref[p] = result[p * tokens_here : (p + 1) * tokens_here]


def per_device(
    states, initial, noise_draws, timesteps, context, modulation, out_gate, embed_weight, qkv_weight, out_weight, head_weight
):
    steps, peers = lax.axis_size("tm"), lax.axis_size("seq")
    chips = steps // 2
    mine = lax.axis_index("tm")
    z, core = mine // 2, mine % 2
    odd = z % 2
    tokens_here, channels = initial.shape
    rows = qkv_weight.shape[1]
    tokens = tokens_here * peers
    half = tokens + channels + 16
    reach = chips * rows
    shape = jax.ShapeDtypeStruct

    flip = [(i, i ^ 1) for i in range(steps)]
    across = [(i, i ^ 2) for i in range(steps)]
    fours = [list(range(4 * i, 4 * i + 4)) for i in range(steps // 4)]
    same_head = [[4 * n + 2 * h + c for n in range(chips // 2)] for h in range(2) for c in range(2)]
    same_core = [list(range(0, steps, 2)), list(range(1, steps, 2))]
    spot = mine % 4
    place = jnp.stack([core, odd, spot ^ 1, spot ^ 3, spot, spot ^ 2]).astype(jnp.int32)

    one = pl.BlockSpec(memory_space=pltpu.VMEM)
    scalar = pl.BlockSpec(memory_space=pltpu.SMEM)
    block_rows = 3 * rows + channels + 16
    payload, embed_half, mods_out, chunk, theirs = pl.pallas_call(
        functools.partial(pack, rows),
        out_shape=(
            shape((peers, tokens_here, reach + 128), BF16),
            shape((channels, reach), BF16),
            shape((4, 4, reach), F32),
            shape((block_rows, HEAD), jnp.int16),
            shape((block_rows, HEAD), jnp.int16),
        ),
        in_specs=[scalar] * 2 + [one] * 8,
        out_specs=[one] * 5,
        compiler_params=pltpu.CompilerParams(vmem_limit_bytes=LIMIT),
        cost_estimate=pl.CostEstimate(flops=30000000, bytes_accessed=5000000, transcendentals=0),
    )(place, timesteps, states[0], out_gate, embed_weight, context, modulation[0], qkv_weight, out_weight.T, head_weight)
    received = lax.ppermute(theirs, "tm", across)
    gathered = lax.all_to_all(payload, "seq", 0, 0).reshape(tokens, reach + 128)
    mods = lax.all_to_all(mods_out, "tm", 0, 0, axis_index_groups=fours)
    both = jnp.concatenate([chunk, received], axis=0)
    chunks = lax.all_gather(both, "tm", axis_index_groups=same_head).reshape(chips // 2, 2, block_rows, HEAD)

    width = 3 * HEAD
    common = [scalar, whole_block(tokens, reach), whole_block(channels, reach), whole_block(4, 4, reach)]
    left = [pltpu.VMEM((half, reach), BF16)]
    send, weights, heads = grid_call(
        functools.partial(project_sent, rows),
        2,
        (shape((2 * half + channels, width), BF16), shape((reach, width), BF16), shape((channels, HEAD), F32)),
        common + [whole_block(chips // 2, 2, block_rows, HEAD)],
        [whole_block(2 * half + channels, width), whole_block(reach, width), whole_block(channels, HEAD)],
        left,
        4000000000,
    )(place, gathered, embed_half, mods, chunks)
    got = lax.ppermute(send, "tm", flip)
    other_tail = lax.ppermute(gathered[:, reach:], "tm", across)
    own = grid_call(
        project_kept,
        2,
        shape((2 * half, width), F32),
        common + [whole_block(reach, width)],
        pl.BlockSpec((half, width), lambda i: (i, 0)),
        left,
        4000000000,
    )(place, gathered, embed_half, mods, weights)

    shares = grid_call(
        attend,
        1,
        shape((peers, tokens_here, 2 * channels), BF16),
        [
            whole_block(2 * half, width),
            whole_block(2 * half + channels, width),
            pl.BlockSpec((tokens, 128), lambda i: (0, reach // 128)),
            whole_block(tokens, 128),
            whole_block(channels, HEAD),
        ],
        whole_block(peers, tokens_here, 2 * channels),
        [],
        600000000,
    )(own, got, gathered, other_tail, heads)
    shares = lax.all_to_all(shares, "seq", 0, 0)
    mixed = jnp.sum(shares.astype(F32), axis=0)

    step_size = sigma_of(timesteps[0, 1]) - sigma_of(timesteps[0, 0])
    gain = 1.0 + out_gate
    factors = jnp.concatenate([step_size * gain, lax.dynamic_slice(mods, (spot ^ 2, 2, 0), (1, 1, channels))[0]], axis=1)
    kicks = jnp.sqrt(-step_size) * noise_draws[0]
    drifts = factors * mixed + jnp.pad(kicks, ((0, 0), (0, channels)))
    rest = lax.ppermute(mixed[:, channels:], "tm", across)
    pair = lax.all_gather(drifts, "tm", axis_index_groups=[[2 * i, 2 * i + 1] for i in range(chips)])
    spread = jnp.broadcast_to((pair[0] + pair[1]).astype(BF16)[None], (chips, tokens_here, 2 * channels))
    everyone = lax.all_to_all(spread, "tm", 0, 0, axis_index_groups=same_core).astype(F32)
    velocity_f = gain * (mixed[:, :channels] + rest)
    drift = step_size * velocity_f + kicks
    place_z = lax.broadcasted_iota(jnp.int32, (chips, 1, 1), 0)
    second = (core == 1).astype(F32)

    def weight_of(chip):
        return jnp.where(chip < z, 1.0, jnp.where(chip == z, second, 0.0))

    before = jnp.sum(
        everyone[:, :, :channels] * weight_of(place_z) + everyone[:, :, channels:] * weight_of(place_z ^ 1), axis=0
    )
    new_states = initial + (before - second * drift)
    return (new_states[None], velocity_f.astype(BF16)[None])


def solution(mesh):
    in_specs = (
        P("tm", "seq", None),
        P("seq", None),
        P("tm", "seq", None),
        P("tm", None),
        P("seq", None),
        P("tm", None, None),
        P("tm", None),
        P(),
        P(None, "tm", "seq"),
        P("seq", "tm"),
        P(None, "tm"),
    )
    out_specs = (P("tm", "seq", None), P("tm", "seq", None))
    return jax.shard_map(per_device, mesh=mesh, in_specs=in_specs, out_specs=out_specs, check_vma=False)
```

time: 150 us -> 157 us (1.047)
  blocking collectives: 66.5 us -> 69.2 us
  local copies, waits for them, and re-layouts: 3.95 us -> 6.21 us
  Pallas kernels: 22.5 us -> 24.5 us
    all_to_all x0 -> x1, blocking collectives: none -> 15.3 us  [per_device(): mods = lax.all_to_all(mods_out, 'tm', 0, 0, axis_index_groups=fours)]
    all_gather x2, blocking collectives: 66.5 us -> 53.9 us  [the longest x1 50.7 us: per_device(): lax.all_gather(both, 'tm', axis_index_groups=same_head)]
    ppermute x1 -> x3, waiting for transfers between devices: 0.01 us -> 4.65 us  [the longest x1 4.65 us: per_device(): received = lax.ppermute(theirs, 'tm', across)]
    all_to_all x1, starting transfers between devices: 7.73 us -> 3.86 us  [per_device(): gathered = lax.all_to_all(payload, 'seq', 0, 0).reshape(tokens, reach + 128)]
    all_to_all x1, waiting for transfers between devices: 11.5 us -> 8.79 us  [per_device(): lax.all_to_all(spread, 'tm', 0, 0, axis_index_groups=same_core).astype(F32)]
    ppermute x1 -> x3, starting transfers between devices: 4.94 us -> 7.16 us  [the longest x1 3.25 us: per_device(): rest = lax.ppermute(mixed[:, channels:], 'tm', across)]
    pallas_call x4, Pallas kernels: 22.5 us -> 24.5 us  [the longest x1 8.67 us: per_device(): grid_call(functools.partial(project_sent, rows), 2, (shape((2 * half + ch...]
  transfers between devices with their start and end apart: 5 -> 7, of which waited for: 2 -> 3; matrix products, arithmetic and copies ran while one was open for 1% -> 2% of each run, Pallas kernels for 5% -> 4%
where the time goes in v4:
time: 157 us; the launch traced here: 155 us
  blocking collectives  69.2 us (44%)
  starting transfers between devices  33 us (21%)
  Pallas kernels  24.5 us (16%)
  waiting for transfers between devices  19.4 us (12%)
  local copies, waits for them, and re-layouts  6.21 us (4%)
  between operations  2.23 us (1%)
    all_gather x1, blocking collectives, per_device(): lax.all_gather(both, 'tm', axis_index_groups=same_head)  50.7 us
    all_to_all x1, blocking collectives, per_device(): mods = lax.all_to_all(mods_out, 'tm', 0, 0, axis_index_groups=fours)  15.3 us
    all_to_all x1, waiting for transfers between devices, per_device(): lax.all_to_all(spread, 'tm', 0, 0, axis_index_groups=same_core).astype(F32)  8.79 us
    pallas_call x1, Pallas kernels, per_device(): grid_call(functools.partial(project_sent, rows), 2, (shape((2 * half + ch...  8.67 us
    all_to_all x1, starting transfers between devices, per_device(): shares = lax.all_to_all(shares, 'seq', 0, 0)  7.57 us
    all_to_all x1, starting transfers between devices, per_device(): lax.all_to_all(spread, 'tm', 0, 0, axis_index_groups=same_core).astype(F32)  7.35 us
    ppermute x1, starting transfers between devices, per_device(): got = lax.ppermute(send, 'tm', flip)  7.01 us
    pallas_call x1, Pallas kernels, per_device(): grid_call(project_kept, 2, shape((2 * half, width), F32), common + [whole...  6.98 us
  transfers between devices with their start and end apart: 7, of which 3 were waited for; matrix products, arithmetic and copies ran while one was open for 2% of the time, Pallas kernels for 4%

profile of v4, /device:TPU:1, one launch (start us, length us, event | category | flops | bytes accessed | tf_op | source)
XLA Modules:
  0.0 155.5 jit_solution(3010592415196249531)
XLA Ops:
  0.7 0.7 stack.27.place_ref
  1.4 3.9 %shard_map.122 = (bf16[16,32,2688]{2,1,0:T(8,128)(2,1)}, bf16[64,2560]{1,0:T(8,128)(2,1)}, f32[4,4,2560]{2,1,0:T(4,128)}, s16[560,128]{1,0:T(8,128)(2,1)}, s16[560,128]{1,0:T(8,128)(2,1)}) custom-call(s32[6]{0:T(128)} %stack.27.place_ref, s32[1,2]{1,0:T(1,128)} %times_ref.1, f32[32,64]{1,0:T(8,128)} %bitcast.33, f32[1,64]{1,0:T(1,128)} %gate_ref.1, ...), custom_call_target="tpu_custom_call" | custom-call | flops 30000000 | bytes 5000000 | tf_op jit(solution)/shard_map/pallas_call | solution.py:235
  5.3 15.3 %all_to_all.20.mods_ref = f32[4,4,2560]{2,1,0:T(4,128)} all-to-all(f32[4,4,2560]{2,1,0:T(4,128)} %get-tuple-element.10), channel_id=1, replica_groups={{0,16,32,48},{64,80,96,112},{128,144,160,176},{192,208,224,240},{256,27..., dimensions={0} | all-to-all | bytes 327680 | tf_op jit(solution)/shard_map/all_to_all | solution.py:251
  20.6 3.9 %all-to-all-start.1 = ((bf16[16,32,2688]{2,1,0:T(8,128)(2,1)}), bf16[16,32,2688]{2,1,0:T(8,128)(2,1)S(1)}, u32[]{:S(2)}, u32[]{:S(2)}) async-start(bf16[16,32,2688]{2,1,0:T(8,128)(2,1)} %get-tuple-element.11), calls=%async_computation.1 | async-start | bytes 5505024 | tf_op jit(solution)/shard_map/all_to_all | solution.py:250
  24.5 2.0 %collective-permute-start = (s16[560,128]{1,0:T(8,128)(2,1)S(1)}, s16[560,128]{1,0:T(8,128)(2,1)S(1)}, u32[]{:S(2)}, u32[]{:S(2)}) collective-permute-start(s16[560,128]{1,0:T(8,128)(2,1)S(1)} %copy-done.8), channel_id=1, source_target_pairs={{0,32},{16,48},{32,0},{48,16},{64,96},{80,112},{96,64},{112,80},{1... | collective-permute-start | bytes 430088 | tf_op jit(solution)/shard_map/ppermute | solution.py:249
  26.5 4.6 %collective-permute-done = s16[560,128]{1,0:T(8,128)(2,1)S(1)} collective-permute-done((s16[560,128]{1,0:T(8,128)(2,1)S(1)}, s16[560,128]{1,0:T(8,128)(2,1)S(1)}, u32[]{:S(2)}, u32[]{:S(2)}) %collective-permute-start) | collective-permute-done | bytes 143392 | tf_op jit(solution)/shard_map/ppermute | solution.py:249
  31.1 50.7 %all-gather.3 = s16[8960,128]{1,0:T(8,128)(2,1)} all-gather(s16[1120,128]{1,0:T(8,128)(2,1)S(1)} %pad_add_fusion), channel_id=2, replica_groups={{0,64,128,192,256,320,384,448},{16,80,144,208,272,336,400,464},{32,96,1..., dimensions={0}, use_global_device_ids=true | all-gather | bytes 2580480 | tf_op jit(solution)/shard_map/all_gather | solution.py:253
  81.8 0.0 all-to-all-done.1
  81.8 1.6 copy-done
  83.4 8.7 %shard_map.123 = (bf16[1248,384]{1,0:T(8,128)(2,1)}, bf16[2560,384]{1,0:T(8,128)(2,1)}, f32[64,128]{1,0:T(8,128)}) custom-call(s32[6]{0:T(128)} %stack.27.place_ref, bf16[512,2688]{1,0:T(8,128)(2,1)} %bitcast.26, bf16[64,2560]{1,0:T(8,128)(2,1)} %get-tuple-element.12.embed_ref, f32[4,4,2560]{2,1,0:T(4,128)} %all_to_all.20.mods_ref, ...), custom_call_target="tpu_custom_call" | custom-call | flops 4000000000 | bytes 5000000 | tf_op jit(solution)/shard_map/pallas_call | solution.py:258
  92.0 7.0 %collective-permute-start.1 = (bf16[1248,384]{1,0:T(8,128)(2,1)}, bf16[1248,384]{1,0:T(8,128)(2,1)S(1)}, u32[]{:S(2)}, u32[]{:S(2)}) collective-permute-start(bf16[1248,384]{1,0:T(8,128)(2,1)} %get-tuple-element.16), channel_id=1, source_target_pairs={{0,16},{16,0},{32,48},{48,32},{64,80},{80,64},{96,112},{112,96},{1... | collective-permute-start | bytes 2875400 | tf_op jit(solution)/shard_map/ppermute | solution.py:267
  99.1 0.6 fusion.4
  101.1 0.9 slice.38
  102.0 1.9 %collective-permute-start.2 = (bf16[512,128]{1,0:T(8,128)(2,1)S(1)}, bf16[512,128]{1,0:T(8,128)(2,1)S(1)}, u32[]{:S(2)}, u32[]{:S(2)}) collective-permute-start(bf16[512,128]{1,0:T(8,128)(2,1)S(1)} %slice.38), channel_id=1, source_target_pairs={{0,32},{16,48},{32,0},{48,16},{64,96},{80,112},{96,64},{112,80},{1... | collective-permute-start | bytes 393224 | tf_op jit(solution)/shard_map/ppermute | solution.py:268
  103.9 7.0 %shard_map.124.own_ref = f32[1184,384]{1,0:T(8,128)} custom-call(s32[6]{0:T(128)} %stack.27.place_ref, bf16[512,2688]{1,0:T(8,128)(2,1)} %bitcast.28, bf16[64,2560]{1,0:T(8,128)(2,1)} %get-tuple-element.12.embed_ref, f32[4,4,2560]{2,1,0:T(4,128)} %all_to_all.20.mods_ref, bf16[2560,384]{1,0:T(8,128)(2,1)} %get-tuple-element.15.weight_ref), custom_call_target="tpu_custom_call" | custom-call | flops 4000000000 | bytes 5000000 | tf_op jit(solution)/shard_map/pallas_call | solution.py:269
  110.9 0.0 collective-permute-done.2.other_ref
  110.9 0.0 collective-permute-done.1.got_ref
  110.9 0.7 copy-done.3
  111.6 0.4 copy-done.1
  112.0 5.0 %shard_map.125 = bf16[16,32,128]{2,1,0:T(8,128)(2,1)} custom-call(f32[1184,384]{1,0:T(8,128)} %shard_map.124.own_ref, bf16[1248,384]{1,0:T(8,128)(2,1)} %copy-done.1, bf16[512,2688]{1,0:T(8,128)(2,1)} %bitcast.29, bf16[512,128]{1,0:T(8,128)(2,1)} %copy-done.3, f32[64,128]{1,0:T(8,128)} %get-tuple-element.17.heads_ref), custom_call_target="tpu_custom_call" | custom-call | flops 600000000 | bytes 5000000 | tf_op jit(solution)/shard_map/pallas_call | solution.py:279
  116.9 7.6 %all-to-all-start.2 = ((bf16[16,32,128]{2,1,0:T(8,128)(2,1)}), bf16[16,32,128]{2,1,0:T(8,128)(2,1)S(1)}, u32[]{:S(2)}, u32[]{:S(2)}) async-start(bf16[16,32,128]{2,1,0:T(8,128)(2,1)} %shard_map.125), calls=%async_computation.2 | async-start | bytes 262144 | tf_op jit(solution)/shard_map/all_to_all | solution.py:294
  124.5 0.6 dynamic-slice_bitcast_fusion
  125.2 0.1 maximum_bitcast_fusion
  125.2 6.0 %all-to-all-done.2 = bf16[16,32,128]{2,1,0:T(8,128)(2,1)S(1)} async-done(((bf16[16,32,128]{2,1,0:T(8,128)(2,1)}), bf16[16,32,128]{2,1,0:T(8,128)(2,1)S(1)}, u32[]{:S(2)}, u32[]{:S(2)}) %all-to-all-start.2) | async-done | bytes 131104 | tf_op jit(solution)/shard_map/all_to_all | solution.py:294
  131.2 3.2 %all-gather.1 = f32[64,128]{1,0:T(8,128)S(1)} all-gather(f32[32,128]{1,0:T(8,128)S(1)} %pad_add_fusion.1), channel_id=3, replica_groups={{0,16},{32,48},{64,80},{96,112},{128,144},{160,176},{192,208},{224,240}..., dimensions={0}, use_global_device_ids=true | all-gather | bytes 49152 | tf_op jit(solution)/shard_map/all_gather | solution.py:303
  134.5 0.7 broadcast_in_dim.30
  135.1 7.4 %all-to-all-start.3 = ((bf16[16,32,128]{2,1,0:T(8,128)(2,1)}), bf16[16,32,128]{2,1,0:T(8,128)(2,1)S(1)}, u32[]{:S(2)}, u32[]{:S(2)}) async-start(bf16[16,32,128]{2,1,0:T(8,128)(2,1)} %broadcast_in_dim.30), calls=%async_computation.3 | async-start | bytes 262144 | tf_op jit(solution)/shard_map/all_to_all | solution.py:305
  142.5 0.1 slice.44
  142.6 3.3 %collective-permute-start.3 = (f32[32,64]{1,0:T(8,128)S(1)}, f32[32,64]{1,0:T(8,128)S(1)}, u32[]{:S(2)}, u32[]{:S(2)}) collective-permute-start(f32[32,64]{1,0:T(8,128)S(1)} %slice.44), channel_id=1, source_target_pairs={{0,32},{16,48},{32,0},{48,16},{64,96},{80,112},{96,64},{112,80},{1... | collective-permute-start | bytes 24584 | tf_op jit(solution)/shard_map/ppermute | solution.py:302
  145.9 8.8 %all-to-all-done.3 = bf16[16,32,128]{2,1,0:T(8,128)(2,1)S(1)} async-done(((bf16[16,32,128]{2,1,0:T(8,128)(2,1)}), bf16[16,32,128]{2,1,0:T(8,128)(2,1)S(1)}, u32[]{:S(2)}, u32[]{:S(2)}) %all-to-all-start.3) | async-done | bytes 131104 | tf_op jit(solution)/shard_map/all_to_all | solution.py:305
  154.7 0.2 fusion.1
  154.9 0.6 convert_bitcast_fusion
  (24 shorter events, 0.1 us)
Async XLA Ops:
  20.6 3.9 %copy-start.8 = (s16[560,128]{1,0:T(8,128)(2,1)S(1)}, s16[560,128]{1,0:T(8,128)(2,1)}, u32[]{:S(2)}) copy-start(s16[560,128]{1,0:T(8,128)(2,1)} %get-tuple-element.14) | copy-start | bytes 430084
  20.6 10.5 %copy-start.2 = (s16[560,128]{1,0:T(8,128)(2,1)S(1)}, s16[560,128]{1,0:T(8,128)(2,1)}, u32[]{:S(2)}) copy-start(s16[560,128]{1,0:T(8,128)(2,1)} %get-tuple-element.13) | copy-start | bytes 430084
  20.6 61.2 %all-to-all-start.1 = ((bf16[16,32,2688]{2,1,0:T(8,128)(2,1)}), bf16[16,32,2688]{2,1,0:T(8,128)(2,1)S(1)}, u32[]{:S(2)}, u32[]{:S(2)}) async-start(bf16[16,32,2688]{2,1,0:T(8,128)(2,1)} %get-tuple-element.11), calls=%async_computation.1 | async-start | bytes 5505024 | tf_op jit(solution)/shard_map/all_to_all | solution.py:250
  24.5 6.6 %collective-permute-start = (s16[560,128]{1,0:T(8,128)(2,1)S(1)}, s16[560,128]{1,0:T(8,128)(2,1)S(1)}, u32[]{:S(2)}, u32[]{:S(2)}) collective-permute-start(s16[560,128]{1,0:T(8,128)(2,1)S(1)} %copy-done.8), channel_id=1, source_target_pairs={{0,32},{16,48},{32,0},{48,16},{64,96},{80,112},{96,64},{112,80},{1... | collective-permute-start | bytes 430088 | tf_op jit(solution)/shard_map/ppermute | solution.py:249
  81.8 1.6 copy-start
  83.4 15.7 %copy-start.6 = (s32[1,2]{1,0:T(1,128)S(1)}, s32[1,2]{1,0:T(1,128)}, u32[]{:S(2)}) copy-start(s32[1,2]{1,0:T(1,128)} %times_ref.1) | copy-start | bytes 28
  83.4 17.7 %copy-start.7 = (f32[1,64]{1,0:T(1,128)S(1)}, f32[1,64]{1,0:T(1,128)}, u32[]{:S(2)}) copy-start(f32[1,64]{1,0:T(1,128)} %gate_ref.1) | copy-start | bytes 772
  83.4 17.7 %copy-start.4 = (f32[1,32,64]{2,1,0:T(8,128)S(1)}, f32[1,32,64]{2,1,0:T(8,128)}, u32[]{:S(2)}) copy-start(f32[1,32,64]{2,1,0:T(8,128)} %param.13) | copy-start | bytes 24580
  92.0 18.9 %collective-permute-start.1 = (bf16[1248,384]{1,0:T(8,128)(2,1)}, bf16[1248,384]{1,0:T(8,128)(2,1)S(1)}, u32[]{:S(2)}, u32[]{:S(2)}) collective-permute-start(bf16[1248,384]{1,0:T(8,128)(2,1)} %get-tuple-element.16), channel_id=1, source_target_pairs={{0,16},{16,0},{32,48},{48,32},{64,80},{80,64},{96,112},{112,96},{1... | collective-permute-start | bytes 2875400 | tf_op jit(solution)/shard_map/ppermute | solution.py:267
  102.0 8.9 %collective-permute-start.2 = (bf16[512,128]{1,0:T(8,128)(2,1)S(1)}, bf16[512,128]{1,0:T(8,128)(2,1)S(1)}, u32[]{:S(2)}, u32[]{:S(2)}) collective-permute-start(bf16[512,128]{1,0:T(8,128)(2,1)S(1)} %slice.38), channel_id=1, source_target_pairs={{0,32},{16,48},{32,0},{48,16},{64,96},{80,112},{96,64},{112,80},{1... | collective-permute-start | bytes 393224 | tf_op jit(solution)/shard_map/ppermute | solution.py:268
  110.9 0.7 copy-start.3
  110.9 1.1 copy-start.1
  112.0 42.9 %copy-start.5 = (f32[32,64]{1,0:T(8,128)S(1)}, f32[32,64]{1,0:T(8,128)}, u32[]{:S(2)}) copy-start(f32[32,64]{1,0:T(8,128)} %param.12) | copy-start | bytes 24580
  116.9 14.3 %all-to-all-start.2 = ((bf16[16,32,128]{2,1,0:T(8,128)(2,1)}), bf16[16,32,128]{2,1,0:T(8,128)(2,1)S(1)}, u32[]{:S(2)}, u32[]{:S(2)}) async-start(bf16[16,32,128]{2,1,0:T(8,128)(2,1)} %shard_map.125), calls=%async_computation.2 | async-start | bytes 262144 | tf_op jit(solution)/shard_map/all_to_all | solution.py:294
  135.1 19.5 %all-to-all-start.3 = ((bf16[16,32,128]{2,1,0:T(8,128)(2,1)}), bf16[16,32,128]{2,1,0:T(8,128)(2,1)S(1)}, u32[]{:S(2)}, u32[]{:S(2)}) async-start(bf16[16,32,128]{2,1,0:T(8,128)(2,1)} %broadcast_in_dim.30), calls=%async_computation.3 | async-start | bytes 262144 | tf_op jit(solution)/shard_map/all_to_all | solution.py:305
  142.6 12.3 %collective-permute-start.3 = (f32[32,64]{1,0:T(8,128)S(1)}, f32[32,64]{1,0:T(8,128)S(1)}, u32[]{:S(2)}, u32[]{:S(2)}) collective-permute-start(f32[32,64]{1,0:T(8,128)S(1)} %slice.44), channel_id=1, source_target_pairs={{0,32},{16,48},{32,0},{48,16},{64,96},{80,112},{96,64},{112,80},{1... | collective-permute-start | bytes 24584 | tf_op jit(solution)/shard_map/ppermute | solution.py:302

commit v5 on v0

v5 whole, which is shorter than its diff:
```python
import math

import jax
import jax.numpy as jnp
from jax import lax
from jax.experimental import pallas as pl
from jax.experimental.pallas import tpu as pltpu
from jax.sharding import PartitionSpec as P

HEAD = 128
NT = 1000
F32 = jnp.float32
BF16 = jnp.bfloat16
KEPT = 14.0
LIMIT = 56 * 1024 * 1024


def sigma_of(level_ids):
    fraction = (level_ids.astype(F32) + 1.0) / NT
    return 5.0 * fraction / (1.0 + 4.0 * fraction)


def dot_nt(a, b):
    return lax.dot_general(a, b, (((1,), (1,)), ((), ())), preferred_element_type=F32)


def dot_nn(a, b):
    return lax.dot_general(a, b, (((1,), (0,)), ((), ())), preferred_element_type=F32)


def split_two(value):
    high = value.astype(BF16)
    return high, (value - high.astype(F32)).astype(BF16)


def to_whole(weight):
    peak = jnp.maximum(jnp.max(jnp.abs(weight), axis=0, keepdims=True), 1e-30)
    power = jnp.floor(-jnp.log2(peak))
    whole = jnp.round(weight * jnp.exp2(power + KEPT))
    return whole.astype(jnp.int32).astype(jnp.int16), power


def from_whole(whole, power):
    return whole.astype(F32) * jnp.exp2(-(power + KEPT))


def pack_weights(qkv_ref, out_ref, head_ref, chunk_ref):
    count, rows, cols = qkv_ref.shape
    channels = head_ref.shape[0]
    row = lax.broadcasted_iota(jnp.int32, (16, cols), 0)
    meta = jnp.zeros((16, cols), F32)
    for i in range(count):
        chunk_ref[i * rows : (i + 1) * rows, :], power = to_whole(qkv_ref[i].astype(F32))
        meta = jnp.where(row == i, power, meta)
    at = count * rows
    chunk_ref[at : at + channels, :], power = to_whole(dot_nn(head_ref[...], out_ref[...]))
    meta = jnp.where(row == count, power, meta)
    chunk_ref[at + channels :, :] = meta.astype(jnp.int32).astype(jnp.int16)


def pack(core_ref, times_ref, states_ref, gate_ref, embed_ref, context_ref, *refs):
    weight_refs, (payload_ref, factors_ref, chunk_ref) = refs[:3], refs[3:]
    peers, tokens, lanes = payload_ref.shape
    channels = embed_ref.shape[0]
    half = lanes - 128
    here = pl.ds(pl.multiple_of(core_ref[0] * half, 128), half)
    latent = states_ref[...].astype(BF16)
    payload_ref[0, :, :half] = context_ref[:, here]
    hidden = dot_nn(latent, embed_ref[...]) + context_ref[...].astype(F32)
    scale = lax.rsqrt(jnp.mean(hidden * hidden, axis=-1, keepdims=True) + 1e-06)
    high, low = split_two(scale)
    lane = lax.broadcasted_iota(jnp.int32, (tokens, 128), 1)
    tail = jnp.concatenate([latent.astype(F32), jnp.zeros((tokens, 128 - channels), F32)], axis=1)
    tail = jnp.where(lane == channels, high.astype(F32), tail)
    tail = jnp.where(lane == channels + 1, low.astype(F32), tail)
    payload_ref[0, :, half:] = tail.astype(BF16)
    for p in range(1, peers):
        payload_ref[p] = payload_ref[0]
    gain = 1.0 + jnp.concatenate([gate_ref[...], gate_ref[...]], axis=1)
    now = jnp.full(gain.shape, times_ref[0, 0], jnp.int32)
    later = jnp.full(gain.shape, times_ref[0, 1], jnp.int32)
    step_size = sigma_of(later) - sigma_of(now)
    row = lax.broadcasted_iota(jnp.int32, (8, gain.shape[1]), 0)
    factors_ref[...] = jnp.where(row == 0, gain, jnp.where(row == 1, step_size, jnp.sqrt(-step_size)))
    pack_weights(*weight_refs, chunk_ref)


def after(value, other):
    anywhere = pl.BlockSpec(memory_space=pl.ANY)
    return pl.pallas_call(
        lambda value_ref, other_ref, out_ref: None,
        out_shape=jax.ShapeDtypeStruct(value.shape, value.dtype),
        in_specs=[anywhere, anywhere],
        out_specs=anywhere,
        input_output_aliases={0: 0},
    )(value, other)


def scale_rows(left_ref, context_ref, embed_ref, mods_ref):
    tokens, channels = context_ref.shape[0], embed_ref.shape[0]
    gain = 1.0 + mods_ref[1:2, :]
    left_ref[:tokens, :] = (context_ref[...].astype(F32) * gain).astype(BF16)
    left_ref[tokens : tokens + channels, :] = (embed_ref[...].astype(F32) * gain).astype(BF16)
    row = lax.broadcasted_iota(jnp.int32, (16, gain.shape[1]), 0)
    left_ref[tokens + channels :, :] = jnp.where(row == 0, mods_ref[0:1, :], 0.0).astype(BF16)


def product(i, chunk_ref, extra_ref, left_ref, weight_ref):
    chips, rows, cols = chunk_ref.shape
    row = lax.broadcasted_iota(jnp.int32, (16, cols), 0)
    for n in range(chips):
        meta = extra_ref[n, extra_ref.shape[1] - 16 :, :].astype(F32)
        power = jnp.sum(jnp.where(row == i, meta, 0.0), axis=0, keepdims=True)
        weight_ref[n * rows : (n + 1) * rows, :] = from_whole(chunk_ref[n], power).astype(BF16)
    return dot_nn(left_ref[...], weight_ref[...])


def head_shares(extra_ref):
    channels = extra_ref.shape[1] - 16
    heads = None
    for n in range(extra_ref.shape[0]):
        power = extra_ref[n, channels:, :].astype(F32)[3:4]
        share = from_whole(extra_ref[n, :channels, :], power)
        heads = share if heads is None else heads + share
    return heads


def first_half(
    place_ref, context_ref, embed_ref, mods_ref, chunk_ref, extra_ref, sums_ref, heads_ref, left_ref, weight_ref
):
    i = pl.program_id(0)

    @pl.when(i == 0)
    def _():
        scale_rows(left_ref, context_ref, embed_ref, mods_ref)
        heads_ref[...] = head_shares(extra_ref)

    sums_ref[...] = product(i, chunk_ref, extra_ref, left_ref, weight_ref)


def second_half(
    place_ref,
    context_ref,
    embed_ref,
    mods_ref,
    chunk_ref,
    extra_ref,
    sums_ref,
    heads_ref,
    tail_ref,
    out_ref,
    left_ref,
    weight_ref,
    made_ref,
):
    i = pl.program_id(0)
    tokens, channels = context_ref.shape[0], embed_ref.shape[0]

    @pl.when(i == 0)
    def _():
        scale_rows(left_ref, context_ref, embed_ref, mods_ref)

    total = sums_ref[...] + product(i, chunk_ref, extra_ref, left_ref, weight_ref)
    latent = tail_ref[:, :channels]
    scale = tail_ref[:, channels : channels + 1].astype(F32) + tail_ref[:, channels + 1 : channels + 2].astype(F32)
    high, low = split_two(total[tokens : tokens + channels])
    body = total[:tokens] + dot_nn(latent, high) + dot_nn(latent, low)
    made_ref[i] = (body * scale + total[tokens + channels : tokens + channels + 1]).astype(BF16)

    @pl.when(i == pl.num_programs(0) - 1)
    def _():
        outs = []
        for h in range(made_ref.shape[2] // HEAD):
            cols = slice(h * HEAD, (h + 1) * HEAD)
            scores = dot_nt(made_ref[0, :, cols], made_ref[1, :, cols]) * (1.0 / math.sqrt(HEAD))
            weights = jnp.exp(scores - jnp.max(scores, axis=-1, keepdims=True))
            norm = jnp.sum(weights, axis=-1, keepdims=True)
            outs.append((dot_nn(weights.astype(BF16), made_ref[2, :, cols]) / norm).astype(BF16))
        attended = jnp.concatenate(outs, axis=1)
        head_high, head_low = split_two(heads_ref[...] + head_shares(extra_ref))
        result = dot_nt(attended, head_high) + dot_nt(attended, head_low)
        peers, pair_rows, _ = out_ref.shape
        for p in range(peers):
            at = 2 * p * pair_rows
            block = jnp.concatenate([result[at : at + pair_rows], result[at + pair_rows : at + 2 * pair_rows]], axis=1)
            out_ref[p] = block.astype(BF16)


def per_device(
    states, initial, noise_draws, timesteps, context, modulation, out_gate, embed_weight, qkv_weight, out_weight, head_weight
):
    steps, peers = lax.axis_size("tm"), lax.axis_size("seq")
    chips = steps // 2
    mine = lax.axis_index("tm")
    z, core = mine >> 1, mine & 1
    tokens_here, channels = initial.shape
    rows, cols = qkv_weight.shape[1:]
    tokens = tokens_here * peers
    half = tokens + channels + 16
    reach = chips * rows
    extra = channels + 16
    shape = jax.ShapeDtypeStruct
    place = core[None]

    flip = [(i, i ^ 1) for i in range(steps)]
    same_core = [list(range(0, steps, 2)), list(range(1, steps, 2))]
    one = pl.BlockSpec(memory_space=pltpu.VMEM)
    scalar = pl.BlockSpec(memory_space=pltpu.SMEM)
    params = pltpu.CompilerParams(vmem_limit_bytes=LIMIT)

    payload, factors, chunk = pl.pallas_call(
        pack,
        out_shape=(
            shape((peers, tokens_here, reach + 128), BF16),
            shape((8, 2 * channels), F32),
            shape((3 * rows + extra, cols), jnp.int16),
        ),
        in_specs=[scalar] * 2 + [one] * 7,
        out_specs=[one] * 3,
        compiler_params=params,
        cost_estimate=pl.CostEstimate(flops=30000000, bytes_accessed=5000000, transcendentals=0),
    )(place, timesteps, states[0], out_gate, embed_weight, context, qkv_weight, out_weight.T, head_weight)
    gathered = lax.all_to_all(payload, "seq", 0, 0).reshape(tokens, reach + 128)
    chunks = lax.all_gather(chunk, "tm")
    gathered = after(gathered, chunks)
    flipped = lax.ppermute(gathered, "tm", flip)

    def fixed(*dims):
        return pl.BlockSpec(dims, lambda i, place: (0,) * len(dims))

    def halved(body, at, more_in, out_shape, out_specs, scratch):
        return pl.pallas_call(
            body,
            out_shape=out_shape,
            grid_spec=pltpu.PrefetchScalarGridSpec(
                num_scalar_prefetch=1,
                grid=(3,),
                in_specs=[
                    fixed(tokens, reach),
                    pl.BlockSpec((channels, reach), lambda i, place: (0, at(place[0]))),
                    pl.BlockSpec((2, reach), lambda i, place: (0, at(place[0]))),
                    pl.BlockSpec((chips, rows, cols), lambda i, place: (at(place[0]), i, 0)),
                    pl.BlockSpec((chips, extra, cols), lambda i, place: (at(place[0]), 3 * rows // extra, 0)),
                ]
                + more_in,
                out_specs=out_specs,
                scratch_shapes=[pltpu.VMEM((half, reach), BF16), pltpu.VMEM((reach, cols), BF16)] + scratch,
            ),
            compiler_params=pltpu.CompilerParams(vmem_limit_bytes=32 * 1024 * 1024),
            cost_estimate=pl.CostEstimate(flops=4000000000, bytes_accessed=9000000, transcendentals=0),
        )

    by_kind = pl.BlockSpec((half, cols), lambda i, place: (i, 0))
    sums, heads = halved(
        first_half,
        lambda c: c,
        [],
        (shape((3 * half, cols), F32), shape((channels, cols), F32)),
        [by_kind, fixed(channels, cols)],
        [],
    )(place, gathered, embed_weight, modulation[0], chunks, chunks)
    pair_rows = tokens_here // 2
    shares = halved(
        second_half,
        lambda c: 1 - c,
        [by_kind, fixed(channels, cols), pl.BlockSpec((tokens, 128), lambda i, place: (0, reach // 128))],
        shape((peers, pair_rows, 2 * channels), BF16),
        fixed(peers, pair_rows, 2 * channels),
        [pltpu.VMEM((3, tokens, cols), BF16)],
    )(place, flipped, embed_weight, modulation[0], chunks, chunks, sums, heads, gathered)
    shares = lax.all_to_all(shares, "seq", 0, 0)
    mixed = jnp.sum(shares.astype(F32), axis=0)

    def pairs(value):
        return jnp.concatenate([value[:pair_rows], value[pair_rows:]], axis=1)

    def unpairs(value):
        return jnp.concatenate([value[:, :channels], value[:, channels:]], axis=0)

    velocity_f = factors[0:1] * mixed
    drift = factors[1:2] * velocity_f + factors[2:3] * pairs(noise_draws[0])
    both = lax.all_gather(drift, "tm", axis_index_groups=[[2 * i, 2 * i + 1] for i in range(chips)])
    spread = jnp.broadcast_to((both[0] + both[1]).astype(BF16)[None], (chips, pair_rows, 2 * channels))
    everyone = lax.all_to_all(spread, "tm", 0, 0, axis_index_groups=same_core).astype(F32)
    earlier = lax.broadcasted_iota(jnp.int32, (chips, 1, 1), 0) < z
    before = jnp.sum(jnp.where(earlier, everyone, 0.0), axis=0) + jnp.where(core == 1, both[0], 0.0)
    new_states = initial + unpairs(before)
    return (new_states[None], unpairs(velocity_f).astype(BF16)[None])


def solution(mesh):
    in_specs = (
        P("tm", "seq", None),
        P("seq", None),
        P("tm", "seq", None),
        P("tm", None),
        P("seq", None),
        P("tm", None, None),
        P("tm", None),
        P(),
        P(None, "tm", "seq"),
        P("seq", "tm"),
        P(None, "tm"),
    )
    out_specs = (P("tm", "seq", None), P("tm", "seq", None))
    return jax.shard_map(per_device, mesh=mesh, in_specs=in_specs, out_specs=out_specs, check_vma=False)
```

time: 377 us -> 143 us (0.38)
  waiting for transfers between devices: 256 us -> 17.4 us
  starting transfers between devices: 0.16 us -> 24.9 us
  matrix products: 21.3 us -> 0 us
  Pallas kernels: 0 us -> 15.7 us
  between operations: 15.4 us -> 0.78 us
  local copies, waits for them, and re-layouts: 3.94 us -> 8.5 us
    all_gather x3 -> x0, waiting for transfers between devices: 172 us -> none  [the longest x1 81.2 us: per_device(): full_qkv = lax.all_gather(qkv_weight, 'tm', axis=1, tiled=True)]
    reduce_scatter x1 -> x0, waiting for transfers between devices: 81.9 us -> none  [per_device(): lax.psum_scatter(jnp.dot(mixed, head_float.T, precision=lax.Precision.HIG...]
    all_to_all x0 -> x3, starting transfers between devices: none -> 22.7 us  [the longest x1 7.79 us: per_device(): shares = lax.all_to_all(shares, 'seq', 0, 0)]
    dot_general x5 -> x0, matrix products: 20.5 us -> none  [the longest x1 9.06 us: per_device(): jnp.einsum('td,idc->itc', everyone, full_qkv, preferred_element_type=jnp....]
    all_to_all x0 -> x3, waiting for transfers between devices: none -> 17.4 us  [the longest x1 10.9 us: per_device(): lax.all_to_all(spread, 'tm', 0, 0, axis_index_groups=same_core).astype(F32)]
    pallas_call x0 -> x4, Pallas kernels: none -> 15.7 us  [the longest x1 7.89 us: per_device(): halved(second_half, lambda c: 1 - c, [by_kind, fixed(channels, cols), pl....]
    unnamed x13 -> x18, local copies, waits for them, and re-layouts: 2.72 us -> 6.92 us
  transfers between devices with their start and end apart: 4 -> 4, of which waited for: 4 -> 2; matrix products, arithmetic and copies ran while one was open for 4% -> 1% of each run, Pallas kernels for 0% -> 3%
where the time goes in v5:
time: 143 us
  blocking collectives  74.3 us (52%)
  starting transfers between devices  24.9 us (17%)
  waiting for transfers between devices  17.4 us (12%)
  Pallas kernels  15.7 us (11%)
  local copies, waits for them, and re-layouts  8.5 us (6%)
    all_gather x1, blocking collectives, per_device(): chunks = lax.all_gather(chunk, 'tm')  71.1 us
    all_to_all x1, waiting for transfers between devices, per_device(): lax.all_to_all(spread, 'tm', 0, 0, axis_index_groups=same_core).astype(F32)  10.9 us
    pallas_call x1, Pallas kernels, per_device(): halved(second_half, lambda c: 1 - c, [by_kind, fixed(channels, cols), pl....  7.89 us
    all_to_all x1, starting transfers between devices, per_device(): shares = lax.all_to_all(shares, 'seq', 0, 0)  7.79 us
    all_to_all x1, starting transfers between devices, per_device(): gathered = lax.all_to_all(payload, 'seq', 0, 0).reshape(tokens, reach + 128)  7.72 us
    all_to_all x1, starting transfers between devices, per_device(): lax.all_to_all(spread, 'tm', 0, 0, axis_index_groups=same_core).astype(F32)  7.19 us
    unnamed x18, local copies, waits for them, and re-layouts  6.92 us
    all_to_all x1, waiting for transfers between devices, per_device(): shares = lax.all_to_all(shares, 'seq', 0, 0)  6.5 us
  transfers between devices with their start and end apart: 4, of which 2 were waited for; matrix products, arithmetic and copies ran while one was open for 1% of the time, Pallas kernels for 3%

profile of v5, /device:TPU:1, one launch (start us, length us, event | category | flops | bytes accessed | tf_op | source)
XLA Modules:
  0.0 143.0 jit_solution(4542136796797579784)
XLA Ops:
  0.6 3.4 %shard_map.122 = (bf16[16,32,2688]{2,1,0:T(8,128)(2,1)}, f32[8,128]{1,0:T(8,128)}, s16[560,256]{1,0:T(8,128)(2,1)}) custom-call(s32[1]{0:T(128)} %bitcast.core_ref.place_ref, s32[1,2]{1,0:T(1,128)} %times_ref.1, f32[32,64]{1,0:T(8,128)} %bitcast.37, f32[1,64]{1,0:T(1,128)} %gate_ref.1, bf16[64,5120]{1,0:T(8,128)(2,1)} %embed_ref.5, ...), custom_call_target="tpu_custom_call" | custom-call | flops 30000000 | bytes 5000000 | tf_op jit(solution)/shard_map/pallas_call | solution.py:211
  4.1 7.7 %all-to-all-start = ((bf16[16,32,2688]{2,1,0:T(8,128)(2,1)}), bf16[16,32,2688]{2,1,0:T(8,128)(2,1)S(1)}, u32[]{:S(2)}, u32[]{:S(2)}) async-start(bf16[16,32,2688]{2,1,0:T(8,128)(2,1)} %get-tuple-element.8), calls=%async_computation | async-start | bytes 5505024 | tf_op jit(solution)/shard_map/all_to_all | solution.py:223
  11.8 0.0 copy-done.6
  11.8 71.1 %all-gather.2 = s16[17920,256]{1,0:T(8,128)(2,1)} all-gather(s16[560,256]{1,0:T(8,128)(2,1)S(1)} %copy-done.6), channel_id=2, replica_groups=mesh['tm'=32,'seq'=16] {'tm'}, dimensions={0}, use_global_device_ids=true | all-gather | bytes 9461760 | tf_op jit(solution)/shard_map/all_gather | solution.py:224
  82.9 0.0 all-to-all-done
  82.9 1.5 %copy-done.1 = bf16[16,32,2688]{2,1,0:T(8,128)(2,1)} copy-done((bf16[16,32,2688]{2,1,0:T(8,128)(2,1)}, bf16[16,32,2688]{2,1,0:T(8,128)(2,1)S(1)}, u32[]{:S(2)}) %copy-start.1) | copy-done | bytes 2752536
  84.4 2.2 %collective-permute-start = (bf16[512,2688]{1,0:T(8,128)(2,1)}, bf16[512,2688]{1,0:T(8,128)(2,1)S(1)}, u32[]{:S(2)}, u32[]{:S(2)}) collective-permute-start(bf16[512,2688]{1,0:T(8,128)(2,1)} %shard_map.123.context_ref.tail_ref), channel_id=1, source_target_pairs={{0,16},{16,0},{32,48},{48,32},{64,80},{80,64},{96,112},{112,96},{1... | collective-permute-start | bytes 8257544 | tf_op jit(solution)/shard_map/ppermute | solution.py:226
  86.6 0.8 slice_bitcast_fusion.4
  87.4 0.0 copy-done.8
  87.4 0.0 copy-done.4
  87.4 0.0 copy-done.5
  87.4 0.0 copy-start
  87.4 3.6 %copy-done = s16[17920,256]{1,0:T(8,128)(2,1)S(1)} copy-done((s16[17920,256]{1,0:T(8,128)(2,1)S(1)}, s16[17920,256]{1,0:T(8,128)(2,1)}, u32[]{:S(2)}) %copy-start) | copy-done | bytes 9175064
  91.0 1.8 %copy-done.2 = bf16[512,2688]{1,0:T(8,128)(2,1)S(1)} copy-done((bf16[512,2688]{1,0:T(8,128)(2,1)S(1)}, bf16[512,2688]{1,0:T(8,128)(2,1)}, u32[]{:S(2)}) %copy-start.2) | copy-done | bytes 2752536
  92.8 4.3 %shard_map.124 = (f32[1776,256]{1,0:T(8,128)S(1)}, f32[64,256]{1,0:T(8,128)S(1)}) custom-call(s32[1]{0:T(128)} %bitcast.core_ref.place_ref, bf16[512,2688]{1,0:T(8,128)(2,1)S(1)} %copy-done.2, bf16[64,5120]{1,0:T(8,128)(2,1)S(1)} %copy-done.4, f32[2,5120]{1,0:T(2,128)S(1)} %bitcast.34, s16[32,560,256]{2,1,0:T(8,128)(2,1)S(1)} %bitcast.29, ...), custom_call_target="tpu_custom_call" | custom-call | flops 4000000000 | bytes 9000000 | tf_op jit(solution)/shard_map/pallas_call | solution.py:254
  97.1 0.0 collective-permute-done.context_ref
  97.1 0.0 copy-done.3
  97.1 0.0 copy-start.7
  97.1 7.9 %shard_map.125 = bf16[16,16,128]{2,1,0:T(8,128)(2,1)} custom-call(s32[1]{0:T(128)} %bitcast.core_ref.place_ref, bf16[512,2688]{1,0:T(8,128)(2,1)S(1)} %collective-permute-done.context_ref, bf16[64,5120]{1,0:T(8,128)(2,1)S(1)} %copy-done.4, f32[2,5120]{1,0:T(2,128)S(1)} %bitcast.35, s16[32,560,256]{2,1,0:T(8,128)(2,1)S(1)} %bitcast.31, ...), custom_call_target="tpu_custom_call" | custom-call | flops 4000000000 | bytes 9000000 | tf_op jit(solution)/shard_map/pallas_call | solution.py:263
  105.0 7.8 %all-to-all-start.1 = ((bf16[16,16,128]{2,1,0:T(8,128)(2,1)}), bf16[16,16,128]{2,1,0:T(8,128)(2,1)S(1)}, u32[]{:S(2)}, u32[]{:S(2)}) async-start(bf16[16,16,128]{2,1,0:T(8,128)(2,1)} %shard_map.125), calls=%async_computation.1 | async-start | bytes 131072 | tf_op jit(solution)/shard_map/all_to_all | solution.py:271
  112.8 6.5 %all-to-all-done.1 = bf16[16,16,128]{2,1,0:T(8,128)(2,1)S(1)} async-done(((bf16[16,16,128]{2,1,0:T(8,128)(2,1)}), bf16[16,16,128]{2,1,0:T(8,128)(2,1)S(1)}, u32[]{:S(2)}, u32[]{:S(2)}) %all-to-all-start.1) | async-done | bytes 65568 | tf_op jit(solution)/shard_map/all_to_all | solution.py:271
  119.4 0.1 fusion.2
  119.5 3.3 %all_gather.12 = f32[2,16,128]{2,1,0:T(8,128)S(1)} all-gather(f32[1,16,128]{2,1,0:T(8,128)S(1)} %fusion.2), channel_id=1, replica_groups={{0,16},{32,48},{64,80},{96,112},{128,144},{160,176},{192,208},{224,240}..., dimensions={0}, use_global_device_ids=true | all-gather | bytes 24576 | tf_op jit(solution)/shard_map/all_gather | solution.py:282
  122.8 0.6 broadcast_in_dim.34
  123.4 7.2 %all-to-all-start.2 = ((bf16[16,16,128]{2,1,0:T(8,128)(2,1)}), bf16[16,16,128]{2,1,0:T(8,128)(2,1)S(1)}, u32[]{:S(2)}, u32[]{:S(2)}) async-start(bf16[16,16,128]{2,1,0:T(8,128)(2,1)} %broadcast_in_dim.34), calls=%async_computation.2 | async-start | bytes 131072 | tf_op jit(solution)/shard_map/all_to_all | solution.py:284
  130.6 0.1 slice_bitcast_fusion.1
  130.7 0.6 pad_maximum_fusion
  131.3 10.9 %all-to-all-done.2 = bf16[16,16,128]{2,1,0:T(8,128)(2,1)S(1)} async-done(((bf16[16,16,128]{2,1,0:T(8,128)(2,1)}), bf16[16,16,128]{2,1,0:T(8,128)(2,1)S(1)}, u32[]{:S(2)}, u32[]{:S(2)}) %all-to-all-start.2) | async-done | bytes 65568 | tf_op jit(solution)/shard_map/all_to_all | solution.py:284
  142.2 0.1 select_reduce_fusion
  142.3 0.1 fusion.6
  142.4 0.0 copy-done.7
  142.4 0.6 fusion
  (14 shorter events, 0.1 us)
Async XLA Ops:
  4.1 7.7 %copy-start.6 = (s16[560,256]{1,0:T(8,128)(2,1)S(1)}, s16[560,256]{1,0:T(8,128)(2,1)}, u32[]{:S(2)}) copy-start(s16[560,256]{1,0:T(8,128)(2,1)} %get-tuple-element.9) | copy-start | bytes 860164
  4.1 78.8 %all-to-all-start = ((bf16[16,32,2688]{2,1,0:T(8,128)(2,1)}), bf16[16,32,2688]{2,1,0:T(8,128)(2,1)S(1)}, u32[]{:S(2)}, u32[]{:S(2)}) async-start(bf16[16,32,2688]{2,1,0:T(8,128)(2,1)} %get-tuple-element.8), calls=%async_computation | async-start | bytes 5505024 | tf_op jit(solution)/shard_map/all_to_all | solution.py:223
  82.9 1.5 %copy-start.1 = (bf16[16,32,2688]{2,1,0:T(8,128)(2,1)}, bf16[16,32,2688]{2,1,0:T(8,128)(2,1)S(1)}, u32[]{:S(2)}) copy-start(bf16[16,32,2688]{2,1,0:T(8,128)(2,1)S(1)} %all-to-all-done) | copy-start | bytes 8257540
  84.4 3.0 %copy-start.8 = (f32[1,32,64]{2,1,0:T(8,128)S(1)}, f32[1,32,64]{2,1,0:T(8,128)}, u32[]{:S(2)}) copy-start(f32[1,32,64]{2,1,0:T(8,128)} %param.13) | copy-start | bytes 24580
  84.4 3.0 %copy-start.4 = (bf16[64,5120]{1,0:T(8,128)(2,1)S(1)}, bf16[64,5120]{1,0:T(8,128)(2,1)}, u32[]{:S(2)}) copy-start(bf16[64,5120]{1,0:T(8,128)(2,1)} %embed_ref.5) | copy-start | bytes 1966084
  84.4 3.0 %copy-start.5 = (f32[1,2,5120]{2,1,0:T(2,128)S(1)}, f32[1,2,5120]{2,1,0:T(2,128)}, u32[]{:S(2)}) copy-start(f32[1,2,5120]{2,1,0:T(2,128)} %param.16) | copy-start | bytes 122884
  84.4 12.7 %collective-permute-start = (bf16[512,2688]{1,0:T(8,128)(2,1)}, bf16[512,2688]{1,0:T(8,128)(2,1)S(1)}, u32[]{:S(2)}, u32[]{:S(2)}) collective-permute-start(bf16[512,2688]{1,0:T(8,128)(2,1)} %shard_map.123.context_ref.tail_ref), channel_id=1, source_target_pairs={{0,16},{16,0},{32,48},{48,32},{64,80},{80,64},{96,112},{112,96},{1... | collective-permute-start | bytes 8257544 | tf_op jit(solution)/shard_map/ppermute | solution.py:226
  87.4 3.6 %copy-start = (s16[17920,256]{1,0:T(8,128)(2,1)S(1)}, s16[17920,256]{1,0:T(8,128)(2,1)}, u32[]{:S(2)}) copy-start(s16[17920,256]{1,0:T(8,128)(2,1)} %all-gather.2) | copy-start | bytes 27525124
  91.0 1.8 %copy-start.2 = (bf16[512,2688]{1,0:T(8,128)(2,1)S(1)}, bf16[512,2688]{1,0:T(8,128)(2,1)}, u32[]{:S(2)}) copy-start(bf16[512,2688]{1,0:T(8,128)(2,1)} %shard_map.123.context_ref.tail_ref) | copy-start | bytes 8257540
  92.8 4.4 %copy-start.3 = (bf16[512,2688]{1,0:T(8,128)(2,1)S(1)}, bf16[512,2688]{1,0:T(8,128)(2,1)}, u32[]{:S(2)}) copy-start(bf16[512,2688]{1,0:T(8,128)(2,1)} %shard_map.123.context_ref.tail_ref) | copy-start | bytes 8257540
  97.1 45.2 %copy-start.7 = (f32[32,64]{1,0:T(8,128)S(1)}, f32[32,64]{1,0:T(8,128)}, u32[]{:S(2)}) copy-start(f32[32,64]{1,0:T(8,128)} %param.12) | copy-start | bytes 24580
  105.0 14.3 %all-to-all-start.1 = ((bf16[16,16,128]{2,1,0:T(8,128)(2,1)}), bf16[16,16,128]{2,1,0:T(8,128)(2,1)S(1)}, u32[]{:S(2)}, u32[]{:S(2)}) async-start(bf16[16,16,128]{2,1,0:T(8,128)(2,1)} %shard_map.125), calls=%async_computation.1 | async-start | bytes 131072 | tf_op jit(solution)/shard_map/all_to_all | solution.py:271
  123.4 18.8 %all-to-all-start.2 = ((bf16[16,16,128]{2,1,0:T(8,128)(2,1)}), bf16[16,16,128]{2,1,0:T(8,128)(2,1)S(1)}, u32[]{:S(2)}, u32[]{:S(2)}) async-start(bf16[16,16,128]{2,1,0:T(8,128)(2,1)} %broadcast_in_dim.34), calls=%async_computation.2 | async-start | bytes 131072 | tf_op jit(solution)/shard_map/all_to_all | solution.py:284

commit v6 on v5

--- a/solution.py
+++ b/solution.py
@@ -58,8 +58,8 @@
     chunk_ref[at + channels :, :] = meta.astype(jnp.int32).astype(jnp.int16)
 
 
-def pack(core_ref, times_ref, states_ref, gate_ref, embed_ref, context_ref, *refs):
-    weight_refs, (payload_ref, factors_ref, chunk_ref) = refs[:3], refs[3:]
+def pack(core_ref, times_ref, states_ref, noise_ref, gate_ref, embed_ref, context_ref, *refs):
+    weight_refs, (payload_ref, gains_ref, sizes_ref, kicks_ref, chunk_ref) = refs[:3], refs[3:]
     peers, tokens, lanes = payload_ref.shape
     channels = embed_ref.shape[0]
     half = lanes - 128
@@ -80,20 +80,12 @@
     now = jnp.full(gain.shape, times_ref[0, 0], jnp.int32)
     later = jnp.full(gain.shape, times_ref[0, 1], jnp.int32)
     step_size = sigma_of(later) - sigma_of(now)
-    row = lax.broadcasted_iota(jnp.int32, (8, gain.shape[1]), 0)
-    factors_ref[...] = jnp.where(row == 0, gain, jnp.where(row == 1, step_size, jnp.sqrt(-step_size)))
+    gains_ref[...] = jnp.broadcast_to(gain, gains_ref.shape)
+    sizes_ref[...] = jnp.broadcast_to(step_size, sizes_ref.shape)
+    pair_rows = tokens // 2
+    noise = jnp.concatenate([noise_ref[:pair_rows], noise_ref[pair_rows:]], axis=1)
+    kicks_ref[...] = jnp.sqrt(-step_size) * noise
     pack_weights(*weight_refs, chunk_ref)
-
-
-def after(value, other):
-    anywhere = pl.BlockSpec(memory_space=pl.ANY)
-    return pl.pallas_call(
-        lambda value_ref, other_ref, out_ref: None,
-        out_shape=jax.ShapeDtypeStruct(value.shape, value.dtype),
-        in_specs=[anywhere, anywhere],
-        out_specs=anywhere,
-        input_output_aliases={0: 0},
-    )(value, other)
 
 
 def scale_rows(left_ref, context_ref, embed_ref, mods_ref):
@@ -208,27 +200,29 @@
     scalar = pl.BlockSpec(memory_space=pltpu.SMEM)
     params = pltpu.CompilerParams(vmem_limit_bytes=LIMIT)
 
-    payload, factors, chunk = pl.pallas_call(
+    pair_rows = tokens_here // 2
+    payload, gains, sizes, kicks, chunk = pl.pallas_call(
         pack,
         out_shape=(
             shape((peers, tokens_here, reach + 128), BF16),
-            shape((8, 2 * channels), F32),
+            shape((pair_rows, 2 * channels), F32),
+            shape((pair_rows, 2 * channels), F32),
+            shape((pair_rows, 2 * channels), F32),
             shape((3 * rows + extra, cols), jnp.int16),
         ),
-        in_specs=[scalar] * 2 + [one] * 7,
-        out_specs=[one] * 3,
+        in_specs=[scalar] * 2 + [one] * 8,
+        out_specs=[one] * 5,
         compiler_params=params,
         cost_estimate=pl.CostEstimate(flops=30000000, bytes_accessed=5000000, transcendentals=0),
-    )(place, timesteps, states[0], out_gate, embed_weight, context, qkv_weight, out_weight.T, head_weight)
+    )(place, timesteps, states[0], noise_draws[0], out_gate, embed_weight, context, qkv_weight, out_weight.T, head_weight)
     gathered = lax.all_to_all(payload, "seq", 0, 0).reshape(tokens, reach + 128)
     chunks = lax.all_gather(chunk, "tm")
-    gathered = after(gathered, chunks)
     flipped = lax.ppermute(gathered, "tm", flip)
 
     def fixed(*dims):
         return pl.BlockSpec(dims, lambda i, place: (0,) * len(dims))
 
-    def halved(body, at, more_in, out_shape, out_specs, scratch):
+    def halved(body, at, more_in, out_shape, out_specs, scratch, flops):
         return pl.pallas_call(
             body,
             out_shape=out_shape,
@@ -246,8 +240,8 @@
                 out_specs=out_specs,
                 scratch_shapes=[pltpu.VMEM((half, reach), BF16), pltpu.VMEM((reach, cols), BF16)] + scratch,
             ),
-            compiler_params=pltpu.CompilerParams(vmem_limit_bytes=32 * 1024 * 1024),
-            cost_estimate=pl.CostEstimate(flops=4000000000, bytes_accessed=9000000, transcendentals=0),
+            compiler_params=pltpu.CompilerParams(vmem_limit_bytes=46 * 1024 * 1024),
+            cost_estimate=pl.CostEstimate(flops=flops, bytes_accessed=9000000, transcendentals=0),
         )
 
     by_kind = pl.BlockSpec((half, cols), lambda i, place: (i, 0))
@@ -258,8 +252,8 @@
         (shape((3 * half, cols), F32), shape((channels, cols), F32)),
         [by_kind, fixed(channels, cols)],
         [],
+        100000000000,
     )(place, gathered, embed_weight, modulation[0], chunks, chunks)
-    pair_rows = tokens_here // 2
     shares = halved(
         second_half,
         lambda c: 1 - c,
@@ -267,18 +261,16 @@
         shape((peers, pair_rows, 2 * channels), BF16),
         fixed(peers, pair_rows, 2 * channels),
         [pltpu.VMEM((3, tokens, cols), BF16)],
+        4000000000,
     )(place, flipped, embed_weight, modulation[0], chunks, chunks, sums, heads, gathered)
     shares = lax.all_to_all(shares, "seq", 0, 0)
     mixed = jnp.sum(shares.astype(F32), axis=0)
 
-    def pairs(value):
-        return jnp.concatenate([value[:pair_rows], value[pair_rows:]], axis=1)
-
     def unpairs(value):
         return jnp.concatenate([value[:, :channels], value[:, channels:]], axis=0)
 
-    velocity_f = factors[0:1] * mixed
-    drift = factors[1:2] * velocity_f + factors[2:3] * pairs(noise_draws[0])
+    velocity_f = gains * mixed
+    drift = sizes * velocity_f + kicks
     both = lax.all_gather(drift, "tm", axis_index_groups=[[2 * i, 2 * i + 1] for i in range(chips)])
     spread = jnp.broadcast_to((both[0] + both[1]).astype(BF16)[None], (chips, pair_rows, 2 * channels))
     everyone = lax.all_to_all(spread, "tm", 0, 0, axis_index_groups=same_core).astype(F32)

time: 143 us -> 138 us (0.965)
  local copies, waits for them, and re-layouts: 8.5 us -> 0.83 us
  Pallas kernels: 15.7 us -> 17.9 us
    unnamed x18 -> x12, local copies, waits for them, and re-layouts: 6.92 us -> 0.04 us
  transfers between devices with their start and end apart: 4 -> 4, of which waited for: 2 -> 2; matrix products, arithmetic and copies ran while one was open for 1% -> 0% of each run, Pallas kernels for 3% -> 4%
where the time goes in v6:
time: 138 us
  blocking collectives  74.6 us (54%)
  starting transfers between devices  24.7 us (18%)
  Pallas kernels  17.9 us (13%)
  waiting for transfers between devices  17.4 us (13%)
    all_gather x1, blocking collectives, per_device(): chunks = lax.all_gather(chunk, 'tm')  71.4 us
    all_to_all x1, waiting for transfers between devices, per_device(): lax.all_to_all(spread, 'tm', 0, 0, axis_index_groups=same_core).astype(F32)  10.9 us
    pallas_call x1, Pallas kernels, per_device(): halved(second_half, lambda c: 1 - c, [by_kind, fixed(channels, cols), pl....  8.86 us
    all_to_all x1, starting transfers between devices, per_device(): shares = lax.all_to_all(shares, 'seq', 0, 0)  7.7 us
    all_to_all x1, starting transfers between devices, per_device(): gathered = lax.all_to_all(payload, 'seq', 0, 0).reshape(tokens, reach + 128)  7.59 us
    all_to_all x1, starting transfers between devices, per_device(): lax.all_to_all(spread, 'tm', 0, 0, axis_index_groups=same_core).astype(F32)  7.33 us
    all_to_all x1, waiting for transfers between devices, per_device(): shares = lax.all_to_all(shares, 'seq', 0, 0)  6.5 us
    pallas_call x1, Pallas kernels, per_device(): halved(first_half, lambda c: c, [], (shape((3 * half, cols), F32), shape(...  5.61 us
  transfers between devices with their start and end apart: 4, of which 2 were waited for; matrix products, arithmetic and copies ran while one was open for 0% of the time, Pallas kernels for 4%

profile of v6, /device:TPU:1, one launch (start us, length us, event | category | flops | bytes accessed | tf_op | source)
XLA Modules:
  0.0 137.6 jit_solution(7485493494654503819)
XLA Ops:
  0.6 3.4 %shard_map.122 = (bf16[16,32,2688]{2,1,0:T(8,128)(2,1)}, f32[16,128]{1,0:T(8,128)}, f32[16,128]{1,0:T(8,128)}, f32[16,128]{1,0:T(8,128)}, s16[560,256]{1,0:T(8,128)(2,1)}) custom-call(s32[1]{0:T(128)} %bitcast.core_ref.place_ref, s32[1,2]{1,0:T(1,128)} %times_ref.1, f32[32,64]{1,0:T(8,128)} %bitcast.23, f32[32,64]{1,0:T(8,128)} %bitcast.24, ...), custom_call_target="tpu_custom_call" | custom-call | flops 30000000 | bytes 5000000 | tf_op jit(solution)/shard_map/pallas_call | solution.py:204
  4.1 7.6 %all-to-all-start = ((bf16[16,32,2688]{2,1,0:T(8,128)(2,1)}), bf16[16,32,2688]{2,1,0:T(8,128)(2,1)S(1)}, u32[]{:S(2)}, u32[]{:S(2)}) async-start(bf16[16,32,2688]{2,1,0:T(8,128)(2,1)} %get-tuple-element.11), calls=%async_computation | async-start | bytes 5505024 | tf_op jit(solution)/shard_map/all_to_all | solution.py:218
  11.7 0.0 copy-start
  11.7 0.0 copy-start.1
  11.7 71.4 %all-gather.3 = s16[17920,256]{1,0:T(8,128)(2,1)} all-gather(s16[560,256]{1,0:T(8,128)(2,1)} %get-tuple-element.12), channel_id=2, replica_groups=mesh['tm'=32,'seq'=16] {'tm'}, dimensions={0}, use_global_device_ids=true | all-gather | bytes 9461760 | tf_op jit(solution)/shard_map/all_gather | solution.py:219
  83.0 0.0 all-to-all-done
  83.0 2.0 %collective-permute-start = (bf16[512,2688]{1,0:T(8,128)(2,1)S(1)}, bf16[512,2688]{1,0:T(8,128)(2,1)S(1)}, u32[]{:S(2)}, u32[]{:S(2)}) collective-permute-start(bf16[512,2688]{1,0:T(8,128)(2,1)S(1)} %bitcast.13), channel_id=1, source_target_pairs={{0,16},{16,0},{32,48},{48,32},{64,80},{80,64},{96,112},{112,96},{1... | collective-permute-start | bytes 8257544 | tf_op jit(solution)/shard_map/ppermute | solution.py:220
  85.1 0.0 copy-done
  85.1 0.0 copy-done.1
  85.1 5.6 %shard_map.123 = (f32[1776,256]{1,0:T(8,128)S(1)}, f32[64,256]{1,0:T(8,128)S(1)}) custom-call(s32[1]{0:T(128)} %bitcast.core_ref.place_ref, bf16[512,2688]{1,0:T(8,128)(2,1)S(1)} %bitcast.14, bf16[64,5120]{1,0:T(8,128)(2,1)S(1)} %copy-done, f32[2,5120]{1,0:T(2,128)S(1)} %bitcast.16, s16[32,560,256]{2,1,0:T(8,128)(2,1)} %bitcast.18, s16[32,560,256]{2,1,0:T(8,128)(2,1)} %bitcast.19), custom_call_target="tpu_custom_call" | custom-call | flops 99999997952 | bytes 9000000 | tf_op jit(solution)/shard_map/pallas_call | solution.py:248
  90.7 0.0 collective-permute-done.context_ref
  90.7 0.0 copy-start.3
  90.7 0.0 copy-start.4
  90.8 0.0 copy-start.5
  90.8 0.0 copy-start.2
  90.8 8.9 %shard_map.124 = bf16[16,16,128]{2,1,0:T(8,128)(2,1)} custom-call(s32[1]{0:T(128)} %bitcast.core_ref.place_ref, bf16[512,2688]{1,0:T(8,128)(2,1)S(1)} %collective-permute-done.context_ref, bf16[64,5120]{1,0:T(8,128)(2,1)S(1)} %copy-done, f32[2,5120]{1,0:T(2,128)S(1)} %bitcast.17, s16[32,560,256]{2,1,0:T(8,128)(2,1)} %bitcast.20, ...), custom_call_target="tpu_custom_call" | custom-call | flops 4000000000 | bytes 9000000 | tf_op jit(solution)/shard_map/pallas_call | solution.py:257
  99.6 7.7 %all-to-all-start.1 = ((bf16[16,16,128]{2,1,0:T(8,128)(2,1)}), bf16[16,16,128]{2,1,0:T(8,128)(2,1)S(1)}, u32[]{:S(2)}, u32[]{:S(2)}) async-start(bf16[16,16,128]{2,1,0:T(8,128)(2,1)} %shard_map.124), calls=%async_computation.1 | async-start | bytes 131072 | tf_op jit(solution)/shard_map/all_to_all | solution.py:266
  107.4 6.5 %all-to-all-done.1 = bf16[16,16,128]{2,1,0:T(8,128)(2,1)S(1)} async-done(((bf16[16,16,128]{2,1,0:T(8,128)(2,1)}), bf16[16,16,128]{2,1,0:T(8,128)(2,1)S(1)}, u32[]{:S(2)}, u32[]{:S(2)}) %all-to-all-start.1) | async-done | bytes 65568 | tf_op jit(solution)/shard_map/all_to_all | solution.py:266
  113.9 0.0 copy-done.3
  113.9 0.0 copy-done.4
  113.9 0.0 copy-done.5
  113.9 3.3 %all-gather.1 = f32[32,128]{1,0:T(8,128)S(1)} all-gather(f32[16,128]{1,0:T(8,128)S(1)} %get-tuple-element.17), channel_id=3, replica_groups={{0,16},{32,48},{64,80},{96,112},{128,144},{160,176},{192,208},{224,240}..., dimensions={0}, use_global_device_ids=true | all-gather | bytes 24576 | tf_op jit(solution)/shard_map/all_gather | solution.py:274
  117.2 0.6 broadcast_in_dim.34
  117.9 7.3 %all-to-all-start.2 = ((bf16[16,16,128]{2,1,0:T(8,128)(2,1)}), bf16[16,16,128]{2,1,0:T(8,128)(2,1)S(1)}, u32[]{:S(2)}, u32[]{:S(2)}) async-start(bf16[16,16,128]{2,1,0:T(8,128)(2,1)} %broadcast_in_dim.34), calls=%async_computation.2 | async-start | bytes 131072 | tf_op jit(solution)/shard_map/all_to_all | solution.py:276
  125.2 0.1 slice_bitcast_fusion.1
  125.3 0.6 pad_maximum_fusion
  125.9 10.9 %all-to-all-done.2 = bf16[16,16,128]{2,1,0:T(8,128)(2,1)S(1)} async-done(((bf16[16,16,128]{2,1,0:T(8,128)(2,1)}), bf16[16,16,128]{2,1,0:T(8,128)(2,1)S(1)}, u32[]{:S(2)}, u32[]{:S(2)}) %all-to-all-start.2) | async-done | bytes 65568 | tf_op jit(solution)/shard_map/all_to_all | solution.py:276
  136.8 0.1 select_reduce_fusion
  136.9 0.1 fusion.2
  137.0 0.0 copy-done.2
  137.0 0.6 fusion
  (5 shorter events, 0.0 us)
Async XLA Ops:
  4.1 79.0 %all-to-all-start = ((bf16[16,32,2688]{2,1,0:T(8,128)(2,1)}), bf16[16,32,2688]{2,1,0:T(8,128)(2,1)S(1)}, u32[]{:S(2)}, u32[]{:S(2)}) async-start(bf16[16,32,2688]{2,1,0:T(8,128)(2,1)} %get-tuple-element.11), calls=%async_computation | async-start | bytes 5505024 | tf_op jit(solution)/shard_map/all_to_all | solution.py:218
  11.7 73.4 %copy-start = (bf16[64,5120]{1,0:T(8,128)(2,1)S(1)}, bf16[64,5120]{1,0:T(8,128)(2,1)}, u32[]{:S(2)}) copy-start(bf16[64,5120]{1,0:T(8,128)(2,1)} %embed_ref.5) | copy-start | bytes 1966084
  11.7 73.4 %copy-start.1 = (f32[1,2,5120]{2,1,0:T(2,128)S(1)}, f32[1,2,5120]{2,1,0:T(2,128)}, u32[]{:S(2)}) copy-start(f32[1,2,5120]{2,1,0:T(2,128)} %param.16) | copy-start | bytes 122884
  83.0 7.7 %collective-permute-start = (bf16[512,2688]{1,0:T(8,128)(2,1)S(1)}, bf16[512,2688]{1,0:T(8,128)(2,1)S(1)}, u32[]{:S(2)}, u32[]{:S(2)}) collective-permute-start(bf16[512,2688]{1,0:T(8,128)(2,1)S(1)} %bitcast.13), channel_id=1, source_target_pairs={{0,16},{16,0},{32,48},{48,32},{64,80},{80,64},{96,112},{112,96},{1... | collective-permute-start | bytes 8257544 | tf_op jit(solution)/shard_map/ppermute | solution.py:220
  90.7 23.2 %copy-start.3 = (f32[16,128]{1,0:T(8,128)S(1)}, f32[16,128]{1,0:T(8,128)}, u32[]{:S(2)}) copy-start(f32[16,128]{1,0:T(8,128)} %get-tuple-element.10) | copy-start | bytes 24580
  90.7 23.2 %copy-start.4 = (f32[16,128]{1,0:T(8,128)S(1)}, f32[16,128]{1,0:T(8,128)}, u32[]{:S(2)}) copy-start(f32[16,128]{1,0:T(8,128)} %get-tuple-element.9) | copy-start | bytes 24580
  90.8 23.2 %copy-start.5 = (f32[16,128]{1,0:T(8,128)S(1)}, f32[16,128]{1,0:T(8,128)}, u32[]{:S(2)}) copy-start(f32[16,128]{1,0:T(8,128)} %get-tuple-element.15) | copy-start | bytes 24580
  90.8 46.2 %copy-start.2 = (f32[32,64]{1,0:T(8,128)S(1)}, f32[32,64]{1,0:T(8,128)}, u32[]{:S(2)}) copy-start(f32[32,64]{1,0:T(8,128)} %param.12) | copy-start | bytes 24580
  99.6 14.2 %all-to-all-start.1 = ((bf16[16,16,128]{2,1,0:T(8,128)(2,1)}), bf16[16,16,128]{2,1,0:T(8,128)(2,1)S(1)}, u32[]{:S(2)}, u32[]{:S(2)}) async-start(bf16[16,16,128]{2,1,0:T(8,128)(2,1)} %shard_map.124), calls=%async_computation.1 | async-start | bytes 131072 | tf_op jit(solution)/shard_map/all_to_all | solution.py:266
  117.9 18.9 %all-to-all-start.2 = ((bf16[16,16,128]{2,1,0:T(8,128)(2,1)}), bf16[16,16,128]{2,1,0:T(8,128)(2,1)S(1)}, u32[]{:S(2)}, u32[]{:S(2)}) async-start(bf16[16,16,128]{2,1,0:T(8,128)(2,1)} %broadcast_in_dim.34), calls=%async_computation.2 | async-start | bytes 131072 | tf_op jit(solution)/shard_map/all_to_all | solution.py:276

commit v7 on v6

--- a/solution.py
+++ b/solution.py
@@ -91,8 +91,9 @@
 def scale_rows(left_ref, context_ref, embed_ref, mods_ref):
     tokens, channels = context_ref.shape[0], embed_ref.shape[0]
     gain = 1.0 + mods_ref[1:2, :]
-    left_ref[:tokens, :] = (context_ref[...].astype(F32) * gain).astype(BF16)
-    left_ref[tokens : tokens + channels, :] = (embed_ref[...].astype(F32) * gain).astype(BF16)
+    short = gain.astype(BF16)
+    left_ref[:tokens, :] = context_ref[...] * short
+    left_ref[tokens : tokens + channels, :] = embed_ref[...] * short
     row = lax.broadcasted_iota(jnp.int32, (16, gain.shape[1]), 0)
     left_ref[tokens + channels :, :] = jnp.where(row == 0, mods_ref[0:1, :], 0.0).astype(BF16)
 
@@ -103,7 +104,7 @@
     for n in range(chips):
         meta = extra_ref[n, extra_ref.shape[1] - 16 :, :].astype(F32)
         power = jnp.sum(jnp.where(row == i, meta, 0.0), axis=0, keepdims=True)
-        weight_ref[n * rows : (n + 1) * rows, :] = from_whole(chunk_ref[n], power).astype(BF16)
+        weight_ref[n * rows : (n + 1) * rows, :] = chunk_ref[n].astype(BF16) * jnp.exp2(-(power + KEPT)).astype(BF16)
     return dot_nn(left_ref[...], weight_ref[...])
 
 
@@ -164,10 +165,11 @@
         outs = []
         for h in range(made_ref.shape[2] // HEAD):
             cols = slice(h * HEAD, (h + 1) * HEAD)
-            scores = dot_nt(made_ref[0, :, cols], made_ref[1, :, cols]) * (1.0 / math.sqrt(HEAD))
-            weights = jnp.exp(scores - jnp.max(scores, axis=-1, keepdims=True))
-            norm = jnp.sum(weights, axis=-1, keepdims=True)
-            outs.append((dot_nn(weights.astype(BF16), made_ref[2, :, cols]) / norm).astype(BF16))
+            scores = dot_nt(made_ref[0, :, cols], made_ref[1, :, cols]) * (math.log2(math.e) / math.sqrt(HEAD))
+            weights = jnp.exp2(scores - jnp.max(scores, axis=-1, keepdims=True)).astype(BF16)
+            values = made_ref[2, :, cols]
+            mixed = dot_nn(weights, jnp.concatenate([values, jnp.ones_like(values)], axis=1))
+            outs.append((mixed[:, :HEAD] / mixed[:, HEAD:]).astype(BF16))
         attended = jnp.concatenate(outs, axis=1)
         head_high, head_low = split_two(heads_ref[...] + head_shares(extra_ref))
         result = dot_nt(attended, head_high) + dot_nt(attended, head_low)

time: 138 us -> 137 us (level)
  transfers between devices with their start and end apart: 4 -> 4, of which waited for: 2 -> 2; matrix products, arithmetic and copies ran while one was open for 0% -> 1% of each run, Pallas kernels for 4% -> 4%
where the time goes in v7:
time: 137 us
  blocking collectives  74.6 us (54%)
  starting transfers between devices  24.7 us (18%)
  waiting for transfers between devices  17.4 us (13%)
  Pallas kernels  17.2 us (13%)
    all_gather x1, blocking collectives, per_device(): chunks = lax.all_gather(chunk, 'tm')  71.4 us
    all_to_all x1, waiting for transfers between devices, per_device(): lax.all_to_all(spread, 'tm', 0, 0, axis_index_groups=same_core).astype(F32)  10.9 us
    pallas_call x1, Pallas kernels, per_device(): halved(second_half, lambda c: 1 - c, [by_kind, fixed(channels, cols), pl....  8.45 us
    all_to_all x1, starting transfers between devices, per_device(): shares = lax.all_to_all(shares, 'seq', 0, 0)  7.7 us
    all_to_all x1, starting transfers between devices, per_device(): gathered = lax.all_to_all(payload, 'seq', 0, 0).reshape(tokens, reach + 128)  7.59 us
    all_to_all x1, starting transfers between devices, per_device(): lax.all_to_all(spread, 'tm', 0, 0, axis_index_groups=same_core).astype(F32)  7.33 us
    all_to_all x1, waiting for transfers between devices, per_device(): shares = lax.all_to_all(shares, 'seq', 0, 0)  6.5 us
    pallas_call x1, Pallas kernels, per_device(): halved(first_half, lambda c: c, [], (shape((3 * half, cols), F32), shape(...  5.33 us
  transfers between devices with their start and end apart: 4, of which 2 were waited for; matrix products, arithmetic and copies ran while one was open for 1% of the time, Pallas kernels for 4%

profile of v7, /device:TPU:1, one launch (start us, length us, event | category | flops | bytes accessed | tf_op | source)
XLA Modules:
  0.0 136.9 jit_solution(15183972846986450073)
XLA Ops:
  0.6 3.4 %shard_map.122 = (bf16[16,32,2688]{2,1,0:T(8,128)(2,1)}, f32[16,128]{1,0:T(8,128)}, f32[16,128]{1,0:T(8,128)}, f32[16,128]{1,0:T(8,128)}, s16[560,256]{1,0:T(8,128)(2,1)}) custom-call(s32[1]{0:T(128)} %bitcast.core_ref.place_ref, s32[1,2]{1,0:T(1,128)} %times_ref.1, f32[32,64]{1,0:T(8,128)} %bitcast.23, f32[32,64]{1,0:T(8,128)} %bitcast.24, ...), custom_call_target="tpu_custom_call" | custom-call | flops 30000000 | bytes 5000000 | tf_op jit(solution)/shard_map/pallas_call | solution.py:206
  4.1 7.6 %all-to-all-start = ((bf16[16,32,2688]{2,1,0:T(8,128)(2,1)}), bf16[16,32,2688]{2,1,0:T(8,128)(2,1)S(1)}, u32[]{:S(2)}, u32[]{:S(2)}) async-start(bf16[16,32,2688]{2,1,0:T(8,128)(2,1)} %get-tuple-element.11), calls=%async_computation | async-start | bytes 5505024 | tf_op jit(solution)/shard_map/all_to_all | solution.py:220
  11.7 0.0 copy-start
  11.7 0.0 copy-start.1
  11.7 71.4 %all-gather.3 = s16[17920,256]{1,0:T(8,128)(2,1)} all-gather(s16[560,256]{1,0:T(8,128)(2,1)} %get-tuple-element.12), channel_id=2, replica_groups=mesh['tm'=32,'seq'=16] {'tm'}, dimensions={0}, use_global_device_ids=true | all-gather | bytes 9461760 | tf_op jit(solution)/shard_map/all_gather | solution.py:221
  83.0 0.0 all-to-all-done
  83.0 2.0 %collective-permute-start = (bf16[512,2688]{1,0:T(8,128)(2,1)S(1)}, bf16[512,2688]{1,0:T(8,128)(2,1)S(1)}, u32[]{:S(2)}, u32[]{:S(2)}) collective-permute-start(bf16[512,2688]{1,0:T(8,128)(2,1)S(1)} %bitcast.13), channel_id=1, source_target_pairs={{0,16},{16,0},{32,48},{48,32},{64,80},{80,64},{96,112},{112,96},{1... | collective-permute-start | bytes 8257544 | tf_op jit(solution)/shard_map/ppermute | solution.py:222
  85.1 0.0 copy-done
  85.1 0.0 copy-done.1
  85.1 5.3 %shard_map.123 = (f32[1776,256]{1,0:T(8,128)S(1)}, f32[64,256]{1,0:T(8,128)S(1)}) custom-call(s32[1]{0:T(128)} %bitcast.core_ref.place_ref, bf16[512,2688]{1,0:T(8,128)(2,1)S(1)} %bitcast.14, bf16[64,5120]{1,0:T(8,128)(2,1)S(1)} %copy-done, f32[2,5120]{1,0:T(2,128)S(1)} %bitcast.16, s16[32,560,256]{2,1,0:T(8,128)(2,1)} %bitcast.18, s16[32,560,256]{2,1,0:T(8,128)(2,1)} %bitcast.19), custom_call_target="tpu_custom_call" | custom-call | flops 99999997952 | bytes 9000000 | tf_op jit(solution)/shard_map/pallas_call | solution.py:250
  90.4 0.0 collective-permute-done.context_ref
  90.4 0.0 copy-start.3
  90.5 0.0 copy-start.4
  90.5 0.0 copy-start.5
  90.5 0.0 copy-start.2
  90.5 8.4 %shard_map.124 = bf16[16,16,128]{2,1,0:T(8,128)(2,1)} custom-call(s32[1]{0:T(128)} %bitcast.core_ref.place_ref, bf16[512,2688]{1,0:T(8,128)(2,1)S(1)} %collective-permute-done.context_ref, bf16[64,5120]{1,0:T(8,128)(2,1)S(1)} %copy-done, f32[2,5120]{1,0:T(2,128)S(1)} %bitcast.17, s16[32,560,256]{2,1,0:T(8,128)(2,1)} %bitcast.20, ...), custom_call_target="tpu_custom_call" | custom-call | flops 4000000000 | bytes 9000000 | tf_op jit(solution)/shard_map/pallas_call | solution.py:259
  98.9 7.7 %all-to-all-start.1 = ((bf16[16,16,128]{2,1,0:T(8,128)(2,1)}), bf16[16,16,128]{2,1,0:T(8,128)(2,1)S(1)}, u32[]{:S(2)}, u32[]{:S(2)}) async-start(bf16[16,16,128]{2,1,0:T(8,128)(2,1)} %shard_map.124), calls=%async_computation.1 | async-start | bytes 131072 | tf_op jit(solution)/shard_map/all_to_all | solution.py:268
  106.7 6.5 %all-to-all-done.1 = bf16[16,16,128]{2,1,0:T(8,128)(2,1)S(1)} async-done(((bf16[16,16,128]{2,1,0:T(8,128)(2,1)}), bf16[16,16,128]{2,1,0:T(8,128)(2,1)S(1)}, u32[]{:S(2)}, u32[]{:S(2)}) %all-to-all-start.1) | async-done | bytes 65568 | tf_op jit(solution)/shard_map/all_to_all | solution.py:268
  113.2 0.0 copy-done.3
  113.2 0.0 copy-done.4
  113.2 0.0 copy-done.5
  113.2 3.3 %all-gather.1 = f32[32,128]{1,0:T(8,128)S(1)} all-gather(f32[16,128]{1,0:T(8,128)S(1)} %get-tuple-element.17), channel_id=3, replica_groups={{0,16},{32,48},{64,80},{96,112},{128,144},{160,176},{192,208},{224,240}..., dimensions={0}, use_global_device_ids=true | all-gather | bytes 24576 | tf_op jit(solution)/shard_map/all_gather | solution.py:276
  116.5 0.6 broadcast_in_dim.34
  117.2 7.3 %all-to-all-start.2 = ((bf16[16,16,128]{2,1,0:T(8,128)(2,1)}), bf16[16,16,128]{2,1,0:T(8,128)(2,1)S(1)}, u32[]{:S(2)}, u32[]{:S(2)}) async-start(bf16[16,16,128]{2,1,0:T(8,128)(2,1)} %broadcast_in_dim.34), calls=%async_computation.2 | async-start | bytes 131072 | tf_op jit(solution)/shard_map/all_to_all | solution.py:278
  124.5 0.1 slice_bitcast_fusion.1
  124.6 0.6 pad_maximum_fusion
  125.2 10.9 %all-to-all-done.2 = bf16[16,16,128]{2,1,0:T(8,128)(2,1)S(1)} async-done(((bf16[16,16,128]{2,1,0:T(8,128)(2,1)}), bf16[16,16,128]{2,1,0:T(8,128)(2,1)S(1)}, u32[]{:S(2)}, u32[]{:S(2)}) %all-to-all-start.2) | async-done | bytes 65568 | tf_op jit(solution)/shard_map/all_to_all | solution.py:278
  136.1 0.1 select_reduce_fusion
  136.2 0.1 fusion.2
  136.3 0.0 copy-done.2
  136.3 0.6 fusion
  (5 shorter events, 0.0 us)
Async XLA Ops:
  4.1 79.0 %all-to-all-start = ((bf16[16,32,2688]{2,1,0:T(8,128)(2,1)}), bf16[16,32,2688]{2,1,0:T(8,128)(2,1)S(1)}, u32[]{:S(2)}, u32[]{:S(2)}) async-start(bf16[16,32,2688]{2,1,0:T(8,128)(2,1)} %get-tuple-element.11), calls=%async_computation | async-start | bytes 5505024 | tf_op jit(solution)/shard_map/all_to_all | solution.py:220
  11.7 73.4 %copy-start = (bf16[64,5120]{1,0:T(8,128)(2,1)S(1)}, bf16[64,5120]{1,0:T(8,128)(2,1)}, u32[]{:S(2)}) copy-start(bf16[64,5120]{1,0:T(8,128)(2,1)} %embed_ref.5) | copy-start | bytes 1966084
  11.7 73.4 %copy-start.1 = (f32[1,2,5120]{2,1,0:T(2,128)S(1)}, f32[1,2,5120]{2,1,0:T(2,128)}, u32[]{:S(2)}) copy-start(f32[1,2,5120]{2,1,0:T(2,128)} %param.16) | copy-start | bytes 122884
  83.0 7.4 %collective-permute-start = (bf16[512,2688]{1,0:T(8,128)(2,1)S(1)}, bf16[512,2688]{1,0:T(8,128)(2,1)S(1)}, u32[]{:S(2)}, u32[]{:S(2)}) collective-permute-start(bf16[512,2688]{1,0:T(8,128)(2,1)S(1)} %bitcast.13), channel_id=1, source_target_pairs={{0,16},{16,0},{32,48},{48,32},{64,80},{80,64},{96,112},{112,96},{1... | collective-permute-start | bytes 8257544 | tf_op jit(solution)/shard_map/ppermute | solution.py:222
  90.4 22.7 %copy-start.3 = (f32[16,128]{1,0:T(8,128)S(1)}, f32[16,128]{1,0:T(8,128)}, u32[]{:S(2)}) copy-start(f32[16,128]{1,0:T(8,128)} %get-tuple-element.10) | copy-start | bytes 24580
  90.5 22.7 %copy-start.4 = (f32[16,128]{1,0:T(8,128)S(1)}, f32[16,128]{1,0:T(8,128)}, u32[]{:S(2)}) copy-start(f32[16,128]{1,0:T(8,128)} %get-tuple-element.9) | copy-start | bytes 24580
  90.5 22.7 %copy-start.5 = (f32[16,128]{1,0:T(8,128)S(1)}, f32[16,128]{1,0:T(8,128)}, u32[]{:S(2)}) copy-start(f32[16,128]{1,0:T(8,128)} %get-tuple-element.15) | copy-start | bytes 24580
  90.5 45.8 %copy-start.2 = (f32[32,64]{1,0:T(8,128)S(1)}, f32[32,64]{1,0:T(8,128)}, u32[]{:S(2)}) copy-start(f32[32,64]{1,0:T(8,128)} %param.12) | copy-start | bytes 24580
  98.9 14.2 %all-to-all-start.1 = ((bf16[16,16,128]{2,1,0:T(8,128)(2,1)}), bf16[16,16,128]{2,1,0:T(8,128)(2,1)S(1)}, u32[]{:S(2)}, u32[]{:S(2)}) async-start(bf16[16,16,128]{2,1,0:T(8,128)(2,1)} %shard_map.124), calls=%async_computation.1 | async-start | bytes 131072 | tf_op jit(solution)/shard_map/all_to_all | solution.py:268
  117.2 18.9 %all-to-all-start.2 = ((bf16[16,16,128]{2,1,0:T(8,128)(2,1)}), bf16[16,16,128]{2,1,0:T(8,128)(2,1)S(1)}, u32[]{:S(2)}, u32[]{:S(2)}) async-start(bf16[16,16,128]{2,1,0:T(8,128)(2,1)} %broadcast_in_dim.34), calls=%async_computation.2 | async-start | bytes 131072 | tf_op jit(solution)/shard_map/all_to_all | solution.py:278

commit v8 on v7

--- a/solution.py
+++ b/solution.py
@@ -180,6 +180,10 @@
             out_ref[p] = block.astype(BF16)
 
 
+def spread_sum(both_ref, out_ref):
+    out_ref[...] = jnp.broadcast_to((both_ref[0] + both_ref[1]).astype(BF16)[None], out_ref.shape)
+
+
 def per_device(
     states, initial, noise_draws, timesteps, context, modulation, out_gate, embed_weight, qkv_weight, out_weight, head_weight
 ):
@@ -274,7 +278,13 @@
     velocity_f = gains * mixed
     drift = sizes * velocity_f + kicks
     both = lax.all_gather(drift, "tm", axis_index_groups=[[2 * i, 2 * i + 1] for i in range(chips)])
-    spread = jnp.broadcast_to((both[0] + both[1]).astype(BF16)[None], (chips, pair_rows, 2 * channels))
+    spread = pl.pallas_call(
+        spread_sum,
+        out_shape=shape((chips, pair_rows, 2 * channels), BF16),
+        in_specs=[one],
+        out_specs=one,
+        compiler_params=pltpu.CompilerParams(vmem_limit_bytes=8 * 1024 * 1024),
+    )(both)
     everyone = lax.all_to_all(spread, "tm", 0, 0, axis_index_groups=same_core).astype(F32)
     earlier = lax.broadcasted_iota(jnp.int32, (chips, 1, 1), 0) < z
     before = jnp.sum(jnp.where(earlier, everyone, 0.0), axis=0) + jnp.where(core == 1, both[0], 0.0)

time: 137 us -> 137 us (level)
  no operation moved by 1% of the time
where the time goes in v8:
time: 137 us
  blocking collectives  74.6 us (54%)
  starting transfers between devices  24.7 us (18%)
  Pallas kernels  17.8 us (13%)
  waiting for transfers between devices  17.4 us (13%)
    all_gather x1, blocking collectives, per_device(): chunks = lax.all_gather(chunk, 'tm')  71.4 us
    all_to_all x1, waiting for transfers between devices, per_device(): lax.all_to_all(spread, 'tm', 0, 0, axis_index_groups=same_core).astype(F32)  10.9 us
    pallas_call x1, Pallas kernels, per_device(): halved(second_half, lambda c: 1 - c, [by_kind, fixed(channels, cols), pl....  8.45 us
    all_to_all x1, starting transfers between devices, per_device(): shares = lax.all_to_all(shares, 'seq', 0, 0)  7.7 us
    all_to_all x1, starting transfers between devices, per_device(): gathered = lax.all_to_all(payload, 'seq', 0, 0).reshape(tokens, reach + 128)  7.59 us
    all_to_all x1, starting transfers between devices, per_device(): lax.all_to_all(spread, 'tm', 0, 0, axis_index_groups=same_core).astype(F32)  7.33 us
    all_to_all x1, waiting for transfers between devices, per_device(): shares = lax.all_to_all(shares, 'seq', 0, 0)  6.5 us
    pallas_call x1, Pallas kernels, per_device(): halved(first_half, lambda c: c, [], (shape((3 * half, cols), F32), shape(...  5.33 us
  transfers between devices with their start and end apart: 4, of which 2 were waited for; matrix products, arithmetic and copies ran while one was open for 1% of the time, Pallas kernels for 4%

profile of v8, /device:TPU:1, one launch (start us, length us, event | category | flops | bytes accessed | tf_op | source)
XLA Modules:
  0.0 136.9 jit_solution(9256834882797439708)
XLA Ops:
  0.6 3.4 %shard_map.122 = (bf16[16,32,2688]{2,1,0:T(8,128)(2,1)}, f32[16,128]{1,0:T(8,128)}, f32[16,128]{1,0:T(8,128)}, f32[16,128]{1,0:T(8,128)}, s16[560,256]{1,0:T(8,128)(2,1)}) custom-call(s32[1]{0:T(128)} %bitcast.core_ref.place_ref, s32[1,2]{1,0:T(1,128)} %times_ref.1, f32[32,64]{1,0:T(8,128)} %bitcast.25, f32[32,64]{1,0:T(8,128)} %bitcast.26, ...), custom_call_target="tpu_custom_call" | custom-call | flops 30000000 | bytes 5000000 | tf_op jit(solution)/shard_map/pallas_call | solution.py:210
  4.1 7.6 %all-to-all-start = ((bf16[16,32,2688]{2,1,0:T(8,128)(2,1)}), bf16[16,32,2688]{2,1,0:T(8,128)(2,1)S(1)}, u32[]{:S(2)}, u32[]{:S(2)}) async-start(bf16[16,32,2688]{2,1,0:T(8,128)(2,1)} %get-tuple-element.11), calls=%async_computation | async-start | bytes 5505024 | tf_op jit(solution)/shard_map/all_to_all | solution.py:224
  11.7 0.0 copy-start
  11.7 0.0 copy-start.1
  11.7 71.4 %all-gather.3 = s16[17920,256]{1,0:T(8,128)(2,1)} all-gather(s16[560,256]{1,0:T(8,128)(2,1)} %get-tuple-element.12), channel_id=2, replica_groups=mesh['tm'=32,'seq'=16] {'tm'}, dimensions={0}, use_global_device_ids=true | all-gather | bytes 9461760 | tf_op jit(solution)/shard_map/all_gather | solution.py:225
  83.0 0.0 all-to-all-done
  83.0 2.0 %collective-permute-start = (bf16[512,2688]{1,0:T(8,128)(2,1)S(1)}, bf16[512,2688]{1,0:T(8,128)(2,1)S(1)}, u32[]{:S(2)}, u32[]{:S(2)}) collective-permute-start(bf16[512,2688]{1,0:T(8,128)(2,1)S(1)} %bitcast.14), channel_id=1, source_target_pairs={{0,16},{16,0},{32,48},{48,32},{64,80},{80,64},{96,112},{112,96},{1... | collective-permute-start | bytes 8257544 | tf_op jit(solution)/shard_map/ppermute | solution.py:226
  85.1 0.0 copy-done
  85.1 0.0 copy-done.1
  85.1 5.3 %shard_map.123 = (f32[1776,256]{1,0:T(8,128)S(1)}, f32[64,256]{1,0:T(8,128)S(1)}) custom-call(s32[1]{0:T(128)} %bitcast.core_ref.place_ref, bf16[512,2688]{1,0:T(8,128)(2,1)S(1)} %bitcast.15, bf16[64,5120]{1,0:T(8,128)(2,1)S(1)} %copy-done, f32[2,5120]{1,0:T(2,128)S(1)} %bitcast.18, s16[32,560,256]{2,1,0:T(8,128)(2,1)} %bitcast.20, s16[32,560,256]{2,1,0:T(8,128)(2,1)} %bitcast.21), custom_call_target="tpu_custom_call" | custom-call | flops 99999997952 | bytes 9000000 | tf_op jit(solution)/shard_map/pallas_call | solution.py:254
  90.4 0.0 collective-permute-done.context_ref
  90.4 0.0 copy-start.3
  90.5 0.0 copy-start.4
  90.5 0.0 copy-start.5
  90.5 0.0 copy-start.2
  90.5 8.4 %shard_map.124 = bf16[16,16,128]{2,1,0:T(8,128)(2,1)} custom-call(s32[1]{0:T(128)} %bitcast.core_ref.place_ref, bf16[512,2688]{1,0:T(8,128)(2,1)S(1)} %collective-permute-done.context_ref, bf16[64,5120]{1,0:T(8,128)(2,1)S(1)} %copy-done, f32[2,5120]{1,0:T(2,128)S(1)} %bitcast.19, s16[32,560,256]{2,1,0:T(8,128)(2,1)} %bitcast.22, ...), custom_call_target="tpu_custom_call" | custom-call | flops 4000000000 | bytes 9000000 | tf_op jit(solution)/shard_map/pallas_call | solution.py:263
  98.9 7.7 %all-to-all-start.1 = ((bf16[16,16,128]{2,1,0:T(8,128)(2,1)}), bf16[16,16,128]{2,1,0:T(8,128)(2,1)S(1)}, u32[]{:S(2)}, u32[]{:S(2)}) async-start(bf16[16,16,128]{2,1,0:T(8,128)(2,1)} %shard_map.124), calls=%async_computation.1 | async-start | bytes 131072 | tf_op jit(solution)/shard_map/all_to_all | solution.py:272
  106.7 6.5 %all-to-all-done.1 = bf16[16,16,128]{2,1,0:T(8,128)(2,1)S(1)} async-done(((bf16[16,16,128]{2,1,0:T(8,128)(2,1)}), bf16[16,16,128]{2,1,0:T(8,128)(2,1)S(1)}, u32[]{:S(2)}, u32[]{:S(2)}) %all-to-all-start.1) | async-done | bytes 65568 | tf_op jit(solution)/shard_map/all_to_all | solution.py:272
  113.2 0.0 copy-done.3
  113.2 0.0 copy-done.4
  113.2 0.0 copy-done.5
  113.2 3.3 %all-gather.1 = f32[32,128]{1,0:T(8,128)S(1)} all-gather(f32[16,128]{1,0:T(8,128)S(1)} %get-tuple-element.17), channel_id=3, replica_groups={{0,16},{32,48},{64,80},{96,112},{128,144},{160,176},{192,208},{224,240}..., dimensions={0}, use_global_device_ids=true | all-gather | bytes 24576 | tf_op jit(solution)/shard_map/all_gather | solution.py:280
  116.5 0.6 shard_map.125
  117.2 7.3 %all-to-all-start.2 = ((bf16[16,16,128]{2,1,0:T(8,128)(2,1)}), bf16[16,16,128]{2,1,0:T(8,128)(2,1)S(1)}, u32[]{:S(2)}, u32[]{:S(2)}) async-start(bf16[16,16,128]{2,1,0:T(8,128)(2,1)} %shard_map.125), calls=%async_computation.2 | async-start | bytes 131072 | tf_op jit(solution)/shard_map/all_to_all | solution.py:288
  124.5 0.1 slice_bitcast_fusion.1
  124.6 0.6 pad_maximum_fusion
  125.2 10.9 %all-to-all-done.2 = bf16[16,16,128]{2,1,0:T(8,128)(2,1)S(1)} async-done(((bf16[16,16,128]{2,1,0:T(8,128)(2,1)}), bf16[16,16,128]{2,1,0:T(8,128)(2,1)S(1)}, u32[]{:S(2)}, u32[]{:S(2)}) %all-to-all-start.2) | async-done | bytes 65568 | tf_op jit(solution)/shard_map/all_to_all | solution.py:288
  136.1 0.1 select_reduce_fusion
  136.2 0.1 fusion.2
  136.3 0.0 copy-done.2
  136.3 0.6 fusion
  (4 shorter events, 0.0 us)
Async XLA Ops:
  4.1 79.0 %all-to-all-start = ((bf16[16,32,2688]{2,1,0:T(8,128)(2,1)}), bf16[16,32,2688]{2,1,0:T(8,128)(2,1)S(1)}, u32[]{:S(2)}, u32[]{:S(2)}) async-start(bf16[16,32,2688]{2,1,0:T(8,128)(2,1)} %get-tuple-element.11), calls=%async_computation | async-start | bytes 5505024 | tf_op jit(solution)/shard_map/all_to_all | solution.py:224
  11.7 73.4 %copy-start = (bf16[64,5120]{1,0:T(8,128)(2,1)S(1)}, bf16[64,5120]{1,0:T(8,128)(2,1)}, u32[]{:S(2)}) copy-start(bf16[64,5120]{1,0:T(8,128)(2,1)} %embed_ref.5) | copy-start | bytes 1966084
  11.7 73.4 %copy-start.1 = (f32[1,2,5120]{2,1,0:T(2,128)S(1)}, f32[1,2,5120]{2,1,0:T(2,128)}, u32[]{:S(2)}) copy-start(f32[1,2,5120]{2,1,0:T(2,128)} %param.16) | copy-start | bytes 122884
  83.0 7.4 %collective-permute-start = (bf16[512,2688]{1,0:T(8,128)(2,1)S(1)}, bf16[512,2688]{1,0:T(8,128)(2,1)S(1)}, u32[]{:S(2)}, u32[]{:S(2)}) collective-permute-start(bf16[512,2688]{1,0:T(8,128)(2,1)S(1)} %bitcast.14), channel_id=1, source_target_pairs={{0,16},{16,0},{32,48},{48,32},{64,80},{80,64},{96,112},{112,96},{1... | collective-permute-start | bytes 8257544 | tf_op jit(solution)/shard_map/ppermute | solution.py:226
  90.4 22.7 %copy-start.3 = (f32[16,128]{1,0:T(8,128)S(1)}, f32[16,128]{1,0:T(8,128)}, u32[]{:S(2)}) copy-start(f32[16,128]{1,0:T(8,128)} %get-tuple-element.10) | copy-start | bytes 24580
  90.5 22.7 %copy-start.4 = (f32[16,128]{1,0:T(8,128)S(1)}, f32[16,128]{1,0:T(8,128)}, u32[]{:S(2)}) copy-start(f32[16,128]{1,0:T(8,128)} %get-tuple-element.9) | copy-start | bytes 24580
  90.5 22.7 %copy-start.5 = (f32[16,128]{1,0:T(8,128)S(1)}, f32[16,128]{1,0:T(8,128)}, u32[]{:S(2)}) copy-start(f32[16,128]{1,0:T(8,128)} %get-tuple-element.15) | copy-start | bytes 24580
  90.5 45.8 %copy-start.2 = (f32[32,64]{1,0:T(8,128)S(1)}, f32[32,64]{1,0:T(8,128)}, u32[]{:S(2)}) copy-start(f32[32,64]{1,0:T(8,128)} %param.12) | copy-start | bytes 24580
  98.9 14.2 %all-to-all-start.1 = ((bf16[16,16,128]{2,1,0:T(8,128)(2,1)}), bf16[16,16,128]{2,1,0:T(8,128)(2,1)S(1)}, u32[]{:S(2)}, u32[]{:S(2)}) async-start(bf16[16,16,128]{2,1,0:T(8,128)(2,1)} %shard_map.124), calls=%async_computation.1 | async-start | bytes 131072 | tf_op jit(solution)/shard_map/all_to_all | solution.py:272
  117.2 18.9 %all-to-all-start.2 = ((bf16[16,16,128]{2,1,0:T(8,128)(2,1)}), bf16[16,16,128]{2,1,0:T(8,128)(2,1)S(1)}, u32[]{:S(2)}, u32[]{:S(2)}) async-start(bf16[16,16,128]{2,1,0:T(8,128)(2,1)} %shard_map.125), calls=%async_computation.2 | async-start | bytes 131072 | tf_op jit(solution)/shard_map/all_to_all | solution.py:288

commit v9 on v8

--- a/solution.py
+++ b/solution.py
@@ -180,6 +180,16 @@
             out_ref[p] = block.astype(BF16)
 
 
+def finish(mine_ref, everyone_ref, both_ref, initial_ref, out_ref):
+    mine = mine_ref[0]
+    chips, pair_rows, lanes = everyone_ref.shape
+    before = both_ref[0] * (mine & 1).astype(F32)
+    for chip in range(chips):
+        before = before + jnp.where(chip < (mine >> 1), everyone_ref[chip].astype(F32), 0.0)
+    out_ref[:pair_rows, :] = initial_ref[:pair_rows, :] + before[:, : lanes // 2]
+    out_ref[pair_rows:, :] = initial_ref[pair_rows:, :] + before[:, lanes // 2 :]
+
+
 def spread_sum(both_ref, out_ref):
     out_ref[...] = jnp.broadcast_to((both_ref[0] + both_ref[1]).astype(BF16)[None], out_ref.shape)
 
@@ -285,10 +295,14 @@
         out_specs=one,
         compiler_params=pltpu.CompilerParams(vmem_limit_bytes=8 * 1024 * 1024),
     )(both)
-    everyone = lax.all_to_all(spread, "tm", 0, 0, axis_index_groups=same_core).astype(F32)
-    earlier = lax.broadcasted_iota(jnp.int32, (chips, 1, 1), 0) < z
-    before = jnp.sum(jnp.where(earlier, everyone, 0.0), axis=0) + jnp.where(core == 1, both[0], 0.0)
-    new_states = initial + unpairs(before)
+    everyone = lax.all_to_all(spread, "tm", 0, 0, axis_index_groups=same_core)
+    new_states = pl.pallas_call(
+        finish,
+        out_shape=shape(initial.shape, F32),
+        in_specs=[scalar, one, one, one],
+        out_specs=one,
+        compiler_params=pltpu.CompilerParams(vmem_limit_bytes=8 * 1024 * 1024),
+    )(mine[None], everyone, both, initial)
     return (new_states[None], unpairs(velocity_f).astype(BF16)[None])
 
 

time: 137 us -> 136 us (level)
  blocking collectives: 74.6 us -> 88.7 us
  starting transfers between devices: 24.7 us -> 16.9 us
  waiting for transfers between devices: 17.4 us -> 10.9 us
    all_to_all x0 -> x1, blocking collectives: none -> 14 us  [per_device(): shares = lax.all_to_all(shares, 'seq', 0, 0)]
    all_to_all x2 -> x1, starting transfers between devices: 15 us -> 7.33 us  [per_device(): everyone = lax.all_to_all(spread, 'tm', 0, 0, axis_index_groups=same_core)]
    all_to_all x2 -> x1, waiting for transfers between devices: 17.4 us -> 10.9 us  [per_device(): everyone = lax.all_to_all(spread, 'tm', 0, 0, axis_index_groups=same_core)]
  transfers between devices with their start and end apart: 4 -> 3, of which waited for: 2 -> 1; matrix products, arithmetic and copies ran while one was open for 1% -> 1% of each run, Pallas kernels for 4% -> 4%
where the time goes in v9:
time: 136 us
  blocking collectives  88.7 us (65%)
  Pallas kernels  17.9 us (13%)
  starting transfers between devices  16.9 us (12%)
  waiting for transfers between devices  10.9 us (8%)
    all_gather x1, blocking collectives, per_device(): chunks = lax.all_gather(chunk, 'tm')  71.4 us
    all_to_all x1, blocking collectives, per_device(): shares = lax.all_to_all(shares, 'seq', 0, 0)  14 us
    all_to_all x1, waiting for transfers between devices, per_device(): everyone = lax.all_to_all(spread, 'tm', 0, 0, axis_index_groups=same_core)  10.9 us
    pallas_call x1, Pallas kernels, per_device(): halved(second_half, lambda c: 1 - c, [by_kind, fixed(channels, cols), pl....  7.82 us
    all_to_all x1, starting transfers between devices, per_device(): gathered = lax.all_to_all(payload, 'seq', 0, 0).reshape(tokens, reach + 128)  7.59 us
    all_to_all x1, starting transfers between devices, per_device(): everyone = lax.all_to_all(spread, 'tm', 0, 0, axis_index_groups=same_core)  7.33 us
    pallas_call x1, Pallas kernels, per_device(): halved(first_half, lambda c: c, [], (shape((3 * half, cols), F32), shape(...  5.33 us
    pallas_call x1, Pallas kernels, per_device(): pl.pallas_call(pack, out_shape=(shape((peers, tokens_here, reach + 128),...  3.42 us
  transfers between devices with their start and end apart: 3, of which 1 were waited for; matrix products, arithmetic and copies ran while one was open for 1% of the time, Pallas kernels for 4%

profile of v9, /device:TPU:1, one launch (start us, length us, event | category | flops | bytes accessed | tf_op | source)
XLA Modules:
  0.0 136.0 jit_solution(9823069667324931334)
XLA Ops:
  0.6 3.4 %shard_map.122 = (bf16[16,32,2688]{2,1,0:T(8,128)(2,1)}, f32[16,128]{1,0:T(8,128)}, f32[16,128]{1,0:T(8,128)}, f32[16,128]{1,0:T(8,128)}, s16[560,256]{1,0:T(8,128)(2,1)}) custom-call(s32[1]{0:T(128)} %bitcast.1.core_ref.place_ref, s32[1,2]{1,0:T(1,128)} %times_ref.1, f32[32,64]{1,0:T(8,128)} %bitcast.26, f32[32,64]{1,0:T(8,128)} %bitcast.27, ...), custom_call_target="tpu_custom_call" | custom-call | flops 30000000 | bytes 5000000 | tf_op jit(solution)/shard_map/pallas_call | solution.py:220
  4.1 7.6 %all-to-all-start = ((bf16[16,32,2688]{2,1,0:T(8,128)(2,1)}), bf16[16,32,2688]{2,1,0:T(8,128)(2,1)S(1)}, u32[]{:S(2)}, u32[]{:S(2)}) async-start(bf16[16,32,2688]{2,1,0:T(8,128)(2,1)} %get-tuple-element.11), calls=%async_computation | async-start | bytes 5505024 | tf_op jit(solution)/shard_map/all_to_all | solution.py:234
  11.7 0.0 copy-start
  11.7 0.0 copy-start.1
  11.7 71.4 %all-gather.3 = s16[17920,256]{1,0:T(8,128)(2,1)} all-gather(s16[560,256]{1,0:T(8,128)(2,1)} %get-tuple-element.12), channel_id=2, replica_groups=mesh['tm'=32,'seq'=16] {'tm'}, dimensions={0}, use_global_device_ids=true | all-gather | bytes 9461760 | tf_op jit(solution)/shard_map/all_gather | solution.py:235
  83.0 0.0 all-to-all-done
  83.0 2.0 %collective-permute-start = (bf16[512,2688]{1,0:T(8,128)(2,1)S(1)}, bf16[512,2688]{1,0:T(8,128)(2,1)S(1)}, u32[]{:S(2)}, u32[]{:S(2)}) collective-permute-start(bf16[512,2688]{1,0:T(8,128)(2,1)S(1)} %bitcast.14), channel_id=1, source_target_pairs={{0,16},{16,0},{32,48},{48,32},{64,80},{80,64},{96,112},{112,96},{1... | collective-permute-start | bytes 8257544 | tf_op jit(solution)/shard_map/ppermute | solution.py:236
  85.1 0.0 copy-done
  85.1 0.0 copy-done.1
  85.1 5.3 %shard_map.123 = (f32[1776,256]{1,0:T(8,128)S(1)}, f32[64,256]{1,0:T(8,128)S(1)}) custom-call(s32[1]{0:T(128)} %bitcast.1.core_ref.place_ref, bf16[512,2688]{1,0:T(8,128)(2,1)S(1)} %bitcast.15, bf16[64,5120]{1,0:T(8,128)(2,1)S(1)} %copy-done, f32[2,5120]{1,0:T(2,128)S(1)} %bitcast.19, s16[32,560,256]{2,1,0:T(8,128)(2,1)} %bitcast.21, ...), custom_call_target="tpu_custom_call" | custom-call | flops 99999997952 | bytes 9000000 | tf_op jit(solution)/shard_map/pallas_call | solution.py:264
  90.4 0.0 collective-permute-done.context_ref
  90.4 0.0 copy-start.3
  90.5 0.0 copy-start.4
  90.5 0.0 copy-start.5
  90.5 0.0 copy-start.2
  90.5 7.8 %shard_map.124 = bf16[16,16,128]{2,1,0:T(8,128)(2,1)S(1)} custom-call(s32[1]{0:T(128)} %bitcast.1.core_ref.place_ref, bf16[512,2688]{1,0:T(8,128)(2,1)S(1)} %collective-permute-done.context_ref, bf16[64,5120]{1,0:T(8,128)(2,1)S(1)} %copy-done, f32[2,5120]{1,0:T(2,128)S(1)} %bitcast.20, s16[32,560,256]{2,1,0:T(8,128)(2,1)} %bitcast.23, ...), custom_call_target="tpu_custom_call" | custom-call | flops 4000000000 | bytes 9000000 | tf_op jit(solution)/shard_map/pallas_call | solution.py:273
  98.3 14.0 %all_to_all.15 = bf16[16,16,128]{2,1,0:T(8,128)(2,1)S(1)} all-to-all(bf16[16,16,128]{2,1,0:T(8,128)(2,1)S(1)} %shard_map.124), channel_id=1, replica_groups=mesh['tm'=32,'seq'=16] {'seq'}, dimensions={0} | all-to-all | bytes 131072 | tf_op jit(solution)/shard_map/all_to_all | solution.py:282
  112.4 0.0 copy-done.3
  112.4 0.0 copy-done.4
  112.4 0.0 copy-done.5
  112.4 3.3 %all-gather.1 = f32[32,128]{1,0:T(8,128)S(1)} all-gather(f32[16,128]{1,0:T(8,128)S(1)} %get-tuple-element.17), channel_id=3, replica_groups={{0,16},{32,48},{64,80},{96,112},{128,144},{160,176},{192,208},{224,240}..., dimensions={0}, use_global_device_ids=true | all-gather | bytes 24576 | tf_op jit(solution)/shard_map/all_gather | solution.py:290
  115.7 0.6 shard_map.125
  116.4 7.3 %all-to-all-start.2 = ((bf16[16,16,128]{2,1,0:T(8,128)(2,1)}), bf16[16,16,128]{2,1,0:T(8,128)(2,1)S(1)}, u32[]{:S(2)}, u32[]{:S(2)}) async-start(bf16[16,16,128]{2,1,0:T(8,128)(2,1)} %shard_map.125), calls=%async_computation.2 | async-start | bytes 131072 | tf_op jit(solution)/shard_map/all_to_all | solution.py:298
  123.7 0.1 slice_bitcast_fusion.1
  123.8 0.6 pad_maximum_fusion
  124.4 10.9 %all-to-all-done.2.everyone_ref = bf16[16,16,128]{2,1,0:T(8,128)(2,1)S(1)} async-done(((bf16[16,16,128]{2,1,0:T(8,128)(2,1)}), bf16[16,16,128]{2,1,0:T(8,128)(2,1)S(1)}, u32[]{:S(2)}, u32[]{:S(2)}) %all-to-all-start.2) | async-done | bytes 65568 | tf_op jit(solution)/shard_map/all_to_all | solution.py:298
  135.3 0.0 copy-done.2
  135.3 0.7 shard_map.126
  (2 shorter events, 0.0 us)
Async XLA Ops:
  4.1 79.0 %all-to-all-start = ((bf16[16,32,2688]{2,1,0:T(8,128)(2,1)}), bf16[16,32,2688]{2,1,0:T(8,128)(2,1)S(1)}, u32[]{:S(2)}, u32[]{:S(2)}) async-start(bf16[16,32,2688]{2,1,0:T(8,128)(2,1)} %get-tuple-element.11), calls=%async_computation | async-start | bytes 5505024 | tf_op jit(solution)/shard_map/all_to_all | solution.py:234
  11.7 73.4 %copy-start = (bf16[64,5120]{1,0:T(8,128)(2,1)S(1)}, bf16[64,5120]{1,0:T(8,128)(2,1)}, u32[]{:S(2)}) copy-start(bf16[64,5120]{1,0:T(8,128)(2,1)} %embed_ref.5) | copy-start | bytes 1966084
  11.7 73.4 %copy-start.1 = (f32[1,2,5120]{2,1,0:T(2,128)S(1)}, f32[1,2,5120]{2,1,0:T(2,128)}, u32[]{:S(2)}) copy-start(f32[1,2,5120]{2,1,0:T(2,128)} %param.16) | copy-start | bytes 122884
  83.0 7.4 %collective-permute-start = (bf16[512,2688]{1,0:T(8,128)(2,1)S(1)}, bf16[512,2688]{1,0:T(8,128)(2,1)S(1)}, u32[]{:S(2)}, u32[]{:S(2)}) collective-permute-start(bf16[512,2688]{1,0:T(8,128)(2,1)S(1)} %bitcast.14), channel_id=1, source_target_pairs={{0,16},{16,0},{32,48},{48,32},{64,80},{80,64},{96,112},{112,96},{1... | collective-permute-start | bytes 8257544 | tf_op jit(solution)/shard_map/ppermute | solution.py:236
  90.4 21.9 %copy-start.3 = (f32[16,128]{1,0:T(8,128)S(1)}, f32[16,128]{1,0:T(8,128)}, u32[]{:S(2)}) copy-start(f32[16,128]{1,0:T(8,128)} %get-tuple-element.10) | copy-start | bytes 24580
  90.5 21.9 %copy-start.4 = (f32[16,128]{1,0:T(8,128)S(1)}, f32[16,128]{1,0:T(8,128)}, u32[]{:S(2)}) copy-start(f32[16,128]{1,0:T(8,128)} %get-tuple-element.9) | copy-start | bytes 24580
  90.5 21.9 %copy-start.5 = (f32[16,128]{1,0:T(8,128)S(1)}, f32[16,128]{1,0:T(8,128)}, u32[]{:S(2)}) copy-start(f32[16,128]{1,0:T(8,128)} %get-tuple-element.15) | copy-start | bytes 24580
  90.5 44.8 %copy-start.2 = (f32[32,64]{1,0:T(8,128)S(1)}, f32[32,64]{1,0:T(8,128)}, u32[]{:S(2)}) copy-start(f32[32,64]{1,0:T(8,128)} %initial_ref.1) | copy-start | bytes 24580
  116.4 18.9 %all-to-all-start.2 = ((bf16[16,16,128]{2,1,0:T(8,128)(2,1)}), bf16[16,16,128]{2,1,0:T(8,128)(2,1)S(1)}, u32[]{:S(2)}, u32[]{:S(2)}) async-start(bf16[16,16,128]{2,1,0:T(8,128)(2,1)} %shard_map.125), calls=%async_computation.2 | async-start | bytes 131072 | tf_op jit(solution)/shard_map/all_to_all | solution.py:298
